TPU v7x, 32 devices: a whole 2x2x4 slice. The times are simulated.
32 devices in a mesh: wide: 8 (over z, y), ep: 4 (over x, core).
Axes of the slice: x: 2, y: 2, z: 4, core: 2. Of those that a mesh axis runs over, the one named last changes fastest.
Arguments:
- activations: bfloat16 [8192, 1280], P(('wide', 'ep')), may hold values from -6 to 6
- segment: int32 [8192], P(('wide', 'ep')), may hold values from 0 to 2, as said below
- routes: int32 [8192, 7], P(('wide', 'ep')), may hold values from 0 to 15, all different within a row; in each aligned block of 256 rows (0 to 255, 256 to 511, ...) at most 160 rows name the same one
- gain_attention: bfloat16 [1280], P(('wide', 'ep')), may hold values from 0.5 to 1.5
- query_weight: bfloat16 [1280, 1280], P(('wide', 'ep')), may hold values from -0.15625 to 0.15625
- key_weight: bfloat16 [1280, 1280], P(('wide', 'ep')), may hold values from -0.15625 to 0.15625
- value_weight: bfloat16 [1280, 1280], P(('wide', 'ep')), may hold values from -0.15625 to 0.15625
- output_weight: bfloat16 [1280, 1280], P(('wide', 'ep')), may hold values from -6 to 6
- gain_experts: bfloat16 [1280], P(('wide', 'ep')), may hold values from 0.5 to 1.5
- router_weight: bfloat16 [1280, 16], P(('wide', 'ep')), may hold values from -0.078125 to 0.078125
- shared_gate: bfloat16 [1280, 896], P(('wide', 'ep')), may hold values from -0.15625 to 0.15625
- shared_up: bfloat16 [1280, 896], P(('wide', 'ep')), may hold values from -0.15625 to 0.15625
- shared_down: bfloat16 [896, 1280], P(('wide', 'ep')), may hold values from -0.1875 to 0.1875
- expert_gate: bfloat16 [16, 1280, 896], P('ep'), may hold values from -0.15625 to 0.15625
- expert_up: bfloat16 [16, 1280, 896], P('ep'), may hold values from -0.15625 to 0.15625
- expert_down: bfloat16 [16, 896, 1280], P('ep'), may hold values from -1.5 to 1.5
- cotangent: bfloat16 [8192, 1280], P(('wide', 'ep')), may hold values from -6 to 6
Outputs:
- block_out: bfloat16 [8192, 1280], P(('wide', 'ep'))
- input_grad: float32 [8192, 1280], P(('wide', 'ep'))
- gain_attention_grad: float32 [1280], P(('wide', 'ep'))
- query_grad: float32 [1280, 1280], P(('wide', 'ep'))
- key_grad: float32 [1280, 1280], P(('wide', 'ep'))
- value_grad: float32 [1280, 1280], P(('wide', 'ep'))
- output_weight_grad: float32 [1280, 1280], P(('wide', 'ep'))
- gain_experts_grad: float32 [1280], P(('wide', 'ep'))
- router_grad: float32 [1280, 16], P(('wide', 'ep'))
- shared_gate_grad: float32 [1280, 896], P(('wide', 'ep'))
- shared_up_grad: float32 [1280, 896], P(('wide', 'ep'))
- shared_down_grad: float32 [896, 1280], P(('wide', 'ep'))
- expert_gate_grad: float32 [16, 1280, 896], P('ep', 'wide')
- expert_up_grad: float32 [16, 1280, 896], P('ep', 'wide')
- expert_down_grad: float32 [16, 896, 1280], P('ep', 'wide')
- expert_counts: int32 [16], P('ep')
Inputs may be any that keep to these rules, and one draw needn't show every extreme that they name: `segment`: within each block of 1024 consecutive tokens the numbers start at 0, never fall and end at 2; document 1 begins in the first quarter of the block's first 256 tokens and ends in the last quarter of its last 256 tokens. `routes`: each row names 7 different experts; among the rows of one device no expert is named more than 160 times, and some device's rows name some expert exactly 160 times.
All inputs are finite; a program needn't handle non-finite values.
Results may differ from a plain program's by a relative error of at most 0.018.
Values may be sent and summed in bfloat16 or wider, within the bound.
A program may use at most 384 MiB of HBM per device.

v0:
```python
import jax
import jax.numpy as jnp
from jax import lax
from jax.sharding import PartitionSpec as P

HEADS = 10
HD = 128


epsilon = 1e-06
masked_value = -1e30


def contract_rows(left, right):
    return lax.dot_general(
        left, right, (((0,), (0,)), ((), ())), preferred_element_type=jnp.float32
    )


def times_transposed(left, right):
    return lax.dot_general(
        left, right, (((1,), (1,)), ((), ())), preferred_element_type=jnp.float32
    )


def norm_scale(values):
    return lax.rsqrt(jnp.mean(values * values, axis=-1, keepdims=True) + epsilon)


def norm_backward(values, inverse, gain, normed_grad):
    weighted = normed_grad * gain
    gain_grad = jnp.sum(normed_grad * values * inverse, axis=0)
    cubed = inverse * inverse * inverse
    values_grad = inverse * weighted - values * cubed * jnp.mean(
        weighted * values, axis=-1, keepdims=True
    )
    return (gain_grad, values_grad)


def silu_parts(gate_act):
    logistic = jax.nn.sigmoid(gate_act)
    return (gate_act * logistic, logistic * (1.0 + gate_act * (1.0 - logistic)))


def make_allowed(segment, labels_all, first_place):
    query_places = first_place + jnp.arange(segment.shape[0], dtype=jnp.int32)
    key_places = jnp.arange(labels_all.shape[0], dtype=jnp.int32)
    same_doc = segment.astype(jnp.float32)[:, None] == labels_all.astype(jnp.float32)[None, :]
    return same_doc & (query_places[:, None] >= key_places[None, :])


def make_probs(queries, keys_all, allowed):
    query_heads = queries.reshape(queries.shape[0], HEADS, HD)
    key_heads = keys_all.reshape(keys_all.shape[0], HEADS, HD)
    scores = jnp.einsum(
        "qhd,khd->hqk", query_heads, key_heads, preferred_element_type=jnp.float32
    ) * HD ** (-0.5)
    scores = jnp.where(allowed[None, :, :], scores, masked_value)
    largest = jnp.max(scores, axis=-1, keepdims=True)
    log_total = largest + jnp.log(jnp.sum(jnp.exp(scores - largest), axis=-1, keepdims=True))
    return (jnp.exp(scores - log_total), log_total)


def body(
    activations,
    segment,
    routes,
    gain_attention,
    query_weight,
    key_weight,
    value_weight,
    output_weight,
    gain_experts,
    router_weight,
    shared_gate,
    shared_up,
    shared_down,
    expert_gate,
    expert_up,
    expert_down,
    cotangent,
):
    gathered = (
        lax.all_gather(gain_attention, ("wide", "ep"), axis=0, tiled=True),
        lax.all_gather(query_weight, ("wide", "ep"), axis=0, tiled=True),
        lax.all_gather(key_weight, ("wide", "ep"), axis=0, tiled=True),
        lax.all_gather(value_weight, ("wide", "ep"), axis=0, tiled=True),
        lax.all_gather(output_weight, ("wide", "ep"), axis=0, tiled=True),
        lax.all_gather(gain_experts, ("wide", "ep"), axis=0, tiled=True),
        lax.all_gather(router_weight, ("wide", "ep"), axis=0, tiled=True),
        lax.all_gather(shared_gate, ("wide", "ep"), axis=0, tiled=True),
        lax.all_gather(shared_up, ("wide", "ep"), axis=0, tiled=True),
        lax.all_gather(shared_down, ("wide", "ep"), axis=0, tiled=True),
    )
    gain_one, w_query, w_key, w_value, w_out, gain_two, w_router, s_gate, s_up, s_down = gathered
    tok_rows, width = activations.shape
    top_count = routes.shape[1]
    experts = w_router.shape[1]
    local_experts = expert_gate.shape[0]
    group_devices = lax.axis_size("ep")
    capacity = min((tok_rows * top_count * 10 // (7 * experts) + 7) // 8 * 8, tok_rows)
    first_place = lax.axis_index("ep") * tok_rows
    inputs = activations.astype(jnp.float32)
    inverse_one = norm_scale(inputs)
    gain_one_f = gain_one.astype(jnp.float32)
    normed_one = (inputs * inverse_one * gain_one_f).astype(jnp.bfloat16)
    queries = jnp.dot(normed_one, w_query, preferred_element_type=jnp.float32).astype(jnp.bfloat16)
    keys_mine = jnp.dot(normed_one, w_key, preferred_element_type=jnp.float32).astype(jnp.bfloat16)
    values_mine = jnp.dot(normed_one, w_value, preferred_element_type=jnp.float32).astype(
        jnp.bfloat16
    )
    labels = segment.astype(jnp.bfloat16)
    keys_all, values_all, labels_all = (
        lax.all_gather(keys_mine, "ep", axis=0, tiled=True),
        lax.all_gather(values_mine, "ep", axis=0, tiled=True),
        lax.all_gather(labels, "ep", axis=0, tiled=True),
    )
    allowed = make_allowed(segment, labels_all, first_place)
    probs, log_first = make_probs(queries, keys_all, allowed)
    value_heads = values_all.reshape(values_all.shape[0], HEADS, HD)
    attended = (
        jnp.einsum(
            "hqk,khd->qhd",
            probs.astype(jnp.bfloat16),
            value_heads,
            preferred_element_type=jnp.float32,
        )
        .reshape(tok_rows, width)
        .astype(jnp.bfloat16)
    )
    middle = inputs + jnp.dot(attended, w_out, preferred_element_type=jnp.float32)
    inverse_two = norm_scale(middle)
    gain_two_f = gain_two.astype(jnp.float32)
    normed_two = (middle * inverse_two * gain_two_f).astype(jnp.bfloat16)
    router_probs = jax.nn.softmax(
        jnp.dot(normed_two, w_router, preferred_element_type=jnp.float32), axis=-1
    )
    gates = jnp.take_along_axis(router_probs, routes, axis=1)
    numbers = jnp.arange(experts, dtype=jnp.int32)
    marks = (routes[:, :, None] == numbers[None, None, :]).astype(jnp.int32)
    flat_marks = marks.reshape(tok_rows * top_count, experts)
    earlier = jnp.cumsum(flat_marks, axis=0) - flat_marks
    slots = jnp.sum(earlier * flat_marks, axis=-1)
    lookup = routes.reshape(-1) * capacity + slots
    picks = jnp.repeat(normed_two, top_count, axis=0)
    send_rows = (
        jnp.zeros((experts * capacity, width), jnp.bfloat16)
        .at[lookup]
        .set(picks)
        .reshape(experts, capacity, width)
    )
    received = lax.all_to_all(send_rows, "ep", split_axis=0, concat_axis=1, tiled=True)
    produced_list = []
    for expert_index in range(local_experts):
        gate_act = jnp.dot(
            received[expert_index], expert_gate[expert_index], preferred_element_type=jnp.float32
        )
        up_act = jnp.dot(
            received[expert_index], expert_up[expert_index], preferred_element_type=jnp.float32
        )
        hidden = (jax.nn.silu(gate_act) * up_act).astype(jnp.bfloat16)
        produced_list.append(
            jnp.dot(hidden, expert_down[expert_index], preferred_element_type=jnp.float32).astype(
                jnp.bfloat16
            )
        )
    produced = jnp.stack(produced_list)
    returned = lax.all_to_all(produced, "ep", split_axis=1, concat_axis=0, tiled=True)
    chosen = (
        returned.reshape(experts * capacity, width)[lookup]
        .reshape(tok_rows, top_count, width)
        .astype(jnp.float32)
    )
    routed = jnp.sum(gates[:, :, None] * chosen, axis=1)
    shared_gate_act = jnp.dot(normed_two, s_gate, preferred_element_type=jnp.float32)
    shared_up_act = jnp.dot(normed_two, s_up, preferred_element_type=jnp.float32)
    shared_act, shared_slope = silu_parts(shared_gate_act)
    shared_hidden = (shared_act * shared_up_act).astype(jnp.bfloat16)
    shared_out = jnp.dot(shared_hidden, s_down, preferred_element_type=jnp.float32)
    block_out = (middle + shared_out + routed).astype(jnp.bfloat16)
    out_grad = cotangent.astype(jnp.float32)
    shared_down_grad = contract_rows(shared_hidden, cotangent)
    shared_hidden_grad = times_transposed(cotangent, s_down)
    shared_gate_act_grad = (shared_hidden_grad * shared_up_act * shared_slope).astype(jnp.bfloat16)
    shared_up_act_grad = (shared_hidden_grad * shared_act).astype(jnp.bfloat16)
    shared_gate_grad = contract_rows(normed_two, shared_gate_act_grad)
    shared_up_grad = contract_rows(normed_two, shared_up_act_grad)
    normed_two_grad = times_transposed(shared_gate_act_grad, s_gate) + times_transposed(
        shared_up_act_grad, s_up
    )
    gate_grads = jnp.einsum("tkd,td->tk", chosen, out_grad)
    slot_grad = (
        (gates[:, :, None] * out_grad[:, None, :])
        .astype(jnp.bfloat16)
        .reshape(tok_rows * top_count, width)
    )
    grad_send = (
        jnp.zeros((experts * capacity, width), jnp.bfloat16)
        .at[lookup]
        .set(slot_grad)
        .reshape(experts, capacity, width)
    )
    grad_received = lax.all_to_all(grad_send, "ep", split_axis=0, concat_axis=1, tiled=True)
    gate_grad_list = []
    up_grad_list = []
    down_grad_list = []
    row_grad_list = []
    for expert_index in range(local_experts):
        rows_here = received[expert_index]
        slot_here = grad_received[expert_index]
        gate_act = jnp.dot(rows_here, expert_gate[expert_index], preferred_element_type=jnp.float32)
        up_act = jnp.dot(rows_here, expert_up[expert_index], preferred_element_type=jnp.float32)
        activated, slope = silu_parts(gate_act)
        hidden = (activated * up_act).astype(jnp.bfloat16)
        down_w_grad = contract_rows(hidden, slot_here)
        hidden_grad = times_transposed(slot_here, expert_down[expert_index])
        act_gate = (hidden_grad * up_act * slope).astype(jnp.bfloat16)
        act_up = (hidden_grad * activated).astype(jnp.bfloat16)
        gate_w_grad = contract_rows(rows_here, act_gate)
        up_w_grad = contract_rows(rows_here, act_up)
        row_grad_list.append(
            (
                times_transposed(act_gate, expert_gate[expert_index])
                + times_transposed(act_up, expert_up[expert_index])
            ).astype(jnp.bfloat16)
        )
        gate_grad_list.append(gate_w_grad)
        up_grad_list.append(up_w_grad)
        down_grad_list.append(down_w_grad)
    expert_gate_grad, expert_up_grad, expert_down_grad = (
        lax.psum_scatter(
            jnp.stack(gate_grad_list).astype(jnp.bfloat16), "wide", scatter_dimension=1, tiled=True
        ).astype(jnp.float32),
        lax.psum_scatter(
            jnp.stack(up_grad_list).astype(jnp.bfloat16), "wide", scatter_dimension=1, tiled=True
        ).astype(jnp.float32),
        lax.psum_scatter(
            jnp.stack(down_grad_list).astype(jnp.bfloat16), "wide", scatter_dimension=1, tiled=True
        ).astype(jnp.float32),
    )
    row_grads = lax.all_to_all(
        jnp.stack(row_grad_list), "ep", split_axis=1, concat_axis=0, tiled=True
    )
    back_rows = (
        row_grads.reshape(experts * capacity, width)[lookup]
        .reshape(tok_rows, top_count, width)
        .astype(jnp.float32)
    )
    normed_two_grad = normed_two_grad + jnp.sum(back_rows, axis=1)
    prob_grad = jnp.einsum("tk,tke->te", gate_grads, marks.astype(jnp.float32))
    logit_grad = router_probs * (
        prob_grad - jnp.sum(router_probs * prob_grad, axis=-1, keepdims=True)
    )
    router_f = w_router.astype(jnp.float32)
    normed_two_f = normed_two.astype(jnp.float32)
    router_grad = lax.dot_general(
        normed_two_f,
        logit_grad,
        (((0,), (0,)), ((), ())),
        precision=lax.Precision.HIGHEST,
        preferred_element_type=jnp.float32,
    )
    normed_two_grad = normed_two_grad + lax.dot_general(
        logit_grad,
        router_f,
        (((1,), (1,)), ((), ())),
        precision=lax.Precision.HIGHEST,
        preferred_element_type=jnp.float32,
    )
    gain_two_grad, middle_part = norm_backward(middle, inverse_two, gain_two_f, normed_two_grad)
    middle_grad = out_grad + middle_part
    branch_grad = middle_grad.astype(jnp.bfloat16)
    output_weight_grad = contract_rows(attended, branch_grad)
    attended_grad = times_transposed(branch_grad, w_out).astype(jnp.bfloat16)
    keys_back, values_back, labels_back = (keys_all, values_all, labels_all)
    probs_back, log_back = make_probs(queries, keys_back, allowed)
    grad_heads = attended_grad.reshape(tok_rows, HEADS, HD)
    query_heads = queries.reshape(tok_rows, HEADS, HD)
    key_heads = keys_back.reshape(keys_back.shape[0], HEADS, HD)
    value_heads_back = values_back.reshape(values_back.shape[0], HEADS, HD)
    prob_grad_att = jnp.einsum(
        "qhd,khd->hqk", grad_heads, value_heads_back, preferred_element_type=jnp.float32
    )
    centre = jnp.sum(probs_back * prob_grad_att, axis=-1, keepdims=True)
    score_grad = (probs_back * (prob_grad_att - centre)).astype(jnp.bfloat16)
    query_act_grad = (
        (
            jnp.einsum("hqk,khd->qhd", score_grad, key_heads, preferred_element_type=jnp.float32)
            * HD ** (-0.5)
        )
        .reshape(tok_rows, width)
        .astype(jnp.bfloat16)
    )
    key_part = (
        jnp.einsum("hqk,qhd->khd", score_grad, query_heads, preferred_element_type=jnp.float32)
        * HD ** (-0.5)
    ).reshape(keys_back.shape[0], width)
    value_part = jnp.einsum(
        "hqk,qhd->khd",
        probs_back.astype(jnp.bfloat16),
        grad_heads,
        preferred_element_type=jnp.float32,
    ).reshape(values_back.shape[0], width)
    key_sum, value_sum = (
        lax.psum_scatter(
            key_part.astype(jnp.bfloat16), "ep", scatter_dimension=0, tiled=True
        ).astype(jnp.float32),
        lax.psum_scatter(
            value_part.astype(jnp.bfloat16), "ep", scatter_dimension=0, tiled=True
        ).astype(jnp.float32),
    )
    key_act_grad = key_sum.astype(jnp.bfloat16)
    value_act_grad = value_sum.astype(jnp.bfloat16)
    query_w_grad = contract_rows(normed_one, query_act_grad)
    key_w_grad = contract_rows(normed_one, key_act_grad)
    value_w_grad = contract_rows(normed_one, value_act_grad)
    normed_one_grad = (
        times_transposed(query_act_grad, w_query)
        + times_transposed(key_act_grad, w_key)
        + times_transposed(value_act_grad, w_value)
    )
    gain_one_grad, input_part = norm_backward(inputs, inverse_one, gain_one_f, normed_one_grad)
    input_grad = middle_grad + input_part
    local_counts = jnp.sum(flat_marks, axis=0).astype(jnp.float32)
    count_table = jnp.tile(
        local_counts.reshape(group_devices, local_experts), (lax.axis_size("wide"), 1)
    )
    summed_all = (
        lax.psum_scatter(gain_one_grad, ("wide", "ep"), scatter_dimension=0, tiled=True),
        lax.psum_scatter(query_w_grad, ("wide", "ep"), scatter_dimension=0, tiled=True),
        lax.psum_scatter(key_w_grad, ("wide", "ep"), scatter_dimension=0, tiled=True),
        lax.psum_scatter(value_w_grad, ("wide", "ep"), scatter_dimension=0, tiled=True),
        lax.psum_scatter(output_weight_grad, ("wide", "ep"), scatter_dimension=0, tiled=True),
        lax.psum_scatter(gain_two_grad, ("wide", "ep"), scatter_dimension=0, tiled=True),
        lax.psum_scatter(router_grad, ("wide", "ep"), scatter_dimension=0, tiled=True),
        lax.psum_scatter(shared_gate_grad, ("wide", "ep"), scatter_dimension=0, tiled=True),
        lax.psum_scatter(shared_up_grad, ("wide", "ep"), scatter_dimension=0, tiled=True),
        lax.psum_scatter(shared_down_grad, ("wide", "ep"), scatter_dimension=0, tiled=True),
        lax.psum_scatter(count_table, ("wide", "ep"), scatter_dimension=0, tiled=True),
    )
    expert_counts = summed_all[10][0].astype(jnp.int32)
    return (
        block_out,
        input_grad,
        summed_all[0],
        summed_all[1],
        summed_all[2],
        summed_all[3],
        summed_all[4],
        summed_all[5],
        summed_all[6],
        summed_all[7],
        summed_all[8],
        summed_all[9],
        expert_gate_grad,
        expert_up_grad,
        expert_down_grad,
        expert_counts,
    )


def solution(mesh):
    in_specs = (
        P(("wide", "ep"), None),
        P(("wide", "ep")),
        P(("wide", "ep"), None),
        P(("wide", "ep")),
        P(("wide", "ep"), None),
        P(("wide", "ep"), None),
        P(("wide", "ep"), None),
        P(("wide", "ep"), None),
        P(("wide", "ep")),
        P(("wide", "ep"), None),
        P(("wide", "ep"), None),
        P(("wide", "ep"), None),
        P(("wide", "ep"), None),
        P("ep", None, None),
        P("ep", None, None),
        P("ep", None, None),
        P(("wide", "ep"), None),
    )
    out_specs = (
        P(("wide", "ep"), None),
        P(("wide", "ep"), None),
        P(("wide", "ep")),
        P(("wide", "ep"), None),
        P(("wide", "ep"), None),
        P(("wide", "ep"), None),
        P(("wide", "ep"), None),
        P(("wide", "ep")),
        P(("wide", "ep"), None),
        P(("wide", "ep"), None),
        P(("wide", "ep"), None),
        P(("wide", "ep"), None),
        P("ep", "wide", None),
        P("ep", "wide", None),
        P("ep", "wide", None),
        P("ep"),
    )
    return jax.shard_map(body, mesh=mesh, in_specs=in_specs, out_specs=out_specs, check_vma=False)
```

profile of v0, /device:TPU:0, one launch (start us, length us, event | category | flops | bytes accessed | tf_op | source)
XLA Modules:
  0.0 2505.0 jit_solution(10555876959186416773)
XLA Ops:
  11.2 42.2 %all-reduce.11 = (bf16[1280]{0:T(1024)(128)(2,1)S(1)}, bf16[1280]{0:T(1024)(128)(2,1)S(1)}) all-reduce(bf16[1280]{0:T(1024)(128)(2,1)S(1)} %dynamic-update-slice, bf16[1280]{0:T(1024)(128)(2,1)S(1)} %dynamic-update-slice.1), channel_id=1, replica_groups=mesh['wide'=8,'ep'=4] {'wide','ep'}, use_global_device_ids=true, to_apply=%add | all-reduce | flops 2560 | bytes 10240
  55.3 17.6 all-gather.19.cloned.1.call-done
  77.1 56.8 %all-gather.13.cloned.1.call-done = bf16[1280,1280]{1,0:T(8,128)(2,1)} async-done(((bf16[40,1280]{1,0:T(8,128)(2,1)}), bf16[1280,1280]{1,0:T(8,128)(2,1)}) %all-gather.13.cloned.1.call-update) | async-done | bytes 3276816 | tf_op jit(solution)/shard_map/all_gather | solution.py:87
  151.5 43.5 %all-gather.17.cloned.1.call-done = bf16[1280,1280]{1,0:T(8,128)(2,1)} async-done(((bf16[40,1280]{1,0:T(8,128)(2,1)}), bf16[1280,1280]{1,0:T(8,128)(2,1)}) %all-gather.17.cloned.1.call-update) | async-done | bytes 3276816 | tf_op jit(solution)/shard_map/all_gather | solution.py:85
  199.1 22.4 all-gather.21.cloned.1.call-done
  224.5 24.6 all-gather.15.cloned.1.call-done
  264.8 46.3 %all-gather.23.cloned.1.call-done = bf16[1280,1280]{1,0:T(8,128)(2,1)} async-done(((bf16[40,1280]{1,0:T(8,128)(2,1)}), bf16[1280,1280]{1,0:T(8,128)(2,1)}) %all-gather.23.cloned.1.call-update) | async-done | bytes 3276816 | tf_op jit(solution)/shard_map/all_gather | solution.py:88
  326.0 15.9 scatter_custom_fusion
  341.9 78.0 %all_to_all.60 = bf16[16,160,1280]{2,1,0:T(8,128)(2,1)S(1)} all-to-all(bf16[16,160,1280]{2,1,0:T(8,128)(2,1)} %bitcast.302), channel_id=1, replica_groups=mesh['wide'=8,'ep'=4] {'ep'}, dimensions={0} | all-to-all | bytes 13107200 | tf_op jit(solution)/shard_map/all_to_all | solution.py:152
  471.9 112.2 %all-gather.2 = bf16[32,40,16]{1,2,0:T(8,128)(2,1)S(1)} all-gather(bf16[1,40,16]{1,2,0:T(8,128)(2,1)S(1)} %bitcast.346), channel_id=1, replica_groups=mesh['wide'=8,'ep'=4] {'wide','ep'}, dimensions={0}, use_global_device_ids=true | all-gather | bytes 42240 | tf_op jit(solution)/shard_map/all_gather | solution.py:90
  648.5 22.8 scatter_custom_fusion.1
  678.1 79.1 %all-to-all-done.2 = bf16[16,160,1280]{2,1,0:T(8,128)(2,1)} async-done(((bf16[16,160,1280]{2,1,0:T(8,128)(2,1)}), bf16[16,160,1280]{2,1,0:T(8,128)(2,1)}, u32[]{:S(2)}, u32[]{:S(2)}) %all-to-all-start.2) | async-done | bytes 6553632 | tf_op jit(solution)/shard_map/all_to_all | solution.py:203
  838.2 59.7 %all-to-all-done.3 = bf16[4,640,1280]{2,0,1:T(4,128)(2,1)} async-done(((bf16[4,640,1280]{2,0,1:T(4,128)(2,1)}), bf16[4,640,1280]{2,0,1:T(4,128)(2,1)}, u32[]{:S(2)}, u32[]{:S(2)}) %all-to-all-start.3) | async-done | bytes 6553632 | tf_op jit(solution)/shard_map/all_to_all | solution.py:241
  1057.3 79.8 %fusion = f32[32,1280]{1,0:T(8,128)S(1)} fusion(f32[896,1280]{1,0:T(8,128)} %fusion.163), kind=kCustom, calls=%all-reduce-scatter | all-reduce-scatter fusion | flops 1310721 | bytes 4751360
  1164.7 44.3 %all-reduce.10 = (f32[1280]{0:T(1024)S(1)}, f32[1280]{0:T(1024)S(1)}, f32[32,4]{0,1:T(4,128)S(1)}) all-reduce(f32[1280]{0:T(1024)S(1)} %get-tuple-element.18, f32[1280]{0:T(1024)S(1)} %get-tuple-element.16, f32[32,4]{0,1:T(4,128)S(1)} %tile.9), channel_id=4, replica_groups=mesh['wide'=8,'ep'=4] {'wide','ep'}, use_global_device_ids=true, to_apply=%region_20.21.clone | all-reduce | flops 2688 | bytes 21504
  1212.2 99.5 %reduce-scatter.38.cloned.1.call-done = bf16[4,112,1280]{2,1,0:T(8,128)(2,1)} async-done(((bf16[4,896,1280]{2,1,0:T(8,128)(2,1)}), bf16[4,112,1280]{2,1,0:T(8,128)(2,1)}) %reduce-scatter.38.cloned.1.call-update) | async-done | bytes 1146896 | tf_op jit(solution)/shard_map/reduce_scatter | solution.py:237
  1314.5 160.0 %reduce-scatter.36.cloned.1.call-done = bf16[4,160,896]{2,1,0:T(8,128)(2,1)} async-done(((bf16[4,1280,896]{2,1,0:T(8,128)(2,1)}), bf16[4,160,896]{2,1,0:T(8,128)(2,1)}) %reduce-scatter.36.cloned.1.call-update) | async-done | bytes 1146896 | tf_op jit(solution)/shard_map/reduce_scatter | solution.py:234
  1477.3 159.7 %reduce-scatter.34.cloned.1.call-done = bf16[4,160,896]{2,1,0:T(8,128)(2,1)} async-done(((bf16[4,1280,896]{2,1,0:T(8,128)(2,1)}), bf16[4,160,896]{2,1,0:T(8,128)(2,1)}) %reduce-scatter.34.cloned.1.call-update) | async-done | bytes 1146896 | tf_op jit(solution)/shard_map/reduce_scatter | solution.py:231
  1639.8 141.0 %reduce-scatter.40.cloned.1.call-done = f32[40,896]{1,0:T(8,128)} async-done(((f32[1280,896]{1,0:T(8,128)}), f32[40,896]{1,0:T(8,128)}) %reduce-scatter.40.cloned.1.call-update) | async-done | bytes 143376
  1780.8 140.4 %reduce-scatter.42.cloned.1.call-done = f32[40,896]{1,0:T(8,128)} async-done(((f32[1280,896]{1,0:T(8,128)}), f32[40,896]{1,0:T(8,128)}) %reduce-scatter.42.cloned.1.call-update) | async-done | bytes 143376
  1921.2 143.9 %reduce-scatter.32.cloned.1.call-done = f32[40,1280]{1,0:T(8,128)} async-done(((f32[1280,1280]{1,0:T(8,128)}), f32[40,1280]{1,0:T(8,128)}) %reduce-scatter.32.cloned.1.call-update) | async-done | bytes 204816 | tf_op jit(solution)/shard_map/reduce_scatter | solution.py:333
  2065.0 144.2 %reduce-scatter.26.cloned.1.call-done = f32[40,1280]{1,0:T(8,128)} async-done(((f32[1280,1280]{1,0:T(8,128)}), f32[40,1280]{1,0:T(8,128)}) %reduce-scatter.26.cloned.1.call-update) | async-done | bytes 204816 | tf_op jit(solution)/shard_map/reduce_scatter | solution.py:330
  2209.3 144.2 %reduce-scatter.30.cloned.1.call-done = f32[40,1280]{1,0:T(8,128)} async-done(((f32[1280,1280]{1,0:T(8,128)}), f32[40,1280]{1,0:T(8,128)}) %reduce-scatter.30.cloned.1.call-update) | async-done | bytes 204816 | tf_op jit(solution)/shard_map/reduce_scatter | solution.py:332
  2353.4 144.5 %reduce-scatter.28.cloned.1.call-done = f32[40,1280]{1,0:T(8,128)} async-done(((f32[1280,1280]{1,0:T(8,128)}), f32[40,1280]{1,0:T(8,128)}) %reduce-scatter.28.cloned.1.call-update) | async-done | bytes 204816 | tf_op jit(solution)/shard_map/reduce_scatter | solution.py:331
  (477 shorter events, 466.2 us)
Async XLA Ops:
  7.2 65.7 %all-gather.19.cloned.1.call-start = ((), (), s32[]{:S(2)}) async-start(), calls=%async_computation.18 | async-start | bytes 3379200 | tf_op jit(solution)/shard_map/all_gather | solution.py:86
  7.9 126.0 %all-gather.13.cloned.1.call-start = ((), (), s32[]{:S(2)}) async-start(), calls=%async_computation.15 | async-start | bytes 3379200 | tf_op jit(solution)/shard_map/all_gather | solution.py:87
  8.7 186.3 %all-gather.17.cloned.1.call-start = ((), (), s32[]{:S(2)}) async-start(), calls=%async_computation.17 | async-start | bytes 3379200 | tf_op jit(solution)/shard_map/all_gather | solution.py:85
  9.4 212.1 %all-gather.21.cloned.1.call-start = ((), (), s32[]{:S(2)}) async-start(), calls=%async_computation.19 | async-start | bytes 3276800 | tf_op jit(solution)/shard_map/all_gather | solution.py:114
  77.0 172.0 %all-gather.15.cloned.1.call-start = ((), (), s32[]{:S(2)}) async-start(), calls=%async_computation.16 | async-start | bytes 3276800 | tf_op jit(solution)/shard_map/all_gather | solution.py:115
  137.8 173.3 %all-gather.23.cloned.1.call-start = ((), (), s32[]{:S(2)}) async-start(), calls=%async_computation.20 | async-start | bytes 3379200 | tf_op jit(solution)/shard_map/all_gather | solution.py:88
  465.7 134.3 %all-to-all-start.1 = ((bf16[4,640,1280]{2,0,1:T(4,128)(2,1)}), bf16[4,640,1280]{2,0,1:T(4,128)(2,1)}, u32[]{:S(2)}, u32[]{:S(2)}) async-start(bf16[4,640,1280]{2,0,1:T(4,128)(2,1)} %copy.102), calls=%async_computation.1 | async-start | bytes 13107200 | tf_op jit(solution)/shard_map/all_to_all | solution.py:168
  471.1 353.8 %all-gather.29.cloned.1.call-start = ((), (), s32[]{:S(2)}) async-start(), calls=%async_computation.32 | async-start | bytes 2703360 | tf_op jit(solution)/shard_map/all_gather | solution.py:93
  671.3 85.9 %all-to-all-start.2 = ((bf16[16,160,1280]{2,1,0:T(8,128)(2,1)}), bf16[16,160,1280]{2,1,0:T(8,128)(2,1)}, u32[]{:S(2)}, u32[]{:S(2)}) async-start(bf16[16,160,1280]{2,1,0:T(8,128)(2,1)} %bitcast.300), calls=%async_computation.2 | async-start | bytes 13107200 | tf_op jit(solution)/shard_map/all_to_all | solution.py:203
  676.6 151.0 %all-gather.25.cloned.1.call-start = ((), (), s32[]{:S(2)}) async-start(), calls=%async_computation.21 | async-start | bytes 2365440 | tf_op jit(solution)/shard_map/all_gather | solution.py:91
  677.4 154.5 %all-gather.27.cloned.1.call-start = ((), (), s32[]{:S(2)}) async-start(), calls=%async_computation.22 | async-start | bytes 2365440 | tf_op jit(solution)/shard_map/all_gather | solution.py:92
  819.1 78.8 %all-to-all-start.3 = ((bf16[4,640,1280]{2,0,1:T(4,128)(2,1)}), bf16[4,640,1280]{2,0,1:T(4,128)(2,1)}, u32[]{:S(2)}, u32[]{:S(2)}) async-start(bf16[4,640,1280]{2,0,1:T(4,128)(2,1)} %copy.105), calls=%async_computation.3 | async-start | bytes 13107200 | tf_op jit(solution)/shard_map/all_to_all | solution.py:241
  824.5 218.6 %reduce-scatter.24.cloned.1.call-start = ((), (), s32[]{:S(2)}) async-start(), calls=%async_computation.24 | async-start | bytes 3276800 | tf_op jit(solution)/shard_map/reduce_scatter | solution.py:308
  951.8 96.3 %reduce-scatter.22.cloned.1.call-start = ((), (), s32[]{:S(2)}) async-start(), calls=%async_computation.23 | async-start | bytes 3276800 | tf_op jit(solution)/shard_map/reduce_scatter | solution.py:305
  969.9 186.1 %all-reduce.14.cloned.1.call-start = ((), (), s32[]{:S(2)}) async-start(), calls=%async_computation.33 | async-start | bytes 163840
  971.0 340.7 %reduce-scatter.38.cloned.1.call-start = ((), (), s32[]{:S(2)}) async-start(), calls=%async_computation.31 | async-start | bytes 10321920 | tf_op jit(solution)/shard_map/reduce_scatter | solution.py:237
  986.2 488.3 %reduce-scatter.36.cloned.1.call-start = ((), (), s32[]{:S(2)}) async-start(), calls=%async_computation.30 | async-start | bytes 10321920 | tf_op jit(solution)/shard_map/reduce_scatter | solution.py:234
  1002.6 634.4 %reduce-scatter.34.cloned.1.call-start = ((), (), s32[]{:S(2)}) async-start(), calls=%async_computation.29 | async-start | bytes 10321920 | tf_op jit(solution)/shard_map/reduce_scatter | solution.py:231
  1019.2 761.6 %reduce-scatter.40.cloned.1.call-start = ((), (), s32[]{:S(2)}) async-start(), calls=%async_computation.34 | async-start | bytes 4730880
  1023.3 897.9 %reduce-scatter.42.cloned.1.call-start = ((), (), s32[]{:S(2)}) async-start(), calls=%async_computation.35 | async-start | bytes 4730880
  1027.3 1037.8 %reduce-scatter.32.cloned.1.call-start = ((), (), s32[]{:S(2)}) async-start(), calls=%async_computation.28 | async-start | bytes 6758400 | tf_op jit(solution)/shard_map/reduce_scatter | solution.py:333
  1032.1 1177.1 %reduce-scatter.26.cloned.1.call-start = ((), (), s32[]{:S(2)}) async-start(), calls=%async_computation.25 | async-start | bytes 6758400 | tf_op jit(solution)/shard_map/reduce_scatter | solution.py:330
  1043.0 1310.5 %reduce-scatter.30.cloned.1.call-start = ((), (), s32[]{:S(2)}) async-start(), calls=%async_computation.27 | async-start | bytes 6758400 | tf_op jit(solution)/shard_map/reduce_scatter | solution.py:332
  1048.1 1449.8 %reduce-scatter.28.cloned.1.call-start = ((), (), s32[]{:S(2)}) async-start(), calls=%async_computation.26 | async-start | bytes 6758400 | tf_op jit(solution)/shard_map/reduce_scatter | solution.py:331
  (130 other events, 2027.5 us)
Sparse Core Ops, SparseCore 0:
  10.9 61.9 all-gather.18
  75.7 58.1 all-gather.12
  136.8 58.1 all-gather.16
  197.0 24.4 all-gather.20
  223.4 25.5 all-gather.14
  251.8 59.2 all-gather.22
  474.8 63.2 all-gather.28
  680.4 59.2 all-gather.24
  742.7 55.9 all-gather.26
  952.0 30.7 reduce-scatter.23
  985.5 34.6 reduce-scatter.21
  1025.7 120.1 all-reduce.13
  1149.5 162.1 reduce-scatter.37
  1315.7 158.7 reduce-scatter.35
  1478.0 158.9 reduce-scatter.33
  1639.8 140.9 reduce-scatter.39
  1783.6 137.5 reduce-scatter.41
  1924.0 140.9 reduce-scatter.31
  2068.0 141.1 reduce-scatter.25
  2212.1 141.3 reduce-scatter.29
  2356.4 141.4 reduce-scatter.27
where the time goes:
time: 2510 us; the launch traced here: 2500 us
  waiting for transfers between devices  1640 us (65%)
  blocking collectives  362 us (14%)
  matrix products  203 us (8%)
  local copies, waits for them, and re-layouts  179 us (7%)
  other arithmetic  87.1 us (3%)
    unnamed x28, waiting for transfers between devices  289 us
    unnamed x3, blocking collectives  166 us
    reduce_scatter x1, waiting for transfers between devices, body(): lax.psum_scatter(jnp.stack(up_grad_list).astype(jnp.bfloat16), 'wide', sc...  160 us
    reduce_scatter x1, waiting for transfers between devices, body(): lax.psum_scatter(jnp.stack(gate_grad_list).astype(jnp.bfloat16), 'wide',...  160 us
    reduce_scatter x1, waiting for transfers between devices, body(): lax.psum_scatter(key_w_grad, ('wide', 'ep'), scatter_dimension=0, tiled=T...  144 us
    reduce_scatter x1, waiting for transfers between devices, body(): lax.psum_scatter(query_w_grad, ('wide', 'ep'), scatter_dimension=0, tiled...  144 us
    reduce_scatter x1, waiting for transfers between devices, body(): lax.psum_scatter(value_w_grad, ('wide', 'ep'), scatter_dimension=0, tiled...  144 us
    reduce_scatter x1, waiting for transfers between devices, body(): lax.psum_scatter(output_weight_grad, ('wide', 'ep'), scatter_dimension=0,...  144 us
  transfers between devices with their start and end apart: 28, of which 18 were waited for; matrix products, arithmetic and copies ran while one was open for 16% of the time, Pallas kernels for 0%

commit v1 on v0

v1 whole, which is shorter than its diff:
```python
import functools

import jax
import jax.numpy as jnp
from jax import lax
from jax.sharding import PartitionSpec as P

HD = 128
NC = 2
NZ = 4
ZP = 2
epsilon = 1e-06
masked_value = -1e30
BOTH = ("wide", "ep")
f32 = jnp.float32
bf16 = jnp.bfloat16


def contract_rows(left, right):
    return lax.dot_general(
        left, right, (((0,), (0,)), ((), ())), preferred_element_type=f32
    )


def times_transposed(left, right):
    return lax.dot_general(
        left, right, (((1,), (1,)), ((), ())), preferred_element_type=f32
    )


def times(left, right):
    return jnp.dot(left, right, preferred_element_type=f32)


def norm_scale(values):
    return lax.rsqrt(jnp.mean(values * values, axis=-1, keepdims=True) + epsilon)


def norm_backward(values, inverse, gain, normed_grad):
    weighted = normed_grad * gain
    gain_grad = jnp.sum(normed_grad * values * inverse, axis=0)
    cubed = inverse * inverse * inverse
    values_grad = inverse * weighted - values * cubed * jnp.mean(
        weighted * values, axis=-1, keepdims=True
    )
    return (gain_grad, values_grad)


def silu_parts(gate_act):
    logistic = jax.nn.sigmoid(gate_act)
    return (gate_act * logistic, logistic * (1.0 + gate_act * (1.0 - logistic)))


class Grid:
    def __init__(self, wide, ep):
        self.ny, self.nx, self.ep = wide // NZ, ep // NC, ep
        w, e = lax.axis_index("wide"), lax.axis_index("ep")
        self.z, self.y, self.x, self.c = w // self.ny, w % self.ny, e // NC, e % NC
        self.zm = self.z % ZP

    def pairs(self, move):
        made = []
        for z in range(NZ):
            for y in range(self.ny):
                for x in range(self.nx):
                    for c in range(NC):
                        tz, ty, tx, tc = move(z, y, x, c)
                        made.append(
                            (
                                (z * self.ny + y) * self.ep + x * NC + c,
                                (tz * self.ny + ty) * self.ep + tx * NC + tc,
                            )
                        )
        return made

    def send(self, value, axis, step):
        moves = {
            "c": lambda z, y, x, c: (z, y, x, (c + step) % NC),
            "x": lambda z, y, x, c: (z, y, (x + step) % self.nx, c),
            "y": lambda z, y, x, c: (z, (y + step) % self.ny, x, c),
            "z": lambda z, y, x, c: ((z + step) % NZ, y, x, c),
            "p": lambda z, y, x, c: (z // ZP * ZP + (z % ZP + step) % ZP, y, x, c),
        }
        return lax.ppermute(value, BOTH, self.pairs(moves[axis]))

    def size(self, axis):
        return {"c": NC, "x": self.nx, "y": self.ny, "z": NZ, "p": ZP}[axis]

    def place(self, axis):
        return {"c": self.c, "x": self.x, "y": self.y, "z": self.z, "p": self.zm}[axis]

    def gather(self, value, axis, at):
        parts = [value] + [
            self.send(value, axis, -d) for d in range(1, self.size(axis))
        ]
        return jnp.stack(parts, axis=at)

    def scatter(self, value, axis, at):
        total = lax.index_in_dim(value, 0, at, keepdims=False).astype(f32)
        for d in range(1, self.size(axis)):
            part = lax.index_in_dim(value, d, at, keepdims=False)
            total = total + self.send(part, axis, d).astype(f32)
        return total.astype(value.dtype)

    def scatter_absolute(self, value, axis, at):
        n, me = self.size(axis), self.place(axis)
        take = lambda i: lax.dynamic_index_in_dim(value, i, at, keepdims=False)
        total = take(me).astype(f32)
        for d in range(1, n):
            total = total + self.send(take((me + d) % n), axis, d).astype(f32)
        return total.astype(value.dtype)


def attention_bias(segment, labels_all, query_places, key_places):
    same_doc = segment[:, None] == labels_all[None, :]
    allowed = same_doc & (query_places[:, None] >= key_places[None, :])
    return jnp.where(allowed, 0.0, masked_value).astype(f32)


def make_probs(query_heads, key_heads, bias):
    scores = (
        jnp.einsum("qhd,khd->hqk", query_heads, key_heads, preferred_element_type=f32)
        * HD ** (-0.5)
    )
    scores = scores + bias[None]
    largest = jnp.max(scores, axis=-1, keepdims=True)
    weights = jnp.exp(scores - largest)
    return weights * (1.0 / jnp.sum(weights, axis=-1, keepdims=True))


def reduce_dense(grid, value, order):
    names = ["z", "y", "x", "c"]
    for axis in order:
        at = names.index(axis)
        value = grid.scatter_absolute(value, axis, at)
        names.pop(at)
    return value


def reduce_experts(grid, value):
    mine, rows, columns = value.shape
    value = value.reshape(mine, NZ, grid.ny, rows // (NZ * grid.ny), columns)
    value = grid.scatter_absolute(value, "y", 2)
    take = lambda i: lax.dynamic_index_in_dim(value, i, 1, keepdims=False)
    sums = [take(grid.z).astype(f32), None]
    for d in range(1, NZ):
        got = grid.send(take((grid.z + d) % NZ), "z", d).astype(f32)
        sums[d % ZP] = got if sums[d % ZP] is None else sums[d % ZP] + got
    first = jnp.where(grid.zm == 0, sums[0], sums[1])
    second = jnp.where(grid.zm == 0, sums[1], sums[0])
    return jnp.concatenate([first, second], axis=0)


def body(
    wide,
    ep,
    activations,
    segment,
    routes,
    gain_attention,
    query_weight,
    key_weight,
    value_weight,
    output_weight,
    gain_experts,
    router_weight,
    shared_gate,
    shared_up,
    shared_down,
    expert_gate,
    expert_up,
    expert_down,
    cotangent,
):
    grid = Grid(wide, ep)
    nx, ny = grid.nx, grid.ny
    tok_rows, width = activations.shape
    heads = width // HD
    top_count = routes.shape[1]
    experts = router_weight.shape[1]
    local_experts = expert_gate.shape[0]
    mine = local_experts // ZP
    hidden_width = expert_gate.shape[2]
    sources = ZP * nx * NC
    capacity = min((tok_rows * top_count * 10 // (7 * experts) + 7) // 8 * 8, tok_rows)

    small = jnp.concatenate(
        [
            router_weight,
            gain_attention[:, None],
            gain_experts[:, None],
            jnp.zeros((gain_experts.shape[0], 128 - experts - 2), bf16),
        ],
        axis=1,
    )
    gather_all = lambda v: lax.all_gather(v, BOTH, axis=0, tiled=True)
    small_all = gather_all(small)
    w_query = gather_all(query_weight)
    w_key = gather_all(key_weight)
    w_value = gather_all(value_weight)
    w_out = gather_all(output_weight)
    s_gate = gather_all(shared_gate)
    s_up = gather_all(shared_up)
    s_down = gather_all(shared_down)
    w_router = small_all[:, :experts]
    gain_one = small_all[:, experts].astype(f32)
    gain_two = small_all[:, experts + 1].astype(f32)

    def gather_group(v):
        return grid.gather(grid.gather(v, "c", 0), "x", 0)

    def gather_pair(v):
        return grid.gather(gather_group(v), "p", 0)

    integers = jnp.concatenate([routes.T, segment[None, :]], axis=0)
    integers_all = gather_pair(integers).reshape(sources, top_count + 1, tok_rows)
    group_rows = gather_group(activations).reshape(nx * NC * tok_rows, width)
    cot_all = gather_pair(cotangent).reshape(sources, tok_rows, width)

    inputs = activations.astype(f32)
    inverse_one = norm_scale(inputs)
    group_inputs = group_rows.astype(f32)
    normed_group = (group_inputs * norm_scale(group_inputs) * gain_one).astype(bf16)
    normed_one = normed_group[:tok_rows]
    queries = times(normed_one, w_query).astype(bf16)
    keys_all = times(normed_group, w_key).astype(bf16)
    values_all = times(normed_group, w_value).astype(bf16)
    labels_all = integers_all[: nx * NC, top_count].reshape(-1)
    steps = jnp.arange(tok_rows, dtype=jnp.int32)
    block_places = (
        (grid.x + jnp.arange(nx, dtype=jnp.int32)[:, None]) % nx * NC
        + (grid.c + jnp.arange(NC, dtype=jnp.int32)[None, :]) % NC
    ).reshape(-1)
    key_places = (block_places[:, None] * tok_rows + steps[None, :]).reshape(-1)
    query_places = (grid.x * NC + grid.c) * tok_rows + steps
    bias = attention_bias(segment, labels_all, query_places, key_places)
    query_heads = queries.reshape(-1, heads, HD)
    key_heads = keys_all.reshape(-1, heads, HD)
    value_heads = values_all.reshape(-1, heads, HD)
    probs = make_probs(query_heads, key_heads, bias)
    attended = (
        jnp.einsum(
            "hqk,khd->qhd", probs.astype(bf16), value_heads, preferred_element_type=f32
        )
        .reshape(tok_rows, width)
        .astype(bf16)
    )
    middle = inputs + times(attended, w_out)
    inverse_two = norm_scale(middle)
    normed_two = (middle * inverse_two * gain_two).astype(bf16)

    rows_all = gather_pair(normed_two).reshape(sources, tok_rows, width)
    router_probs_all = jax.nn.softmax(
        times(rows_all.reshape(-1, width), w_router).reshape(sources, tok_rows, experts),
        axis=-1,
    )
    router_probs = router_probs_all[0]
    first_expert = (grid.x * NC + grid.c) * local_experts + grid.zm * mine
    routes_all = integers_all[:, :top_count]
    numbers = first_expert + jnp.arange(mine, dtype=jnp.int32)
    marks = jnp.any(
        routes_all[None] == numbers[:, None, None, None], axis=2
    )
    earlier = (steps[:, None] < steps[None, :]).astype(bf16)
    ranks = jnp.einsum(
        "irt,tu->iru", marks.astype(bf16), earlier, preferred_element_type=f32
    ).astype(jnp.int32)
    slots = jnp.arange(capacity, dtype=jnp.int32)
    chosen = marks[:, :, None, :] & (ranks[:, :, None, :] == slots[None, None, :, None])
    picks = chosen.astype(bf16)
    gates_mine = jnp.moveaxis(
        lax.dynamic_slice_in_dim(router_probs_all, first_expert, mine, axis=2), 2, 0
    )
    gate_rows = jnp.sum(
        jnp.where(chosen, gates_mine[:, :, None, :], 0.0), axis=-1
    ).reshape(mine, sources * capacity, 1)
    out_parts = 0.0
    row_parts = 0.0
    prob_parts = []
    gate_w_grads, up_w_grads, down_w_grads = [], [], []
    w_gates = lax.dynamic_slice_in_dim(expert_gate, grid.zm * mine, mine, axis=0)
    w_ups = lax.dynamic_slice_in_dim(expert_up, grid.zm * mine, mine, axis=0)
    w_downs = lax.dynamic_slice_in_dim(expert_down, grid.zm * mine, mine, axis=0)
    for i in range(mine):
        pick = lambda v: (
            jnp.einsum("rst,rtd->rsd", picks[i], v, preferred_element_type=f32)
            .astype(bf16)
            .reshape(sources * capacity, width)
        )
        unpick = lambda v: jnp.einsum(
            "rst,rsd->rtd",
            picks[i],
            v.reshape(sources, capacity, width),
            preferred_element_type=f32,
        )
        rows_here = pick(rows_all)
        cot_here = pick(cot_all).astype(f32)
        slot_here = (gate_rows[i] * cot_here).astype(bf16)
        gate_act = times(rows_here, w_gates[i])
        up_act = times(rows_here, w_ups[i])
        activated, slope = silu_parts(gate_act)
        hidden = (activated * up_act).astype(bf16)
        produced = times(hidden, w_downs[i]).astype(bf16).astype(f32)
        row_probs = jnp.sum(produced * cot_here, axis=-1).reshape(sources, capacity, 1)
        prob_parts.append(jnp.sum(jnp.where(chosen[i], row_probs, 0.0), axis=1))
        out_parts = out_parts + unpick((gate_rows[i] * produced).astype(bf16))
        hidden_grad = times_transposed(slot_here, w_downs[i])
        act_gate = (hidden_grad * up_act * slope).astype(bf16)
        act_up = (hidden_grad * activated).astype(bf16)
        down_w_grads.append(contract_rows(hidden, slot_here).astype(bf16))
        gate_w_grads.append(contract_rows(rows_here, act_gate).astype(bf16))
        up_w_grads.append(contract_rows(rows_here, act_up).astype(bf16))
        row_grad = (
            times_transposed(act_gate, w_gates[i]) + times_transposed(act_up, w_ups[i])
        ).astype(bf16)
        row_parts = row_parts + unpick(row_grad)

    def scatter_pair(v):
        v = v.reshape((ZP, nx, NC) + v.shape[1:])
        return grid.scatter(grid.scatter(grid.scatter(v, "c", 2), "x", 1), "p", 0)

    routed_grad = scatter_pair(row_parts.astype(bf16)).astype(f32)
    routed = scatter_pair(out_parts.astype(bf16)).astype(f32)
    expert_down_grad = reduce_experts(grid, jnp.stack(down_w_grads))
    expert_gate_grad = reduce_experts(grid, jnp.stack(gate_w_grads))
    expert_up_grad = reduce_experts(grid, jnp.stack(up_w_grads))
    sent = jnp.stack(prob_parts, axis=1).reshape(ZP, nx, NC, mine, tok_rows)
    for axis, at in (("c", 2), ("x", 1), ("p", 0)):
        n = grid.size(axis)
        parts = [lax.index_in_dim(sent, d, at, keepdims=False) for d in range(n)]
        got = [parts[0]] + [grid.send(parts[n - d], axis, n - d) for d in range(1, n)]
        sent = jnp.stack(got, axis=at)
    dz = (grid.zm + jnp.arange(ZP, dtype=jnp.int32)) % ZP
    owner = block_places.reshape(1, nx, NC, 1) * local_experts
    owner = owner + dz[:, None, None, None] * mine + jnp.arange(mine, dtype=jnp.int32)
    same = owner.reshape(-1)[None, :] == jnp.arange(experts, dtype=jnp.int32)[:, None]
    prob_grad = jnp.sum(
        jnp.where(same[:, :, None], sent.reshape(1, experts, tok_rows), 0.0), axis=1
    ).T

    shared_gate_act = times(normed_two, s_gate)
    shared_up_act = times(normed_two, s_up)
    shared_act, shared_slope = silu_parts(shared_gate_act)
    shared_hidden = (shared_act * shared_up_act).astype(bf16)
    shared_out = times(shared_hidden, s_down)
    out_grad = cotangent.astype(f32)
    shared_down_grad = contract_rows(shared_hidden, cotangent)
    shared_hidden_grad = times_transposed(cotangent, s_down)
    shared_gate_act_grad = (shared_hidden_grad * shared_up_act * shared_slope).astype(
        bf16
    )
    shared_up_act_grad = (shared_hidden_grad * shared_act).astype(bf16)
    shared_gate_grad = contract_rows(normed_two, shared_gate_act_grad)
    shared_up_grad = contract_rows(normed_two, shared_up_act_grad)
    normed_two_grad = times_transposed(shared_gate_act_grad, s_gate) + times_transposed(
        shared_up_act_grad, s_up
    )
    block_out = (middle + shared_out + routed).astype(bf16)

    logit_grad = router_probs * (
        prob_grad - jnp.sum(router_probs * prob_grad, axis=-1, keepdims=True)
    )
    router_grad = lax.dot_general(
        normed_two.astype(f32),
        logit_grad,
        (((0,), (0,)), ((), ())),
        precision=lax.Precision.HIGHEST,
        preferred_element_type=f32,
    )
    normed_two_grad = (
        normed_two_grad
        + routed_grad
        + lax.dot_general(
            logit_grad,
            w_router.astype(f32),
            (((1,), (1,)), ((), ())),
            precision=lax.Precision.HIGHEST,
            preferred_element_type=f32,
        )
    )
    gain_two_grad, middle_part = norm_backward(
        middle, inverse_two, gain_two, normed_two_grad
    )
    middle_grad = out_grad + middle_part
    branch_grad = middle_grad.astype(bf16)
    output_weight_grad = contract_rows(attended, branch_grad)
    attended_grad = times_transposed(branch_grad, w_out).astype(bf16)

    grad_heads = attended_grad.reshape(tok_rows, heads, HD)
    prob_grad_att = jnp.einsum(
        "qhd,khd->hqk", grad_heads, value_heads, preferred_element_type=f32
    )
    centre = jnp.sum(probs * prob_grad_att, axis=-1, keepdims=True)
    score_grad = (probs * (prob_grad_att - centre)).astype(bf16)
    query_act_grad = (
        (
            jnp.einsum("hqk,khd->qhd", score_grad, key_heads, preferred_element_type=f32)
            * HD ** (-0.5)
        )
        .reshape(tok_rows, width)
        .astype(bf16)
    )
    key_part = (
        jnp.einsum("hqk,qhd->khd", score_grad, query_heads, preferred_element_type=f32)
        * HD ** (-0.5)
    )
    value_part = jnp.einsum(
        "hqk,qhd->khd", probs.astype(bf16), grad_heads, preferred_element_type=f32
    )

    def scatter_group(v):
        v = v.astype(bf16).reshape(nx, NC, tok_rows, width)
        return grid.scatter(grid.scatter(v, "c", 1), "x", 0)

    value_act_grad = scatter_group(value_part)
    key_act_grad = scatter_group(key_part)
    query_w_grad = contract_rows(normed_one, query_act_grad)
    key_w_grad = contract_rows(normed_one, key_act_grad)
    value_w_grad = contract_rows(normed_one, value_act_grad)
    normed_one_grad = (
        times_transposed(query_act_grad, w_query)
        + times_transposed(key_act_grad, w_key)
        + times_transposed(value_act_grad, w_value)
    )
    gain_one_grad, input_part = norm_backward(
        inputs, inverse_one, gain_one, normed_one_grad
    )
    input_grad = middle_grad + input_part

    def by_place(v):
        return v.reshape((NZ, ny, nx, NC, v.shape[0] // (wide * ep)) + v.shape[1:])

    def reduce_all(v, order):
        return reduce_dense(grid, by_place(v.astype(bf16)), order).astype(f32)

    output_weight_sum = reduce_all(output_weight_grad, "cxyz")
    shared_gate_sum = reduce_all(shared_gate_grad, "cyxz")
    shared_up_sum = reduce_all(shared_up_grad, "cxyz")
    shared_down_sum = reduce_all(shared_down_grad, "cyxz")
    query_sum = reduce_all(query_w_grad, "cxyz")
    key_sum = reduce_all(key_w_grad, "cyxz")
    value_sum = reduce_all(value_w_grad, "cxyz")
    counts = jnp.sum(
        (routes[:, :, None] == jnp.arange(experts, dtype=jnp.int32)).astype(f32),
        axis=(0, 1),
    )
    share = gain_attention.shape[0]
    count_block = jnp.pad(
        jnp.tile(counts.reshape(1, ep, 1, local_experts), (wide, 1, 1, 1)),
        ((0, 0), (0, 0), (0, 0), (0, 128 - local_experts)),
    )
    extras = jnp.concatenate(
        [
            router_grad,
            gain_one_grad[:, None],
            gain_two_grad[:, None],
            jnp.zeros((width, 128 - experts - 2), f32),
        ],
        axis=1,
    ).reshape(wide, ep, share, 128)
    extras = jnp.concatenate(
        [extras, count_block, jnp.zeros((wide, ep, 7, 128), f32)], axis=2
    )
    extra_sum = lax.psum_scatter(
        extras.reshape(wide * ep, share + 8, 128),
        BOTH,
        scatter_dimension=0,
        tiled=True,
    )[0]
    return (
        block_out,
        input_grad,
        extra_sum[:share, experts],
        query_sum,
        key_sum,
        value_sum,
        output_weight_sum,
        extra_sum[:share, experts + 1],
        extra_sum[:share, :experts],
        shared_gate_sum,
        shared_up_sum,
        shared_down_sum,
        expert_gate_grad,
        expert_up_grad,
        expert_down_grad,
        extra_sum[share, :local_experts].astype(jnp.int32),
    )


def solution(mesh):
    split = P(BOTH, None)
    line = P(BOTH)
    held = P("ep", None, None)
    out_held = P("ep", "wide", None)
    in_specs = (
        (split, line, split, line)
        + (split,) * 4
        + (line,)
        + (split,) * 4
        + (held,) * 3
        + (split,)
    )
    out_specs = (
        (split, split, line)
        + (split,) * 4
        + (line,)
        + (split,) * 4
        + (out_held,) * 3
        + (P("ep"),)
    )
    return jax.shard_map(
        functools.partial(body, mesh.shape["wide"], mesh.shape["ep"]),
        mesh=mesh,
        in_specs=in_specs,
        out_specs=out_specs,
        check_vma=False,
    )
```

time: 2510 us -> 1340 us (0.53)
  waiting for transfers between devices: 1640 us -> 746 us
  blocking collectives: 362 us -> 44.3 us
  local copies, waits for them, and re-layouts: 179 us -> 119 us
  starting transfers between devices: 23.2 us -> 82.6 us
    reduce_scatter x9 -> x1, waiting for transfers between devices: 996 us -> 87 us  [body(): lax.psum_scatter(extras.reshape(wide * ep, share + 8, 128), BOTH, scatter...]
    ppermute x0 -> x78, waiting for transfers between devices: none -> 448 us  [send(): return lax.ppermute(value, BOTH, self.pairs(moves[axis]))]
    unnamed x28 -> x8, waiting for transfers between devices: 289 us -> 3.67 us
    unnamed x3 -> x0, blocking collectives: 166 us -> none
    all_to_all x3 -> x0, waiting for transfers between devices: 139 us -> none  [the longest x1 79.1 us: body(): lax.all_to_all(grad_send, 'ep', split_axis=0, concat_axis=1, tiled=True)]
    ppermute x0 -> x78, starting transfers between devices: none -> 82.3 us  [send(): return lax.ppermute(value, BOTH, self.pairs(moves[axis]))]
    all_to_all x1 -> x0, blocking collectives: 78 us -> none  [body(): lax.all_to_all(send_rows, 'ep', split_axis=0, concat_axis=1, tiled=True)]
    all_gather x2 -> x1, blocking collectives: 117 us -> 44.3 us  [body(): gather_all = lambda v: lax.all_gather(v, BOTH, axis=0, tiled=True)]
  transfers between devices with their start and end apart: 28 -> 86, of which waited for: 18 -> 43; matrix products, arithmetic and copies ran while one was open for 16% -> 23% of each run, Pallas kernels for 0% -> 0%
where the time goes in v1:
time: 1340 us; the launch traced here: 1330 us
  waiting for transfers between devices  746 us (56%)
  matrix products  226 us (17%)
  local copies, waits for them, and re-layouts  119 us (9%)
  other arithmetic  91.2 us (7%)
  starting transfers between devices  82.6 us (6%)
  blocking collectives  44.3 us (3%)
  between operations  16.5 us (1%)
    ppermute x78, waiting for transfers between devices, send(): return lax.ppermute(value, BOTH, self.pairs(moves[axis]))  448 us
    all_gather x7, waiting for transfers between devices, body(): gather_all = lambda v: lax.all_gather(v, BOTH, axis=0, tiled=True)  208 us
    reduce_scatter x1, waiting for transfers between devices, body(): lax.psum_scatter(extras.reshape(wide * ep, share + 8, 128), BOTH, scatter...  87 us
    ppermute x78, starting transfers between devices, send(): return lax.ppermute(value, BOTH, self.pairs(moves[axis]))  82.3 us
    dot_general x13, matrix products, times(): return jnp.dot(left, right, preferred_element_type=f32)  70.7 us
    dot_general x13, matrix products, times_transposed(): lax.dot_general(left, right, (((1,), (1,)), ((), ())), preferred_element_...  55.5 us
    unnamed x220, local copies, waits for them, and re-layouts  51.9 us
    all_gather x1, blocking collectives, body(): gather_all = lambda v: lax.all_gather(v, BOTH, axis=0, tiled=True)  44.3 us
  transfers between devices with their start and end apart: 86, of which 43 were waited for; matrix products, arithmetic and copies ran while one was open for 23% of the time, Pallas kernels for 0%

profile of v1, /device:TPU:0, one launch (start us, length us, event | category | flops | bytes accessed | tf_op | source)
XLA Modules:
  0.0 1325.6 jit_solution(17218323047036749350)
XLA Ops:
  18.0 44.3 %all_gather.24 = bf16[1280,128]{1,0:T(8,128)(2,1)S(1)} all-gather(bf16[40,128]{1,0:T(8,128)(2,1)S(1)} %maximum_maximum_fusion), channel_id=1, replica_groups=mesh['wide'=8,'ep'=4] {'wide','ep'}, dimensions={0}, use_global_device_ids=true | all-gather | bytes 337920 | tf_op jit(solution)/shard_map/all_gather | solution.py:196
  67.9 29.0 %collective-permute-done.3 = s32[2,8,256]{2,1,0:T(8,128)S(1)} collective-permute-done((s32[2,8,256]{2,1,0:T(8,128)S(1)}, s32[2,8,256]{2,1,0:T(8,128)S(1)}, u32[]{:S(2)}, u32[]{:S(2)}) %collective-permute-start.3) | collective-permute-done | bytes 16416 | tf_op jit(solution)/shard_map/ppermute | solution.py:84
  110.8 28.7 %collective-permute-done.1 = bf16[2,256,1280]{2,1,0:T(8,128)(2,1)} collective-permute-done((bf16[2,256,1280]{2,1,0:T(8,128)(2,1)}, bf16[2,256,1280]{2,1,0:T(8,128)(2,1)}, u32[]{:S(2)}, u32[]{:S(2)}) %collective-permute-start.1) | collective-permute-done | bytes 1310752 | tf_op jit(solution)/shard_map/ppermute | solution.py:84
  149.1 30.0 %collective-permute-done.13 = bf16[2,2,256,1280]{3,2,1,0:T(8,128)(2,1)} collective-permute-done((bf16[2,2,256,1280]{3,2,1,0:T(8,128)(2,1)}, bf16[2,2,256,1280]{3,2,1,0:T(8,128)(2,1)}, u32[]{:S(2)}, u32[]{:S(2)}) %collective-permute-start.13) | collective-permute-done | bytes 2621472 | tf_op jit(solution)/shard_map/ppermute | solution.py:84
  192.3 14.6 %all-gather.11.cloned.1.call-done = bf16[1280,1280]{1,0:T(8,128)(2,1)} async-done(((bf16[40,1280]{1,0:T(8,128)(2,1)}), bf16[1280,1280]{1,0:T(8,128)(2,1)}) %all-gather.11.cloned.1.call-update) | async-done | bytes 3276816 | tf_op jit(solution)/shard_map/all_gather | solution.py:196
  214.8 52.9 %all-gather.9.cloned.1.call-done = bf16[1280,1280]{1,0:T(8,128)(2,1)} async-done(((bf16[40,1280]{1,0:T(8,128)(2,1)}), bf16[1280,1280]{1,0:T(8,128)(2,1)}) %all-gather.9.cloned.1.call-update) | async-done | bytes 3276816 | tf_op jit(solution)/shard_map/all_gather | solution.py:196
  280.2 9.6 fusion.182
  297.4 31.2 %all-gather.15.cloned.1.call-done = bf16[1280,1280]{1,0:T(8,128)(2,1)} async-done(((bf16[40,1280]{1,0:T(8,128)(2,1)}), bf16[1280,1280]{1,0:T(8,128)(2,1)}) %all-gather.15.cloned.1.call-update) | async-done | bytes 3276816 | tf_op jit(solution)/shard_map/all_gather | solution.py:196
  333.1 54.3 %all-gather.17.cloned.1.call-done = bf16[1280,896]{1,0:T(8,128)(2,1)} async-done(((bf16[40,896]{1,0:T(8,128)(2,1)}), bf16[1280,896]{1,0:T(8,128)(2,1)}) %all-gather.17.cloned.1.call-update) | async-done | bytes 2293776 | tf_op jit(solution)/shard_map/all_gather | solution.py:196
  391.8 54.5 %all-gather.19.cloned.1.call-done = bf16[1280,896]{1,0:T(8,128)(2,1)} async-done(((bf16[40,896]{1,0:T(8,128)(2,1)}), bf16[1280,896]{1,0:T(8,128)(2,1)}) %all-gather.19.cloned.1.call-update) | async-done | bytes 2293776 | tf_op jit(solution)/shard_map/all_gather | solution.py:196
  479.4 12.3 collective-permute-done.61
  492.5 24.9 %collective-permute-done.55 = bf16[4,2,40,896]{3,2,0,1:T(8,128)(2,1)S(1)} collective-permute-done((bf16[4,2,40,896]{3,2,0,1:T(8,128)(2,1)S(1)}, bf16[4,2,40,896]{3,2,0,1:T(8,128)(2,1)S(1)}, u32[]{:S(2)}, u32[]{:S(2)}) %collective-permute-start.55) | collective-permute-done | bytes 573472 | tf_op jit(solution)/shard_map/ppermute | solution.py:84
  532.2 50.0 %collective-permute-done.57 = bf16[40,896]{1,0:T(8,128)(2,1)S(1)} collective-permute-done((bf16[40,896]{1,0:T(8,128)(2,1)S(1)}, bf16[40,896]{1,0:T(8,128)(2,1)S(1)}, u32[]{:S(2)}, u32[]{:S(2)}) %collective-permute-start.57) | collective-permute-done | bytes 71712 | tf_op jit(solution)/shard_map/ppermute | solution.py:84
  637.9 9.6 multiply_convert_fusion.3
  683.8 9.2 fusion.10
  772.6 43.5 %collective-permute-done.70 = bf16[2,4,160,896]{3,2,0,1:T(8,128)(2,1)} collective-permute-done((bf16[2,4,160,896]{3,2,0,1:T(8,128)(2,1)}, bf16[2,4,160,896]{3,2,0,1:T(8,128)(2,1)}, u32[]{:S(2)}, u32[]{:S(2)}) %collective-permute-start.70) | collective-permute-done | bytes 2293792 | tf_op jit(solution)/shard_map/ppermute | solution.py:84
  818.7 41.7 %collective-permute-done.66 = bf16[2,4,160,896]{3,2,0,1:T(8,128)(2,1)} collective-permute-done((bf16[2,4,160,896]{3,2,0,1:T(8,128)(2,1)}, bf16[2,4,160,896]{3,2,0,1:T(8,128)(2,1)}, u32[]{:S(2)}, u32[]{:S(2)}) %collective-permute-start.66) | collective-permute-done | bytes 2293792 | tf_op jit(solution)/shard_map/ppermute | solution.py:84
  879.2 54.5 %collective-permute-done.71 = bf16[2,160,896]{2,1,0:T(8,128)(2,1)S(1)} collective-permute-done((bf16[2,160,896]{2,1,0:T(8,128)(2,1)S(1)}, bf16[2,160,896]{2,1,0:T(8,128)(2,1)S(1)}, u32[]{:S(2)}, u32[]{:S(2)}) %collective-permute-start.71) | collective-permute-done | bytes 573472 | tf_op jit(solution)/shard_map/ppermute | solution.py:84
  940.0 24.4 %collective-permute-done.67 = bf16[2,160,896]{2,1,0:T(8,128)(2,1)S(1)} collective-permute-done((bf16[2,160,896]{2,1,0:T(8,128)(2,1)S(1)}, bf16[2,160,896]{2,1,0:T(8,128)(2,1)S(1)}, u32[]{:S(2)}, u32[]{:S(2)}) %collective-permute-start.67) | collective-permute-done | bytes 573472 | tf_op jit(solution)/shard_map/ppermute | solution.py:84
  979.0 14.0 %collective-permute-done.16 = bf16[256,1280]{1,0:T(8,128)(2,1)S(1)} collective-permute-done((bf16[256,1280]{1,0:T(8,128)(2,1)S(1)}, bf16[256,1280]{1,0:T(8,128)(2,1)S(1)}, u32[]{:S(2)}, u32[]{:S(2)}) %collective-permute-start.16) | collective-permute-done | bytes 655392 | tf_op jit(solution)/shard_map/ppermute | solution.py:84
  1101.4 11.4 collective-permute-done.21
  1133.9 16.8 %collective-permute-done.25 = bf16[4,2,40,1280]{3,2,0,1:T(8,128)(2,1)} collective-permute-done((bf16[4,2,40,1280]{3,2,0,1:T(8,128)(2,1)}, bf16[4,2,40,1280]{3,2,0,1:T(8,128)(2,1)}, u32[]{:S(2)}, u32[]{:S(2)}) %collective-permute-start.25) | collective-permute-done | bytes 819232 | tf_op jit(solution)/shard_map/ppermute | solution.py:84
  1178.6 87.0 %reduce-scatter.2.cloned.1.call-done = f32[1,48,128]{1,2,0:T(8,128)} async-done(((f32[32,48,128]{1,2,0:T(8,128)}), f32[1,48,128]{1,2,0:T(8,128)}) %reduce-scatter.2.cloned.1.call-update) | async-done | bytes 24592 | tf_op jit(solution)/shard_map/reduce_scatter | solution.py:464
  1273.7 12.7 collective-permute-done.37
  (626 shorter events, 547.9 us)
Async XLA Ops:
  7.2 137.9 %all-gather.21.cloned.1.call-start = ((), (), s32[]{:S(2)}) async-start(), calls=%async_computation.8 | async-start | bytes 2703360 | tf_op jit(solution)/shard_map/all_gather | solution.py:196
  7.9 176.6 %all-gather.13.cloned.1.call-start = ((), (), s32[]{:S(2)}) async-start(), calls=%async_computation.3 | async-start | bytes 3379200 | tf_op jit(solution)/shard_map/all_gather | solution.py:196
  8.7 198.2 %all-gather.11.cloned.1.call-start = ((), (), s32[]{:S(2)}) async-start(), calls=%async_computation.2 | async-start | bytes 3379200 | tf_op jit(solution)/shard_map/all_gather | solution.py:196
  9.4 258.3 %all-gather.9.cloned.1.call-start = ((), (), s32[]{:S(2)}) async-start(), calls=%async_computation.1 | async-start | bytes 3379200 | tf_op jit(solution)/shard_map/all_gather | solution.py:196
  10.0 318.6 %all-gather.15.cloned.1.call-start = ((), (), s32[]{:S(2)}) async-start(), calls=%async_computation.4 | async-start | bytes 3379200 | tf_op jit(solution)/shard_map/all_gather | solution.py:196
  10.6 376.8 %all-gather.17.cloned.1.call-start = ((), (), s32[]{:S(2)}) async-start(), calls=%async_computation.5 | async-start | bytes 2365440 | tf_op jit(solution)/shard_map/all_gather | solution.py:196
  11.1 435.2 %all-gather.19.cloned.1.call-start = ((), (), s32[]{:S(2)}) async-start(), calls=%async_computation.6 | async-start | bytes 2365440 | tf_op jit(solution)/shard_map/all_gather | solution.py:196
  12.4 84.6 %collective-permute-start = (bf16[256,1280]{1,0:T(8,128)(2,1)}, bf16[256,1280]{1,0:T(8,128)(2,1)S(1)}, u32[]{:S(2)}, u32[]{:S(2)}) collective-permute-start(bf16[256,1280]{1,0:T(8,128)(2,1)} %param.17), channel_id=1, source_target_pairs={{0,1},{1,0},{2,3},{3,2},{4,5},{5,4},{6,7},{7,6},{8,9},{9,8},{10,11... | collective-permute-start | bytes 1966088 | tf_op jit(solution)/shard_map/ppermute | solution.py:84
  12.9 1252.7 %reduce-scatter.2.cloned.1.call-start = ((), (), s32[]{:S(2)}) async-start(), calls=%async_computation.7 | async-start | bytes 2162688 | tf_op jit(solution)/shard_map/reduce_scatter | solution.py:464
  105.0 74.2 %collective-permute-start.13 = (bf16[2,2,256,1280]{3,2,1,0:T(8,128)(2,1)}, bf16[2,2,256,1280]{3,2,1,0:T(8,128)(2,1)}, u32[]{:S(2)}, u32[]{:S(2)}) collective-permute-start(bf16[2,2,256,1280]{3,2,1,0:T(8,128)(2,1)} %get-tuple-element.65), channel_id=1, source_target_pairs={{0,8},{1,9},{2,10},{3,11},{4,12},{5,13},{6,14},{7,15},{8,0},{9,1},... | collective-permute-start | bytes 7864328 | tf_op jit(solution)/shard_map/ppermute | solution.py:84
  332.7 139.3 %collective-permute-start.5 = (bf16[256,1280]{1,0:T(8,128)(2,1)S(1)}, bf16[256,1280]{1,0:T(8,128)(2,1)}, u32[]{:S(2)}, u32[]{:S(2)}) collective-permute-start(bf16[256,1280]{1,0:T(8,128)(2,1)S(1)} %multiply_convert_fusion.13), channel_id=1, source_target_pairs={{0,1},{1,0},{2,3},{3,2},{4,5},{5,4},{6,7},{7,6},{8,9},{9,8},{10,11... | collective-permute-start | bytes 1966088 | tf_op jit(solution)/shard_map/ppermute | solution.py:84
  519.5 76.6 %collective-permute-start.7 = (bf16[2,2,256,1280]{3,2,1,0:T(8,128)(2,1)S(1)}, bf16[2,2,256,1280]{3,2,1,0:T(8,128)(2,1)S(1)}, u32[]{:S(2)}, u32[]{:S(2)}) collective-permute-start(bf16[2,2,256,1280]{3,2,1,0:T(8,128)(2,1)S(1)} %get-tuple-element.67), channel_id=1, source_target_pairs={{0,8},{1,9},{2,10},{3,11},{4,12},{5,13},{6,14},{7,15},{8,0},{9,1},... | collective-permute-start | bytes 7864328 | tf_op jit(solution)/shard_map/ppermute | solution.py:84
  524.6 69.5 %collective-permute-start.63 = (bf16[28,1280]{1,0:T(8,128)(2,1)S(1)}, bf16[28,1280]{1,0:T(8,128)(2,1)S(1)}, u32[]{:S(2)}, u32[]{:S(2)}) collective-permute-start(bf16[28,1280]{1,0:T(8,128)(2,1)S(1)} %get-tuple-element.102), channel_id=1, source_target_pairs={{0,8},{1,9},{2,10},{3,11},{4,12},{5,13},{6,14},{7,15},{8,16},{9,17... | collective-permute-start | bytes 215048 | tf_op jit(solution)/shard_map/ppermute | solution.py:84
  726.4 89.7 %collective-permute-start.70 = (bf16[2,4,160,896]{3,2,0,1:T(8,128)(2,1)}, bf16[2,4,160,896]{3,2,0,1:T(8,128)(2,1)}, u32[]{:S(2)}, u32[]{:S(2)}) collective-permute-start(bf16[2,4,160,896]{3,2,0,1:T(8,128)(2,1)} %bitcast.593), channel_id=1, source_target_pairs={{0,4},{1,5},{2,6},{3,7},{4,0},{5,1},{6,2},{7,3},{8,12},{9,13},{10,... | collective-permute-start | bytes 6881288 | tf_op jit(solution)/shard_map/ppermute | solution.py:84
  731.5 128.8 %collective-permute-start.66 = (bf16[2,4,160,896]{3,2,0,1:T(8,128)(2,1)}, bf16[2,4,160,896]{3,2,0,1:T(8,128)(2,1)}, u32[]{:S(2)}, u32[]{:S(2)}) collective-permute-start(bf16[2,4,160,896]{3,2,0,1:T(8,128)(2,1)} %bitcast.594), channel_id=1, source_target_pairs={{0,4},{1,5},{2,6},{3,7},{4,0},{5,1},{6,2},{7,3},{8,12},{9,13},{10,... | collective-permute-start | bytes 6881288 | tf_op jit(solution)/shard_map/ppermute | solution.py:84
  750.3 116.8 %collective-permute-start.14 = (bf16[2,2,256,1280]{3,2,0,1:T(8,128)(2,1)}, bf16[2,2,256,1280]{3,2,0,1:T(8,128)(2,1)}, u32[]{:S(2)}, u32[]{:S(2)}) collective-permute-start(bf16[2,2,256,1280]{3,2,0,1:T(8,128)(2,1)} %bitcast.590), channel_id=1, source_target_pairs={{0,1},{1,0},{2,3},{3,2},{4,5},{5,4},{6,7},{7,6},{8,9},{9,8},{10,11... | collective-permute-start | bytes 7864328 | tf_op jit(solution)/shard_map/ppermute | solution.py:84
  762.9 108.2 %collective-permute-start.8 = (bf16[2,2,256,1280]{3,2,0,1:T(8,128)(2,1)}, bf16[2,2,256,1280]{3,2,0,1:T(8,128)(2,1)}, u32[]{:S(2)}, u32[]{:S(2)}) collective-permute-start(bf16[2,2,256,1280]{3,2,0,1:T(8,128)(2,1)} %bitcast.591), channel_id=1, source_target_pairs={{0,1},{1,0},{2,3},{3,2},{4,5},{5,4},{6,7},{7,6},{8,9},{9,8},{10,11... | collective-permute-start | bytes 7864328 | tf_op jit(solution)/shard_map/ppermute | solution.py:84
  769.9 103.8 %collective-permute-start.75 = (bf16[2,112,1280]{2,1,0:T(8,128)(2,1)S(1)}, bf16[2,112,1280]{2,1,0:T(8,128)(2,1)S(1)}, u32[]{:S(2)}, u32[]{:S(2)}) collective-permute-start(bf16[2,112,1280]{2,1,0:T(8,128)(2,1)S(1)} %get-tuple-element.68), channel_id=1, source_target_pairs={{0,16},{1,17},{2,18},{3,19},{4,20},{5,21},{6,22},{7,23},{8,24},{9,... | collective-permute-start | bytes 1720328 | tf_op jit(solution)/shard_map/ppermute | solution.py:84
  867.1 66.6 %collective-permute-start.71 = (bf16[2,160,896]{2,1,0:T(8,128)(2,1)S(1)}, bf16[2,160,896]{2,1,0:T(8,128)(2,1)S(1)}, u32[]{:S(2)}, u32[]{:S(2)}) collective-permute-start(bf16[2,160,896]{2,1,0:T(8,128)(2,1)S(1)} %get-tuple-element.71), channel_id=1, source_target_pairs={{0,16},{1,17},{2,18},{3,19},{4,20},{5,21},{6,22},{7,23},{8,24},{9,... | collective-permute-start | bytes 1720328 | tf_op jit(solution)/shard_map/ppermute | solution.py:84
  877.6 86.8 %collective-permute-start.67 = (bf16[2,160,896]{2,1,0:T(8,128)(2,1)S(1)}, bf16[2,160,896]{2,1,0:T(8,128)(2,1)S(1)}, u32[]{:S(2)}, u32[]{:S(2)}) collective-permute-start(bf16[2,160,896]{2,1,0:T(8,128)(2,1)S(1)} %get-tuple-element.74), channel_id=1, source_target_pairs={{0,16},{1,17},{2,18},{3,19},{4,20},{5,21},{6,22},{7,23},{8,24},{9,... | collective-permute-start | bytes 1720328 | tf_op jit(solution)/shard_map/ppermute | solution.py:84
  878.2 94.7 %collective-permute-start.15 = (bf16[2,256,1280]{2,1,0:T(8,128)(2,1)S(1)}, bf16[2,256,1280]{2,1,0:T(8,128)(2,1)S(1)}, u32[]{:S(2)}, u32[]{:S(2)}) collective-permute-start(bf16[2,256,1280]{2,1,0:T(8,128)(2,1)S(1)} %slice_bitcast_fusion), channel_id=1, source_target_pairs={{0,2},{1,3},{2,0},{3,1},{4,6},{5,7},{6,4},{7,5},{8,10},{9,11},{10,... | collective-permute-start | bytes 3932168 | tf_op jit(solution)/shard_map/ppermute | solution.py:84
  978.7 97.0 %collective-permute-start.10 = (bf16[256,1280]{1,0:T(8,128)(2,1)}, bf16[256,1280]{1,0:T(8,128)(2,1)}, u32[]{:S(2)}, u32[]{:S(2)}) collective-permute-start(bf16[256,1280]{1,0:T(8,128)(2,1)} %slice_bitcast_fusion.12), channel_id=1, source_target_pairs={{0,8},{1,9},{2,10},{3,11},{4,12},{5,13},{6,14},{7,15},{8,0},{9,1},... | collective-permute-start | bytes 1966088 | tf_op jit(solution)/shard_map/ppermute | solution.py:84
  1101.4 166.8 %collective-permute-start.36 = (bf16[4,2,2,40,1280]{4,3,0,1,2:T(8,128)(2,1)}, bf16[4,2,2,40,1280]{4,3,0,1,2:T(8,128)(2,1)}, u32[]{:S(2)}, u32[]{:S(2)}) collective-permute-start(bf16[4,2,2,40,1280]{4,3,0,1,2:T(8,128)(2,1)} %bitcast.596), channel_id=1, source_target_pairs={{0,1},{1,0},{2,3},{3,2},{4,5},{5,4},{6,7},{7,6},{8,9},{9,8},{10,11... | collective-permute-start | bytes 4915208 | tf_op jit(solution)/shard_map/ppermute | solution.py:84
  1116.7 153.6 %collective-permute-start.30 = (bf16[4,2,2,40,1280]{4,3,0,2,1:T(8,128)(2,1)}, bf16[4,2,2,40,1280]{4,3,0,2,1:T(8,128)(2,1)}, u32[]{:S(2)}, u32[]{:S(2)}) collective-permute-start(bf16[4,2,2,40,1280]{4,3,0,2,1:T(8,128)(2,1)} %bitcast.597), channel_id=1, source_target_pairs={{0,1},{1,0},{2,3},{3,2},{4,5},{5,4},{6,7},{7,6},{8,9},{9,8},{10,11... | collective-permute-start | bytes 4915208 | tf_op jit(solution)/shard_map/ppermute | solution.py:84
  (162 other events, 3646.1 us)
Sparse Core Ops, SparseCore 0:
  10.9 63.3 all-gather.20
  77.1 66.8 all-gather.12
  146.9 59.9 all-gather.10
  209.6 58.1 all-gather.8
  270.4 58.1 all-gather.14
  331.4 55.9 all-gather.16
  390.3 55.9 all-gather.18
  1128.7 136.8 reduce-scatter.1

commit v2 on v1

--- a/solution.py
+++ b/solution.py
@@ -3,6 +3,8 @@
 import jax
 import jax.numpy as jnp
 from jax import lax
+from jax.experimental import pallas as pl
+from jax.experimental.pallas import tpu as pltpu
 from jax.sharding import PartitionSpec as P
 
 HD = 128
@@ -109,6 +111,450 @@
         for d in range(1, n):
             total = total + self.send(take((me + d) % n), axis, d).astype(f32)
         return total.astype(value.dtype)
+
+
+def gather_kernel(
+    grid_of,
+    cut,
+    w_ref,
+    rows_ref,
+    ints_ref,
+    w_all,
+    rows_all,
+    ints_all,
+    plane_sem,
+    core_sem,
+    rows_sem,
+    ints_sem,
+    send_sem,
+    local_sem,
+):
+    grid = grid_of()
+    z, y, x, c, nx, ny = grid.z, grid.y, grid.x, grid.c, grid.nx, grid.ny
+    width = w_ref.shape[1]
+
+    def device(tz, ty, tx, tc):
+        return (tz * ny + ty, tx * NC + tc)
+
+    def slot(tz, ty, tx, tc):
+        return (tz * ny + ty) * (nx * NC) + tx * NC + tc
+
+    shift_z = lambda d: (z + d) % NZ
+    shift_p = lambda d: z // ZP * ZP + (z % ZP + d) % ZP
+    shift_y = lambda d: (y + d) % ny
+    shift_x = lambda d: (x + d) % nx
+    other = (c + 1) % NC
+    octet = [
+        (dz, dx, dc)
+        for dz in range(ZP)
+        for dx in range(nx)
+        for dc in range(NC)
+        if (dz, dx, dc) != (0, 0, 0)
+    ]
+
+    barrier = pltpu.get_barrier_semaphore()
+    greeted = (
+        [device(shift_z(d), y, x, c) for d in range(1, NZ)]
+        + [device(z, shift_y(d), x, c) for d in range(1, ny)]
+        + [device(shift_p(a), y, shift_x(b), (c + e) % NC) for a, b, e in octet]
+    )
+    for target in greeted:
+        pl.semaphore_signal(
+            barrier, inc=1, device_id=target, device_id_type=pl.DeviceIdType.MESH
+        )
+    pl.semaphore_wait(barrier, len(greeted))
+
+    started = []
+
+    def send(src, dst, sem, target):
+        copy = pltpu.make_async_remote_copy(
+            src_ref=src,
+            dst_ref=dst,
+            send_sem=send_sem.at[len(started)],
+            recv_sem=sem,
+            device_id=target,
+            device_id_type=pl.DeviceIdType.MESH,
+        )
+        copy.start()
+        started.append(copy)
+
+    def arrived(dst, sem):
+        pltpu.make_async_copy(dst, dst, sem).wait()
+
+    half = (pl.ds(0, cut), pl.ds(cut, width - cut))
+    block = lambda dz, dy, dx, tc: w_all.at[
+        slot(shift_z(-dz), shift_y(-dy), shift_x(-dx), tc)
+    ]
+
+    own = pltpu.make_async_copy(w_ref, block(0, 0, 0, c), local_sem)
+    own.start()
+    my_slot = w_all.at[slot(z, y, x, c)]
+    for d in range(1, nx):
+        send(rows_ref, rows_all.at[nx - d, 0], rows_sem.at[nx - d, 0], device(z, y, shift_x(d), c))
+    for d in range(1, NZ):
+        send(w_ref, my_slot, plane_sem.at[d, 0, 0, 0], device(shift_z(d), y, x, c))
+    send(rows_ref, rows_all.at[0, 1], rows_sem.at[0, 1], device(z, y, x, other))
+    for a, b, e in octet:
+        send(
+            ints_ref,
+            ints_all.at[(ZP - a) % ZP, (nx - b) % nx, e],
+            ints_sem.at[(ZP - a) % ZP, (nx - b) % nx, e],
+            device(shift_p(a), y, shift_x(b), (c + e) % NC),
+        )
+
+    def spread(src, dst, dz):
+        for d in range(1, ny):
+            send(src, dst, plane_sem.at[dz, d, 0, 0], device(z, shift_y(d), x, c))
+        for d in range(1, nx):
+            send(src, dst, plane_sem.at[dz, 0, d, 0], device(z, y, shift_x(d), c))
+        send(src, dst, core_sem.at[dz, 0, 0], device(z, y, x, other))
+
+    spread(w_ref, my_slot, 0)
+    for d in range(1, NZ):
+        here = block(d, 0, 0, c)
+        arrived(here, plane_sem.at[d, 0, 0, 0])
+        spread(here, here, d)
+    for d in range(1, nx):
+        arrived(rows_all.at[nx - d, 0], rows_sem.at[nx - d, 0])
+        send(rows_all.at[nx - d, 0], rows_all.at[nx - d, 1], rows_sem.at[nx - d, 1], device(z, y, x, other))
+    for dz in range(NZ):
+        for dy in range(1, ny):
+            here = block(dz, dy, 0, c)
+            arrived(here, plane_sem.at[dz, dy, 0, 0])
+            for d in range(1, nx):
+                send(
+                    here.at[:, half[0]],
+                    here.at[:, half[0]],
+                    plane_sem.at[dz, dy, d, 0],
+                    device(z, y, shift_x(d), c),
+                )
+            send(here, here, core_sem.at[dz, dy, 0], device(z, y, x, other))
+        for dx in range(1, nx):
+            here = block(dz, 0, dx, c)
+            arrived(here, plane_sem.at[dz, 0, dx, 0])
+            for d in range(1, ny):
+                send(
+                    here.at[:, half[1]],
+                    here.at[:, half[1]],
+                    plane_sem.at[dz, d, dx, 1],
+                    device(z, shift_y(d), x, c),
+                )
+            send(here, here, core_sem.at[dz, 0, dx], device(z, y, x, other))
+    for dz in range(NZ):
+        for dy in range(1, ny):
+            for dx in range(1, nx):
+                here = block(dz, dy, dx, c)
+                for part in range(2):
+                    arrived(here.at[:, half[part]], plane_sem.at[dz, dy, dx, part])
+                send(here, here, core_sem.at[dz, dy, dx], device(z, y, x, other))
+    for dx in range(nx):
+        arrived(rows_all.at[dx, 1], rows_sem.at[dx, 1])
+    for a, b, e in octet:
+        arrived(ints_all.at[a, b, e], ints_sem.at[a, b, e])
+    for dz in range(NZ):
+        for dy in range(ny):
+            for dx in range(nx):
+                arrived(block(dz, dy, dx, other), core_sem.at[dz, dy, dx])
+    own.wait()
+    for copy in started:
+        copy.wait_send()
+
+
+def gather_first(grid_of, w, rows, ints):
+    grid = grid_of()
+    nx, ny = grid.nx, grid.ny
+    places = NZ * ny * nx * NC
+    cut = w.shape[1] // 2 // 128 * 128
+    sends = (
+        (nx - 1) * 2 + 1 + (NZ - 1) + (ZP * nx * NC - 1)
+        + NZ * (ny + nx - 1)
+        + NZ * ((ny - 1) * nx + (nx - 1) * ny + (ny - 1) * (nx - 1))
+    )
+    anywhere = pl.BlockSpec(memory_space=pl.ANY)
+    dma = pltpu.SemaphoreType.DMA
+    return pl.pallas_call(
+        functools.partial(gather_kernel, grid_of, cut),
+        out_shape=(
+            jax.ShapeDtypeStruct((places,) + w.shape, w.dtype),
+            jax.ShapeDtypeStruct((nx, NC) + rows.shape, rows.dtype),
+            jax.ShapeDtypeStruct((ZP, nx, NC) + ints.shape, ints.dtype),
+        ),
+        in_specs=[anywhere] * 3,
+        out_specs=(anywhere,) * 3,
+        scratch_shapes=[
+            dma((NZ, ny, nx, 2)),
+            dma((NZ, ny, nx)),
+            dma((nx, NC)),
+            dma((ZP, nx, NC)),
+            dma((sends,)),
+            dma,
+        ],
+        compiler_params=pltpu.CompilerParams(collective_id=0, has_side_effects=True),
+    )(w, rows, ints)
+
+
+class Sender:
+    def __init__(self, sems):
+        self.sems, self.started = sems, []
+
+    def __call__(self, src, dst, sem, target):
+        copy = pltpu.make_async_remote_copy(
+            src_ref=src,
+            dst_ref=dst,
+            send_sem=self.sems.at[len(self.started)],
+            recv_sem=sem,
+            device_id=target,
+            device_id_type=pl.DeviceIdType.MESH,
+        )
+        copy.start()
+        self.started.append(copy)
+
+    def finish(self):
+        for copy in self.started:
+            copy.wait_send()
+
+
+def arrived(dst, sem):
+    pltpu.make_async_copy(dst, dst, sem).wait()
+
+
+def greet(targets):
+    barrier = pltpu.get_barrier_semaphore()
+    for target in targets:
+        pl.semaphore_signal(
+            barrier, inc=1, device_id=target, device_id_type=pl.DeviceIdType.MESH
+        )
+    pl.semaphore_wait(barrier, len(targets))
+
+
+def around(grid, zp):
+    steps = [(a, b, e) for a in range(zp) for b in range(grid.nx) for e in range(NC)]
+    return steps[1:]
+
+
+def stepped(grid, zp, a, b, e):
+    z = grid.z // zp * zp + (grid.z % zp + a) % zp
+    return (
+        z * grid.ny + grid.y,
+        (grid.x + b) % grid.nx * NC + (grid.c + e) % NC,
+    )
+
+
+def exchange_kernel(grid_of, zp, cut, count, *refs):
+    grid = grid_of()
+    nx = grid.nx
+    ins, outs = refs[:count], refs[count : 2 * count]
+    plane_sem, core_sem, local_sem, send_sem = refs[2 * count :]
+    send = Sender(send_sem)
+    to = functools.partial(stepped, grid, zp)
+    greet([to(*s) for s in around(grid, zp)])
+    back = lambda d: (nx - d) % nx
+    for k in range(count):
+        src, out = ins[k], outs[k]
+        for a in range(1, zp):
+            send(src, out.at[zp - a, 0, 0], plane_sem.at[k, zp - a, 0, 0], to(a, 0, 0))
+        for b in range(1, nx):
+            send(src, out.at[0, back(b), 0], plane_sem.at[k, 0, back(b), 0], to(0, b, 0))
+        send(src, out.at[0, 0, 1], core_sem.at[k, 0, 0], to(0, 0, 1))
+        pltpu.make_async_copy(src, out.at[0, 0, 0], local_sem.at[k]).start()
+    for k in range(count):
+        out = outs[k]
+        h0 = (slice(None), pl.ds(0, cut))
+        h1 = (slice(None), pl.ds(cut, ins[k].shape[1] - cut))
+        for a in range(1, zp):
+            here = out.at[a, 0, 0]
+            arrived(here, plane_sem.at[k, a, 0, 0])
+            for b in range(1, nx):
+                send(here.at[h0], out.at[a, back(b), 0].at[h0], plane_sem.at[k, a, back(b), 0], to(0, b, 0))
+            send(here, out.at[a, 0, 1], core_sem.at[k, a, 0], to(0, 0, 1))
+        for b in range(1, nx):
+            here = out.at[0, b, 0]
+            arrived(here, plane_sem.at[k, 0, b, 0])
+            for a in range(1, zp):
+                send(here.at[h1], out.at[zp - a, b, 0].at[h1], plane_sem.at[k, zp - a, b, 1], to(a, 0, 0))
+            send(here, out.at[0, b, 1], core_sem.at[k, 0, b], to(0, 0, 1))
+    for k in range(count):
+        out = outs[k]
+        h0 = (slice(None), pl.ds(0, cut))
+        h1 = (slice(None), pl.ds(cut, ins[k].shape[1] - cut))
+        for a in range(1, zp):
+            for b in range(1, nx):
+                here = out.at[a, b, 0]
+                arrived(here.at[h0], plane_sem.at[k, a, b, 0])
+                arrived(here.at[h1], plane_sem.at[k, a, b, 1])
+                send(here, out.at[a, b, 1], core_sem.at[k, a, b], to(0, 0, 1))
+    for k in range(count):
+        for a in range(zp):
+            for b in range(nx):
+                arrived(outs[k].at[a, b, 1], core_sem.at[k, a, b])
+        pltpu.make_async_copy(ins[k], outs[k].at[0, 0, 0], local_sem.at[k]).wait()
+    send.finish()
+
+
+def exchange(grid_of, zp, number, *arrays):
+    grid = grid_of()
+    nx = grid.nx
+    count = len(arrays)
+    sends = count * (zp * nx * 2 + zp * nx * nx * 2)
+    anywhere = pl.BlockSpec(memory_space=pl.ANY)
+    dma = pltpu.SemaphoreType.DMA
+    return pl.pallas_call(
+        functools.partial(
+            exchange_kernel, grid_of, zp, arrays[0].shape[1] // 256 * 128, count
+        ),
+        out_shape=tuple(
+            jax.ShapeDtypeStruct((zp, nx, NC) + v.shape, v.dtype) for v in arrays
+        ),
+        in_specs=[anywhere] * count,
+        out_specs=(anywhere,) * count,
+        scratch_shapes=[
+            dma((count, zp, nx, 2)),
+            dma((count, zp, nx)),
+            dma((count,)),
+            dma((sends,)),
+        ],
+        compiler_params=pltpu.CompilerParams(
+            collective_id=number, has_side_effects=True
+        ),
+    )(*arrays)
+
+
+def add_into(dst, src, rows):
+    for k in range(dst.shape[0]):
+
+        @pl.loop(0, dst.shape[1], step=rows)
+        def _(i):
+            at = pl.ds(pl.multiple_of(i, rows), rows)
+            dst[k, at] = (dst[k, at].astype(f32) + src[k, at].astype(f32)).astype(
+                dst.dtype
+            )
+
+
+def sum_kernel(grid_of, zp, cut, small, parts, *refs):
+    grid = grid_of()
+    nx = grid.nx
+    if small:
+        pieces, out, pieces_out = refs[:3]
+        refs = refs[3:]
+    else:
+        out = refs[0]
+        refs = refs[1:]
+    own, got_c, turn_x, turn_p, got_p, got_x = refs[:6]
+    local_sem, c_sem, turn_sem, p_sem, x_sem, small_sem, send_sem = refs[6:]
+    send = Sender(send_sem)
+    to = functools.partial(stepped, grid, zp)
+    greet([to(*s) for s in around(grid, zp)])
+    width = parts.shape[-1]
+    h0, h1 = pl.ds(0, cut), pl.ds(cut, width - cut)
+    order = (
+        [(a, b) for a in range(1, zp) for b in range(1, nx)]
+        + [(a, 0) for a in range(1, zp)]
+        + [(0, b) for b in range(1, nx)]
+        + [(0, 0)]
+    )
+    for a, b in order:
+        send(parts.at[:, a, b, 1], got_c.at[:, a, b], c_sem.at[a, b], to(0, 0, 1))
+        pltpu.make_async_copy(
+            parts.at[:, a, b, 0], own.at[:, a, b], local_sem.at[a, b]
+        ).start()
+    if small:
+        for a, b, e in around(grid, zp):
+            mirror = ((zp - a) % zp, (nx - b) % nx, e)
+            send(
+                pieces.at[a, b, e],
+                pieces_out.at[mirror],
+                small_sem.at[mirror],
+                to(a, b, e),
+            )
+        pltpu.make_async_copy(
+            pieces.at[0, 0, 0], pieces_out.at[0, 0, 0], small_sem.at[0, 0, 0]
+        ).start()
+    rows = 32
+
+    def ready(a, b):
+        arrived(got_c.at[:, a, b], c_sem.at[a, b])
+        pltpu.make_async_copy(
+            parts.at[:, a, b, 0], own.at[:, a, b], local_sem.at[a, b]
+        ).wait()
+        add_into(own.at[:, a, b], got_c.at[:, a, b], rows)
+
+    for a in range(1, zp):
+        for b in range(1, nx):
+            ready(a, b)
+            send(own.at[:, a, b, :, h0], turn_x.at[:, a - 1, b - 1], turn_sem.at[a - 1, b - 1, 0], to(0, b, 0))
+            send(own.at[:, a, b, :, h1], turn_p.at[:, a - 1, b - 1], turn_sem.at[a - 1, b - 1, 1], to(a, 0, 0))
+    for a in range(1, zp):
+        ready(a, 0)
+    for b in range(1, nx):
+        ready(0, b)
+    for a in range(1, zp):
+        for b in range(1, nx):
+            arrived(turn_x.at[:, a - 1, b - 1], turn_sem.at[a - 1, b - 1, 0])
+            add_into(own.at[:, a, 0, :, h0], turn_x.at[:, a - 1, b - 1], rows)
+        send(own.at[:, a, 0], got_p.at[:, a - 1], p_sem.at[a - 1], to(a, 0, 0))
+    for b in range(1, nx):
+        for a in range(1, zp):
+            arrived(turn_p.at[:, a - 1, b - 1], turn_sem.at[a - 1, b - 1, 1])
+            add_into(own.at[:, 0, b, :, h1], turn_p.at[:, a - 1, b - 1], rows)
+        send(own.at[:, 0, b], got_x.at[:, b - 1], x_sem.at[b - 1], to(0, b, 0))
+    ready(0, 0)
+    for a in range(1, zp):
+        arrived(got_p.at[:, a - 1], p_sem.at[a - 1])
+        add_into(own.at[:, 0, 0], got_p.at[:, a - 1], rows)
+    for b in range(1, nx):
+        arrived(got_x.at[:, b - 1], x_sem.at[b - 1])
+        add_into(own.at[:, 0, 0], got_x.at[:, b - 1], rows)
+    result = pltpu.make_async_copy(own.at[:, 0, 0], out, local_sem.at[0, 0])
+    result.start()
+    if small:
+        for a, b, e in [(0, 0, 0)] + around(grid, zp):
+            arrived(pieces_out.at[a, b, e], small_sem.at[a, b, e])
+    result.wait()
+    send.finish()
+
+
+def sum_around(grid_of, zp, number, parts, pieces=None):
+    grid = grid_of()
+    nx = grid.nx
+    payloads, rows, width = parts.shape[0], parts.shape[-2], parts.shape[-1]
+    cut = width // 256 * 128
+    anywhere = pl.BlockSpec(memory_space=pl.ANY)
+    dma = pltpu.SemaphoreType.DMA
+    small = pieces is not None
+    out_shape = [jax.ShapeDtypeStruct((payloads, rows, width), parts.dtype)]
+    args = [parts]
+    if small:
+        out_shape.append(jax.ShapeDtypeStruct(pieces.shape, pieces.dtype))
+        args.append(pieces)
+    turns = (max(zp - 1, 1), max(nx - 1, 1))
+    vmem = lambda shape: pltpu.VMEM(shape, parts.dtype)
+    made = pl.pallas_call(
+        functools.partial(sum_kernel, grid_of, zp, cut, small),
+        out_shape=tuple(out_shape),
+        in_specs=[anywhere] * len(args),
+        out_specs=(anywhere,) * len(args),
+        scratch_shapes=[
+            vmem((payloads, zp, nx, rows, width)),
+            vmem((payloads, zp, nx, rows, width)),
+            vmem((payloads,) + turns + (rows, cut)),
+            vmem((payloads,) + turns + (rows, width - cut)),
+            vmem((payloads, turns[0], rows, width)),
+            vmem((payloads, turns[1], rows, width)),
+            dma((zp, nx)),
+            dma((zp, nx)),
+            dma(turns + (2,)),
+            dma((turns[0],)),
+            dma((turns[1],)),
+            dma((zp, nx, NC)),
+            dma((zp * nx * 6 + 8,)),
+        ],
+        compiler_params=pltpu.CompilerParams(
+            collective_id=number,
+            has_side_effects=True,
+            vmem_limit_bytes=56 * 2**20,
+        ),
+    )(*args)
+    return made if small else made[0]
 
 
 def attention_bias(segment, labels_all, query_places, key_places):
@@ -172,7 +618,8 @@
     expert_down,
     cotangent,
 ):
-    grid = Grid(wide, ep)
+    grid_of = functools.partial(Grid, wide, ep)
+    grid = grid_of()
     nx, ny = grid.nx, grid.ny
     tok_rows, width = activations.shape
     heads = width // HD
@@ -184,8 +631,12 @@
     sources = ZP * nx * NC
     capacity = min((tok_rows * top_count * 10 // (7 * experts) + 7) // 8 * 8, tok_rows)
 
-    small = jnp.concatenate(
+    bundle = jnp.concatenate(
         [
+            query_weight,
+            key_weight,
+            value_weight,
+            output_weight,
             router_weight,
             gain_attention[:, None],
             gain_experts[:, None],
@@ -193,29 +644,25 @@
         ],
         axis=1,
     )
+    integers = jnp.concatenate([routes.T, segment[None, :]], axis=0)
+    bundle_all, group_rows, integers_all = gather_first(
+        grid_of, bundle, activations, integers
+    )
+    group_rows = group_rows.at[0, 0].set(activations).reshape(-1, width)
+    integers_all = integers_all.at[0, 0, 0].set(integers)
+    integers_all = integers_all.reshape(sources, top_count + 1, tok_rows)
+    bundle_all = bundle_all.reshape(width, bundle.shape[1])
+    w_query, w_key, w_value, w_out = (
+        bundle_all[:, i * width : (i + 1) * width] for i in range(4)
+    )
+    small_all = bundle_all[:, 4 * width :]
     gather_all = lambda v: lax.all_gather(v, BOTH, axis=0, tiled=True)
-    small_all = gather_all(small)
-    w_query = gather_all(query_weight)
-    w_key = gather_all(key_weight)
-    w_value = gather_all(value_weight)
-    w_out = gather_all(output_weight)
-    s_gate = gather_all(shared_gate)
-    s_up = gather_all(shared_up)
+    s_both = gather_all(jnp.concatenate([shared_gate, shared_up], axis=1))
+    s_gate, s_up = s_both[:, :hidden_width], s_both[:, hidden_width:]
     s_down = gather_all(shared_down)
     w_router = small_all[:, :experts]
     gain_one = small_all[:, experts].astype(f32)
     gain_two = small_all[:, experts + 1].astype(f32)
-
-    def gather_group(v):
-        return grid.gather(grid.gather(v, "c", 0), "x", 0)
-
-    def gather_pair(v):
-        return grid.gather(gather_group(v), "p", 0)
-
-    integers = jnp.concatenate([routes.T, segment[None, :]], axis=0)
-    integers_all = gather_pair(integers).reshape(sources, top_count + 1, tok_rows)
-    group_rows = gather_group(activations).reshape(nx * NC * tok_rows, width)
-    cot_all = gather_pair(cotangent).reshape(sources, tok_rows, width)
 
     inputs = activations.astype(f32)
     inverse_one = norm_scale(inputs)
@@ -249,7 +696,9 @@
     inverse_two = norm_scale(middle)
     normed_two = (middle * inverse_two * gain_two).astype(bf16)
 
-    rows_all = gather_pair(normed_two).reshape(sources, tok_rows, width)
+    rows_all, cot_all = exchange(grid_of, ZP, 1, normed_two, cotangent)
+    rows_all = rows_all.reshape(sources, tok_rows, width)
+    cot_all = cot_all.reshape(sources, tok_rows, width)
     router_probs_all = jax.nn.softmax(
         times(rows_all.reshape(-1, width), w_router).reshape(sources, tok_rows, experts),
         axis=-1,
@@ -315,21 +764,19 @@
         ).astype(bf16)
         row_parts = row_parts + unpick(row_grad)
 
-    def scatter_pair(v):
-        v = v.reshape((ZP, nx, NC) + v.shape[1:])
-        return grid.scatter(grid.scatter(grid.scatter(v, "c", 2), "x", 1), "p", 0)
-
-    routed_grad = scatter_pair(row_parts.astype(bf16)).astype(f32)
-    routed = scatter_pair(out_parts.astype(bf16)).astype(f32)
+    both_parts = jnp.stack([row_parts.astype(bf16), out_parts.astype(bf16)])
+    sums, sent = sum_around(
+        grid_of,
+        ZP,
+        2,
+        both_parts.reshape(2, ZP, nx, NC, tok_rows, width),
+        jnp.stack(prob_parts, axis=1).reshape(ZP, nx, NC, mine, tok_rows),
+    )
+    routed_grad = sums[0].astype(f32)
+    routed = sums[1].astype(f32)
     expert_down_grad = reduce_experts(grid, jnp.stack(down_w_grads))
     expert_gate_grad = reduce_experts(grid, jnp.stack(gate_w_grads))
     expert_up_grad = reduce_experts(grid, jnp.stack(up_w_grads))
-    sent = jnp.stack(prob_parts, axis=1).reshape(ZP, nx, NC, mine, tok_rows)
-    for axis, at in (("c", 2), ("x", 1), ("p", 0)):
-        n = grid.size(axis)
-        parts = [lax.index_in_dim(sent, d, at, keepdims=False) for d in range(n)]
-        got = [parts[0]] + [grid.send(parts[n - d], axis, n - d) for d in range(1, n)]
-        sent = jnp.stack(got, axis=at)
     dz = (grid.zm + jnp.arange(ZP, dtype=jnp.int32)) % ZP
     owner = block_places.reshape(1, nx, NC, 1) * local_experts
     owner = owner + dz[:, None, None, None] * mine + jnp.arange(mine, dtype=jnp.int32)
@@ -408,12 +855,10 @@
         "hqk,qhd->khd", probs.astype(bf16), grad_heads, preferred_element_type=f32
     )
 
-    def scatter_group(v):
-        v = v.astype(bf16).reshape(nx, NC, tok_rows, width)
-        return grid.scatter(grid.scatter(v, "c", 1), "x", 0)
-
-    value_act_grad = scatter_group(value_part)
-    key_act_grad = scatter_group(key_part)
+    parts = jnp.stack([value_part.astype(bf16), key_part.astype(bf16)])
+    value_act_grad, key_act_grad = sum_around(
+        grid_of, 1, 3, parts.reshape(2, 1, nx, NC, tok_rows, width)
+    )
     query_w_grad = contract_rows(normed_one, query_act_grad)
     key_w_grad = contract_rows(normed_one, key_act_grad)
     value_w_grad = contract_rows(normed_one, value_act_grad)
@@ -461,12 +906,9 @@
     extras = jnp.concatenate(
         [extras, count_block, jnp.zeros((wide, ep, 7, 128), f32)], axis=2
     )
-    extra_sum = lax.psum_scatter(
-        extras.reshape(wide * ep, share + 8, 128),
-        BOTH,
-        scatter_dimension=0,
-        tiled=True,
-    )[0]
+    extra_sum = reduce_dense(
+        grid, extras.reshape(NZ, ny, nx, NC, share + 8, 128), "cxyz"
+    )
     return (
         block_out,
         input_grad,

time: 1340 us -> 997 us (0.74)
  waiting for transfers between devices: 746 us -> 183 us
  Pallas kernels: 0 us -> 227 us
  matrix products: 226 us -> 276 us
  blocking collectives: 44.3 us -> 0 us
  starting transfers between devices: 82.6 us -> 117 us
  local copies, waits for them, and re-layouts: 119 us -> 95 us
  other arithmetic: 91.2 us -> 72.5 us
    ppermute x78 -> x60, waiting for transfers between devices: 448 us -> 183 us  [send(): return lax.ppermute(value, BOTH, self.pairs(moves[axis]))]
    pallas_call x0 -> x4, Pallas kernels: none -> 227 us  [the longest x2 92.5 us: sum_around(): pl.pallas_call(functools.partial(sum_kernel, grid_of, zp, cut, small), ou...]
    all_gather x7 -> x2, waiting for transfers between devices: 208 us -> 0.02 us  [body(): gather_all = lambda v: lax.all_gather(v, BOTH, axis=0, tiled=True)]
    reduce_scatter x1 -> x0, waiting for transfers between devices: 87 us -> none  [body(): lax.psum_scatter(extras.reshape(wide * ep, share + 8, 128), BOTH, scatter...]
    all_gather x1 -> x0, blocking collectives: 44.3 us -> none  [body(): gather_all = lambda v: lax.all_gather(v, BOTH, axis=0, tiled=True)]
    ppermute x78 -> x60, starting transfers between devices: 82.3 us -> 117 us  [send(): return lax.ppermute(value, BOTH, self.pairs(moves[axis]))]
    unnamed x220 -> x199, local copies, waits for them, and re-layouts: 51.9 us -> 18.4 us
    another operation x3 -> x6, local copies, waits for them, and re-layouts: 0.03 us -> 26 us  [the longest x4 26 us: body(): parts = jnp.stack([value_part.astype(bf16), key_part.astype(bf16)])]
  transfers between devices with their start and end apart: 86 -> 62, of which waited for: 43 -> 26; matrix products, arithmetic and copies ran while one was open for 23% -> 34% of each run, Pallas kernels for 0% -> 19%
where the time goes in v2:
time: 997 us; the launch traced here: 987 us
  matrix products  276 us (28%)
  Pallas kernels  227 us (23%)
  waiting for transfers between devices  183 us (18%)
  starting transfers between devices  117 us (12%)
  local copies, waits for them, and re-layouts  95 us (10%)
  other arithmetic  72.5 us (7%)
  between operations  16.1 us (2%)
    ppermute x60, waiting for transfers between devices, send(): return lax.ppermute(value, BOTH, self.pairs(moves[axis]))  183 us
    ppermute x60, starting transfers between devices, send(): return lax.ppermute(value, BOTH, self.pairs(moves[axis]))  117 us
    pallas_call x2, Pallas kernels, sum_around(): pl.pallas_call(functools.partial(sum_kernel, grid_of, zp, cut, small), ou...  92.5 us
    pallas_call x1, Pallas kernels, gather_first(): pl.pallas_call(functools.partial(gather_kernel, grid_of, cut), out_shape=...  85.8 us
    dot_general x13, matrix products, times(): return jnp.dot(left, right, preferred_element_type=f32)  82.1 us
    dot_general x13, matrix products, times_transposed(): lax.dot_general(left, right, (((1,), (1,)), ((), ())), preferred_element_...  72 us
    pallas_call x1, Pallas kernels, exchange(): pl.pallas_call(functools.partial(exchange_kernel, grid_of, zp, arrays[0]....  48.3 us
    dot_general x13, matrix products, contract_rows(): lax.dot_general(left, right, (((0,), (0,)), ((), ())), preferred_element_...  40.7 us
  transfers between devices with their start and end apart: 62, of which 26 were waited for; matrix products, arithmetic and copies ran while one was open for 34% of the time, Pallas kernels for 19%

profile of v2, /device:TPU:0, one launch (start us, length us, event | category | flops | bytes accessed | tf_op | source)
XLA Modules:
  0.0 987.2 jit_solution(10500562623887910798)
XLA Ops:
  13.5 85.8 %shard_map.288 = (bf16[32,40,5248]{2,1,0:T(8,128)(2,1)}, bf16[2,2,256,1280]{3,2,1,0:T(8,128)(2,1)}, s32[2,2,2,8,256]{4,3,2,1,0:T(8,128)}) custom-call(bf16[40,5248]{1,0:T(8,128)(2,1)} %concatenate.41.w_ref, bf16[256,1280]{1,0:T(8,128)(2,1)} %rows_ref.1, s32[8,256]{1,0:T(8,128)} %pad_add_fusion.ints_ref), custom_call_target="tpu_custom_call" | custom-call | tf_op jit(solution)/shard_map/pallas_call | solution.py:275
  105.7 7.7 convolution_convert_fusion.10
  131.8 9.0 fusion.199
  156.8 48.3 %shard_map.289 = (bf16[2,2,2,256,1280]{4,3,2,1,0:T(8,128)(2,1)}, bf16[2,2,2,256,1280]{4,3,2,1,0:T(8,128)(2,1)}) custom-call(bf16[256,1280]{1,0:T(8,128)(2,1)} %multiply_convert_fusion.13.refs_0_, bf16[256,1280]{1,0:T(8,128)(2,1)} %refs_1_.1), custom_call_target="tpu_custom_call" | custom-call | tf_op jit(solution)/shard_map/pallas_call | solution.py:401
  218.4 8.4 fusion.81
  240.4 17.5 %fusion.79 = f32[1280,896]{1,0:T(8,128)} fusion(bf16[1280,1280]{1,0:T(8,128)(2,1)S(1)} %bitcast.541, bf16[4,1280,896]{2,1,0:T(8,128)(2,1)} %param.34, s32[]{:T(128)S(6)} %select_n.398), kind=kOutput, calls=%fused_computation.167 | convolution fusion | flops 2936012800 | bytes 10158084 | tf_op jit(solution)/shard_map/dot_general | solution.py:34
  262.6 9.2 multiply_convert_fusion.5
  287.4 12.6 %multiply_convert_fusion.7 = (bf16[1280,896]{1,0:T(8,128)(2,1)}, bf16[1280,896]{1,0:T(8,128)(2,1)}, bf16[1280,896]{1,0:T(8,128)(2,1)S(1)}) fusion(f32[1280,896]{1,0:T(8,128)} %fusion.79, f32[1280,896]{1,0:T(8,128)} %fusion.77, bf16[1280,1280]{1,0:T(8,128)(2,1)} %bitcast.558, bf16[4,896,1280]{2,1,0:T(8,128)(2,1)} %param.36, s32[]{:T(128)S(6)} %select_n.398), kind=kOutput, calls=%fused_computation.69 | convolution fusion | flops 2953216000 | bytes 21626884 | tf_op jit(solution)/shard_map/dot_general | solution.py:28
  344.9 8.8 fusion.82
  361.0 9.7 fusion.4
  399.8 8.9 pad_maximum_fusion.parts
  408.7 56.2 %shard_map.290 = (bf16[2,256,1280]{2,1,0:T(8,128)(2,1)}, f32[2,2,2,2,256]{4,3,2,1,0:T(2,128)}) custom-call(bf16[2,2,2,2,256,1280]{5,4,3,2,1,0:T(8,128)(2,1)} %pad_maximum_fusion.parts, f32[2,2,2,2,256]{4,3,2,1,0:T(2,128)} %pad_maximum_fusion.6.refs_0_), custom_call_target="tpu_custom_call" | custom-call | tf_op jit(solution)/shard_map/pallas_call | solution.py:531
  491.5 23.7 %collective-permute-done.53 = bf16[2,160,896]{2,1,0:T(8,128)(2,1)S(1)} collective-permute-done((bf16[2,160,896]{2,1,0:T(8,128)(2,1)S(1)}, bf16[2,160,896]{2,1,0:T(8,128)(2,1)S(1)}, u32[]{:S(2)}, u32[]{:S(2)}) %collective-permute-start.53) | collective-permute-done | bytes 573472 | tf_op jit(solution)/shard_map/ppermute | solution.py:86
  515.2 12.8 %collective-permute-start.51 = (bf16[2,160,896]{2,1,0:T(8,128)(2,1)S(1)}, bf16[2,160,896]{2,1,0:T(8,128)(2,1)S(1)}, u32[]{:S(2)}, u32[]{:S(2)}) collective-permute-start(bf16[2,160,896]{2,1,0:T(8,128)(2,1)S(1)} %get-tuple-element.101), channel_id=1, source_target_pairs={{0,24},{1,25},{2,26},{3,27},{4,28},{5,29},{6,30},{7,31},{8,0},{9,1... | collective-permute-start | bytes 1720328 | tf_op jit(solution)/shard_map/ppermute | solution.py:86
  528.1 31.1 %collective-permute-start.57 = (bf16[2,112,1280]{2,1,0:T(8,128)(2,1)S(1)}, bf16[2,112,1280]{2,1,0:T(8,128)(2,1)S(1)}, u32[]{:S(2)}, u32[]{:S(2)}) collective-permute-start(bf16[2,112,1280]{2,1,0:T(8,128)(2,1)S(1)} %get-tuple-element.94), channel_id=1, source_target_pairs={{0,16},{1,17},{2,18},{3,19},{4,20},{5,21},{6,22},{7,23},{8,24},{9,... | collective-permute-start | bytes 1720328 | tf_op jit(solution)/shard_map/ppermute | solution.py:86
  559.5 28.1 %collective-permute-done.49 = bf16[2,160,896]{2,1,0:T(8,128)(2,1)S(1)} collective-permute-done((bf16[2,160,896]{2,1,0:T(8,128)(2,1)S(1)}, bf16[2,160,896]{2,1,0:T(8,128)(2,1)S(1)}, u32[]{:S(2)}, u32[]{:S(2)}) %collective-permute-start.49) | collective-permute-done | bytes 573472 | tf_op jit(solution)/shard_map/ppermute | solution.py:86
  591.0 21.2 %collective-permute-done.57 = bf16[2,112,1280]{2,1,0:T(8,128)(2,1)S(1)} collective-permute-done((bf16[2,112,1280]{2,1,0:T(8,128)(2,1)S(1)}, bf16[2,112,1280]{2,1,0:T(8,128)(2,1)S(1)}, u32[]{:S(2)}, u32[]{:S(2)}) %collective-permute-start.57) | collective-permute-done | bytes 573472 | tf_op jit(solution)/shard_map/ppermute | solution.py:86
  668.0 7.9 multiply_convert_fusion
  686.2 7.6 copy.306
  699.1 36.3 %shard_map.291 = bf16[2,256,1280]{2,1,0:T(8,128)(2,1)} custom-call(bf16[2,1,2,2,256,1280]{5,4,3,2,1,0:T(8,128)(2,1)} %pad_maximum_fusion.1.parts), custom_call_target="tpu_custom_call" | custom-call | tf_op jit(solution)/shard_map/pallas_call | solution.py:531
  801.9 10.8 %collective-permute-start.3 = (f32[48,128]{0,1:T(8,128)S(1)}, f32[48,128]{0,1:T(8,128)S(1)}, u32[]{:S(2)}, u32[]{:S(2)}) collective-permute-start(f32[48,128]{0,1:T(8,128)S(1)} %bitcast.596), channel_id=1, source_target_pairs={{0,8},{1,9},{2,10},{3,11},{4,12},{5,13},{6,14},{7,15},{8,16},{9,17... | collective-permute-start | bytes 73736 | tf_op jit(solution)/shard_map/ppermute | solution.py:86
  851.2 9.5 collective-permute-done.31
  862.0 30.1 %collective-permute-done.44 = bf16[4,28,1280]{2,1,0:T(8,128)(2,1)S(1)} collective-permute-done((bf16[4,28,1280]{2,1,0:T(8,128)(2,1)S(1)}, bf16[4,28,1280]{2,1,0:T(8,128)(2,1)S(1)}, u32[]{:S(2)}, u32[]{:S(2)}) %collective-permute-start.44) | collective-permute-done | bytes 286752 | tf_op jit(solution)/shard_map/ppermute | solution.py:86
  918.0 14.7 %collective-permute-done.13 = bf16[4,2,40,1280]{3,2,0,1:T(8,128)(2,1)S(1)} collective-permute-done((bf16[4,2,40,1280]{3,2,0,1:T(8,128)(2,1)S(1)}, bf16[4,2,40,1280]{3,2,0,1:T(8,128)(2,1)S(1)}, u32[]{:S(2)}, u32[]{:S(2)}) %collective-permute-start.13) | collective-permute-done | bytes 819232 | tf_op jit(solution)/shard_map/ppermute | solution.py:86
  (537 shorter events, 455.2 us)
Async XLA Ops:
  7.2 608.6 %all-gather.6.cloned.1.call-start = ((), (), s32[]{:S(2)}) async-start(), calls=%async_computation.1 | async-start | bytes 2703360 | tf_op jit(solution)/shard_map/all_gather | solution.py:659
  7.9 611.0 %all-gather.4.cloned.1.call-start = ((), (), s32[]{:S(2)}) async-start(), calls=%async_computation | async-start | bytes 4730880 | tf_op jit(solution)/shard_map/all_gather | solution.py:659
  317.6 170.3 %collective-permute-start.56 = (bf16[2,4,112,1280]{3,2,0,1:T(8,128)(2,1)}, bf16[2,4,112,1280]{3,2,0,1:T(8,128)(2,1)}, u32[]{:S(2)}, u32[]{:S(2)}) collective-permute-start(bf16[2,4,112,1280]{3,2,0,1:T(8,128)(2,1)} %bitcast.507), channel_id=1, source_target_pairs={{0,4},{1,5},{2,6},{3,7},{4,0},{5,1},{6,2},{7,3},{8,12},{9,13},{10,... | collective-permute-start | bytes 6881288 | tf_op jit(solution)/shard_map/ppermute | solution.py:86
  330.4 139.4 %collective-permute-start.52 = (bf16[2,4,160,896]{3,2,0,1:T(8,128)(2,1)}, bf16[2,4,160,896]{3,2,0,1:T(8,128)(2,1)}, u32[]{:S(2)}, u32[]{:S(2)}) collective-permute-start(bf16[2,4,160,896]{3,2,0,1:T(8,128)(2,1)} %bitcast.508), channel_id=1, source_target_pairs={{0,4},{1,5},{2,6},{3,7},{4,0},{5,1},{6,2},{7,3},{8,12},{9,13},{10,... | collective-permute-start | bytes 6881288 | tf_op jit(solution)/shard_map/ppermute | solution.py:86
  343.3 136.7 %collective-permute-start.48 = (bf16[2,4,160,896]{3,2,0,1:T(8,128)(2,1)}, bf16[2,4,160,896]{3,2,0,1:T(8,128)(2,1)}, u32[]{:S(2)}, u32[]{:S(2)}) collective-permute-start(bf16[2,4,160,896]{3,2,0,1:T(8,128)(2,1)} %bitcast.509), channel_id=1, source_target_pairs={{0,4},{1,5},{2,6},{3,7},{4,0},{5,1},{6,2},{7,3},{8,12},{9,13},{10,... | collective-permute-start | bytes 6881288 | tf_op jit(solution)/shard_map/ppermute | solution.py:86
  472.8 42.3 %collective-permute-start.53 = (bf16[2,160,896]{2,1,0:T(8,128)(2,1)S(1)}, bf16[2,160,896]{2,1,0:T(8,128)(2,1)S(1)}, u32[]{:S(2)}, u32[]{:S(2)}) collective-permute-start(bf16[2,160,896]{2,1,0:T(8,128)(2,1)S(1)} %get-tuple-element.97), channel_id=1, source_target_pairs={{0,16},{1,17},{2,18},{3,19},{4,20},{5,21},{6,22},{7,23},{8,24},{9,... | collective-permute-start | bytes 1720328 | tf_op jit(solution)/shard_map/ppermute | solution.py:86
  476.2 51.9 %collective-permute-start.54 = (bf16[2,160,896]{2,1,0:T(8,128)(2,1)S(1)}, bf16[2,160,896]{2,1,0:T(8,128)(2,1)S(1)}, u32[]{:S(2)}, u32[]{:S(2)}) collective-permute-start(bf16[2,160,896]{2,1,0:T(8,128)(2,1)S(1)} %get-tuple-element.99), channel_id=1, source_target_pairs={{0,8},{1,9},{2,10},{3,11},{4,12},{5,13},{6,14},{7,15},{8,16},{9,17... | collective-permute-start | bytes 1720328 | tf_op jit(solution)/shard_map/ppermute | solution.py:86
  477.2 82.1 %collective-permute-start.55 = (bf16[2,160,896]{2,1,0:T(8,128)(2,1)S(1)}, bf16[2,160,896]{2,1,0:T(8,128)(2,1)S(1)}, u32[]{:S(2)}, u32[]{:S(2)}) collective-permute-start(bf16[2,160,896]{2,1,0:T(8,128)(2,1)S(1)} %get-tuple-element.98), channel_id=1, source_target_pairs={{0,24},{1,25},{2,26},{3,27},{4,28},{5,29},{6,30},{7,31},{8,0},{9,1... | collective-permute-start | bytes 1720328 | tf_op jit(solution)/shard_map/ppermute | solution.py:86
  482.4 105.3 %collective-permute-start.49 = (bf16[2,160,896]{2,1,0:T(8,128)(2,1)S(1)}, bf16[2,160,896]{2,1,0:T(8,128)(2,1)S(1)}, u32[]{:S(2)}, u32[]{:S(2)}) collective-permute-start(bf16[2,160,896]{2,1,0:T(8,128)(2,1)S(1)} %get-tuple-element.100), channel_id=1, source_target_pairs={{0,16},{1,17},{2,18},{3,19},{4,20},{5,21},{6,22},{7,23},{8,24},{9,... | collective-permute-start | bytes 1720328 | tf_op jit(solution)/shard_map/ppermute | solution.py:86
  488.0 101.2 %collective-permute-start.50 = (bf16[2,160,896]{2,1,0:T(8,128)(2,1)S(1)}, bf16[2,160,896]{2,1,0:T(8,128)(2,1)S(1)}, u32[]{:S(2)}, u32[]{:S(2)}) collective-permute-start(bf16[2,160,896]{2,1,0:T(8,128)(2,1)S(1)} %get-tuple-element.102), channel_id=1, source_target_pairs={{0,8},{1,9},{2,10},{3,11},{4,12},{5,13},{6,14},{7,15},{8,16},{9,17... | collective-permute-start | bytes 1720328 | tf_op jit(solution)/shard_map/ppermute | solution.py:86
  515.2 74.0 %collective-permute-start.51 = (bf16[2,160,896]{2,1,0:T(8,128)(2,1)S(1)}, bf16[2,160,896]{2,1,0:T(8,128)(2,1)S(1)}, u32[]{:S(2)}, u32[]{:S(2)}) collective-permute-start(bf16[2,160,896]{2,1,0:T(8,128)(2,1)S(1)} %get-tuple-element.101), channel_id=1, source_target_pairs={{0,24},{1,25},{2,26},{3,27},{4,28},{5,29},{6,30},{7,31},{8,0},{9,1... | collective-permute-start | bytes 1720328 | tf_op jit(solution)/shard_map/ppermute | solution.py:86
  528.1 84.2 %collective-permute-start.57 = (bf16[2,112,1280]{2,1,0:T(8,128)(2,1)S(1)}, bf16[2,112,1280]{2,1,0:T(8,128)(2,1)S(1)}, u32[]{:S(2)}, u32[]{:S(2)}) collective-permute-start(bf16[2,112,1280]{2,1,0:T(8,128)(2,1)S(1)} %get-tuple-element.94), channel_id=1, source_target_pairs={{0,16},{1,17},{2,18},{3,19},{4,20},{5,21},{6,22},{7,23},{8,24},{9,... | collective-permute-start | bytes 1720328 | tf_op jit(solution)/shard_map/ppermute | solution.py:86
  559.2 53.1 %collective-permute-start.58 = (bf16[2,112,1280]{2,1,0:T(8,128)(2,1)S(1)}, bf16[2,112,1280]{2,1,0:T(8,128)(2,1)S(1)}, u32[]{:S(2)}, u32[]{:S(2)}) collective-permute-start(bf16[2,112,1280]{2,1,0:T(8,128)(2,1)S(1)} %get-tuple-element.96), channel_id=1, source_target_pairs={{0,8},{1,9},{2,10},{3,11},{4,12},{5,13},{6,14},{7,15},{8,16},{9,17... | collective-permute-start | bytes 1720328 | tf_op jit(solution)/shard_map/ppermute | solution.py:86
  587.7 26.3 %collective-permute-start.59 = (bf16[2,112,1280]{2,1,0:T(8,128)(2,1)S(1)}, bf16[2,112,1280]{2,1,0:T(8,128)(2,1)S(1)}, u32[]{:S(2)}, u32[]{:S(2)}) collective-permute-start(bf16[2,112,1280]{2,1,0:T(8,128)(2,1)S(1)} %get-tuple-element.95), channel_id=1, source_target_pairs={{0,24},{1,25},{2,26},{3,27},{4,28},{5,29},{6,30},{7,31},{8,0},{9,1... | collective-permute-start | bytes 1720328 | tf_op jit(solution)/shard_map/ppermute | solution.py:86
  759.0 69.0 %collective-permute-start.42 = (bf16[4,2,2,28,1280]{4,0,3,2,1:T(4,128)(2,1)}, bf16[4,2,2,28,1280]{4,0,3,2,1:T(4,128)(2,1)}, u32[]{:S(2)}, u32[]{:S(2)}) collective-permute-start(bf16[4,2,2,28,1280]{4,0,3,2,1:T(4,128)(2,1)} %copy.327), channel_id=1, source_target_pairs={{0,1},{1,0},{2,3},{3,2},{4,5},{5,4},{6,7},{7,6},{8,9},{9,8},{10,11... | collective-permute-start | bytes 3440648 | tf_op jit(solution)/shard_map/ppermute | solution.py:86
  761.5 69.4 %collective-permute-start.36 = (bf16[4,2,2,40,896]{4,3,0,1,2:T(8,128)(2,1)}, bf16[4,2,2,40,896]{4,3,0,1,2:T(8,128)(2,1)}, u32[]{:S(2)}, u32[]{:S(2)}) collective-permute-start(bf16[4,2,2,40,896]{4,3,0,1,2:T(8,128)(2,1)} %bitcast.514), channel_id=1, source_target_pairs={{0,1},{1,0},{2,3},{3,2},{4,5},{5,4},{6,7},{7,6},{8,9},{9,8},{10,11... | collective-permute-start | bytes 3440648 | tf_op jit(solution)/shard_map/ppermute | solution.py:86
  835.6 25.2 %collective-permute-start.31 = (bf16[4,2,40,896]{3,2,0,1:T(8,128)(2,1)S(1)}, bf16[4,2,40,896]{3,2,0,1:T(8,128)(2,1)S(1)}, u32[]{:S(2)}, u32[]{:S(2)}) collective-permute-start(bf16[4,2,40,896]{3,2,0,1:T(8,128)(2,1)S(1)} %dynamic-slice_bitcast_fusion.34), channel_id=1, source_target_pairs={{0,4},{1,5},{2,6},{3,7},{4,0},{5,1},{6,2},{7,3},{8,12},{9,13},{10,... | collective-permute-start | bytes 1720328 | tf_op jit(solution)/shard_map/ppermute | solution.py:86
  838.0 77.3 %collective-permute-start.25 = (bf16[4,2,40,1280]{3,2,0,1:T(8,128)(2,1)S(1)}, bf16[4,2,40,1280]{3,2,0,1:T(8,128)(2,1)S(1)}, u32[]{:S(2)}, u32[]{:S(2)}) collective-permute-start(bf16[4,2,40,1280]{3,2,0,1:T(8,128)(2,1)S(1)} %dynamic-slice_bitcast_fusion.19), channel_id=1, source_target_pairs={{0,2},{1,3},{2,0},{3,1},{4,6},{5,7},{6,4},{7,5},{8,10},{9,11},{10,... | collective-permute-start | bytes 2457608 | tf_op jit(solution)/shard_map/ppermute | solution.py:86
  839.4 77.3 %collective-permute-start.19 = (bf16[4,2,40,1280]{3,2,0,1:T(8,128)(2,1)S(1)}, bf16[4,2,40,1280]{3,2,0,1:T(8,128)(2,1)S(1)}, u32[]{:S(2)}, u32[]{:S(2)}) collective-permute-start(bf16[4,2,40,1280]{3,2,0,1:T(8,128)(2,1)S(1)} %dynamic-slice_bitcast_fusion.20), channel_id=1, source_target_pairs={{0,2},{1,3},{2,0},{3,1},{4,6},{5,7},{6,4},{7,5},{8,10},{9,11},{10,... | collective-permute-start | bytes 2457608 | tf_op jit(solution)/shard_map/ppermute | solution.py:86
  848.6 43.4 %collective-permute-start.44 = (bf16[4,28,1280]{2,1,0:T(8,128)(2,1)S(1)}, bf16[4,28,1280]{2,1,0:T(8,128)(2,1)S(1)}, u32[]{:S(2)}, u32[]{:S(2)}) collective-permute-start(bf16[4,28,1280]{2,1,0:T(8,128)(2,1)S(1)} %dynamic-slice_bitcast_fusion.40), channel_id=1, source_target_pairs={{0,2},{1,3},{2,0},{3,1},{4,6},{5,7},{6,4},{7,5},{8,10},{9,11},{10,... | collective-permute-start | bytes 860168 | tf_op jit(solution)/shard_map/ppermute | solution.py:86
  850.1 42.1 %collective-permute-start.38 = (bf16[4,40,896]{2,1,0:T(8,128)(2,1)S(1)}, bf16[4,40,896]{2,1,0:T(8,128)(2,1)S(1)}, u32[]{:S(2)}, u32[]{:S(2)}) collective-permute-start(bf16[4,40,896]{2,1,0:T(8,128)(2,1)S(1)} %dynamic-slice_bitcast_fusion.41), channel_id=1, source_target_pairs={{0,4},{1,5},{2,6},{3,7},{4,0},{5,1},{6,2},{7,3},{8,12},{9,13},{10,... | collective-permute-start | bytes 860168 | tf_op jit(solution)/shard_map/ppermute | solution.py:86
  860.9 36.5 %collective-permute-start.32 = (bf16[4,40,896]{2,1,0:T(8,128)(2,1)S(1)}, bf16[4,40,896]{2,1,0:T(8,128)(2,1)S(1)}, u32[]{:S(2)}, u32[]{:S(2)}) collective-permute-start(bf16[4,40,896]{2,1,0:T(8,128)(2,1)S(1)} %dynamic-slice_bitcast_fusion.42), channel_id=1, source_target_pairs={{0,2},{1,3},{2,0},{3,1},{4,6},{5,7},{6,4},{7,5},{8,10},{9,11},{10,... | collective-permute-start | bytes 860168 | tf_op jit(solution)/shard_map/ppermute | solution.py:86
  915.6 25.9 %collective-permute-start.26 = (bf16[4,40,1280]{2,1,0:T(8,128)(2,1)S(1)}, bf16[4,40,1280]{2,1,0:T(8,128)(2,1)S(1)}, u32[]{:S(2)}, u32[]{:S(2)}) collective-permute-start(bf16[4,40,1280]{2,1,0:T(8,128)(2,1)S(1)} %dynamic-slice_bitcast_fusion.35), channel_id=1, source_target_pairs={{0,4},{1,5},{2,6},{3,7},{4,0},{5,1},{6,2},{7,3},{8,12},{9,13},{10,... | collective-permute-start | bytes 1228808 | tf_op jit(solution)/shard_map/ppermute | solution.py:86
  916.9 33.3 %collective-permute-start.20 = (bf16[4,40,1280]{2,1,0:T(8,128)(2,1)S(1)}, bf16[4,40,1280]{2,1,0:T(8,128)(2,1)S(1)}, u32[]{:S(2)}, u32[]{:S(2)}) collective-permute-start(bf16[4,40,1280]{2,1,0:T(8,128)(2,1)S(1)} %dynamic-slice_bitcast_fusion.36), channel_id=1, source_target_pairs={{0,4},{1,5},{2,6},{3,7},{4,0},{5,1},{6,2},{7,3},{8,12},{9,13},{10,... | collective-permute-start | bytes 1228808 | tf_op jit(solution)/shard_map/ppermute | solution.py:86
  (133 other events, 1313.6 us)
Sparse Core Ops, SparseCore 0:
  10.9 80.3 all-gather.5
  345.0 75.9 all-gather.3

commit v3 on v2

--- a/solution.py
+++ b/solution.py
@@ -113,186 +113,6 @@
         return total.astype(value.dtype)
 
 
-def gather_kernel(
-    grid_of,
-    cut,
-    w_ref,
-    rows_ref,
-    ints_ref,
-    w_all,
-    rows_all,
-    ints_all,
-    plane_sem,
-    core_sem,
-    rows_sem,
-    ints_sem,
-    send_sem,
-    local_sem,
-):
-    grid = grid_of()
-    z, y, x, c, nx, ny = grid.z, grid.y, grid.x, grid.c, grid.nx, grid.ny
-    width = w_ref.shape[1]
-
-    def device(tz, ty, tx, tc):
-        return (tz * ny + ty, tx * NC + tc)
-
-    def slot(tz, ty, tx, tc):
-        return (tz * ny + ty) * (nx * NC) + tx * NC + tc
-
-    shift_z = lambda d: (z + d) % NZ
-    shift_p = lambda d: z // ZP * ZP + (z % ZP + d) % ZP
-    shift_y = lambda d: (y + d) % ny
-    shift_x = lambda d: (x + d) % nx
-    other = (c + 1) % NC
-    octet = [
-        (dz, dx, dc)
-        for dz in range(ZP)
-        for dx in range(nx)
-        for dc in range(NC)
-        if (dz, dx, dc) != (0, 0, 0)
-    ]
-
-    barrier = pltpu.get_barrier_semaphore()
-    greeted = (
-        [device(shift_z(d), y, x, c) for d in range(1, NZ)]
-        + [device(z, shift_y(d), x, c) for d in range(1, ny)]
-        + [device(shift_p(a), y, shift_x(b), (c + e) % NC) for a, b, e in octet]
-    )
-    for target in greeted:
-        pl.semaphore_signal(
-            barrier, inc=1, device_id=target, device_id_type=pl.DeviceIdType.MESH
-        )
-    pl.semaphore_wait(barrier, len(greeted))
-
-    started = []
-
-    def send(src, dst, sem, target):
-        copy = pltpu.make_async_remote_copy(
-            src_ref=src,
-            dst_ref=dst,
-            send_sem=send_sem.at[len(started)],
-            recv_sem=sem,
-            device_id=target,
-            device_id_type=pl.DeviceIdType.MESH,
-        )
-        copy.start()
-        started.append(copy)
-
-    def arrived(dst, sem):
-        pltpu.make_async_copy(dst, dst, sem).wait()
-
-    half = (pl.ds(0, cut), pl.ds(cut, width - cut))
-    block = lambda dz, dy, dx, tc: w_all.at[
-        slot(shift_z(-dz), shift_y(-dy), shift_x(-dx), tc)
-    ]
-
-    own = pltpu.make_async_copy(w_ref, block(0, 0, 0, c), local_sem)
-    own.start()
-    my_slot = w_all.at[slot(z, y, x, c)]
-    for d in range(1, nx):
-        send(rows_ref, rows_all.at[nx - d, 0], rows_sem.at[nx - d, 0], device(z, y, shift_x(d), c))
-    for d in range(1, NZ):
-        send(w_ref, my_slot, plane_sem.at[d, 0, 0, 0], device(shift_z(d), y, x, c))
-    send(rows_ref, rows_all.at[0, 1], rows_sem.at[0, 1], device(z, y, x, other))
-    for a, b, e in octet:
-        send(
-            ints_ref,
-            ints_all.at[(ZP - a) % ZP, (nx - b) % nx, e],
-            ints_sem.at[(ZP - a) % ZP, (nx - b) % nx, e],
-            device(shift_p(a), y, shift_x(b), (c + e) % NC),
-        )
-
-    def spread(src, dst, dz):
-        for d in range(1, ny):
-            send(src, dst, plane_sem.at[dz, d, 0, 0], device(z, shift_y(d), x, c))
-        for d in range(1, nx):
-            send(src, dst, plane_sem.at[dz, 0, d, 0], device(z, y, shift_x(d), c))
-        send(src, dst, core_sem.at[dz, 0, 0], device(z, y, x, other))
-
-    spread(w_ref, my_slot, 0)
-    for d in range(1, NZ):
-        here = block(d, 0, 0, c)
-        arrived(here, plane_sem.at[d, 0, 0, 0])
-        spread(here, here, d)
-    for d in range(1, nx):
-        arrived(rows_all.at[nx - d, 0], rows_sem.at[nx - d, 0])
-        send(rows_all.at[nx - d, 0], rows_all.at[nx - d, 1], rows_sem.at[nx - d, 1], device(z, y, x, other))
-    for dz in range(NZ):
-        for dy in range(1, ny):
-            here = block(dz, dy, 0, c)
-            arrived(here, plane_sem.at[dz, dy, 0, 0])
-            for d in range(1, nx):
-                send(
-                    here.at[:, half[0]],
-                    here.at[:, half[0]],
-                    plane_sem.at[dz, dy, d, 0],
-                    device(z, y, shift_x(d), c),
-                )
-            send(here, here, core_sem.at[dz, dy, 0], device(z, y, x, other))
-        for dx in range(1, nx):
-            here = block(dz, 0, dx, c)
-            arrived(here, plane_sem.at[dz, 0, dx, 0])
-            for d in range(1, ny):
-                send(
-                    here.at[:, half[1]],
-                    here.at[:, half[1]],
-                    plane_sem.at[dz, d, dx, 1],
-                    device(z, shift_y(d), x, c),
-                )
-            send(here, here, core_sem.at[dz, 0, dx], device(z, y, x, other))
-    for dz in range(NZ):
-        for dy in range(1, ny):
-            for dx in range(1, nx):
-                here = block(dz, dy, dx, c)
-                for part in range(2):
-                    arrived(here.at[:, half[part]], plane_sem.at[dz, dy, dx, part])
-                send(here, here, core_sem.at[dz, dy, dx], device(z, y, x, other))
-    for dx in range(nx):
-        arrived(rows_all.at[dx, 1], rows_sem.at[dx, 1])
-    for a, b, e in octet:
-        arrived(ints_all.at[a, b, e], ints_sem.at[a, b, e])
-    for dz in range(NZ):
-        for dy in range(ny):
-            for dx in range(nx):
-                arrived(block(dz, dy, dx, other), core_sem.at[dz, dy, dx])
-    own.wait()
-    for copy in started:
-        copy.wait_send()
-
-
-def gather_first(grid_of, w, rows, ints):
-    grid = grid_of()
-    nx, ny = grid.nx, grid.ny
-    places = NZ * ny * nx * NC
-    cut = w.shape[1] // 2 // 128 * 128
-    sends = (
-        (nx - 1) * 2 + 1 + (NZ - 1) + (ZP * nx * NC - 1)
-        + NZ * (ny + nx - 1)
-        + NZ * ((ny - 1) * nx + (nx - 1) * ny + (ny - 1) * (nx - 1))
-    )
-    anywhere = pl.BlockSpec(memory_space=pl.ANY)
-    dma = pltpu.SemaphoreType.DMA
-    return pl.pallas_call(
-        functools.partial(gather_kernel, grid_of, cut),
-        out_shape=(
-            jax.ShapeDtypeStruct((places,) + w.shape, w.dtype),
-            jax.ShapeDtypeStruct((nx, NC) + rows.shape, rows.dtype),
-            jax.ShapeDtypeStruct((ZP, nx, NC) + ints.shape, ints.dtype),
-        ),
-        in_specs=[anywhere] * 3,
-        out_specs=(anywhere,) * 3,
-        scratch_shapes=[
-            dma((NZ, ny, nx, 2)),
-            dma((NZ, ny, nx)),
-            dma((nx, NC)),
-            dma((ZP, nx, NC)),
-            dma((sends,)),
-            dma,
-        ],
-        compiler_params=pltpu.CompilerParams(collective_id=0, has_side_effects=True),
-    )(w, rows, ints)
-
-
 class Sender:
     def __init__(self, sems):
         self.sems, self.started = sems, []
@@ -338,6 +158,173 @@
         z * grid.ny + grid.y,
         (grid.x + b) % grid.nx * NC + (grid.c + e) % NC,
     )
+
+
+def gather_kernel(
+    grid_of,
+    w_ref,
+    rows_ref,
+    cot_ref,
+    ints_ref,
+    w_all,
+    rows_all,
+    cot_all,
+    ints_all,
+    plane_sem,
+    core_sem,
+    rows_sem,
+    cot_sem,
+    ints_sem,
+    send_sem,
+    local_sem,
+):
+    grid = grid_of()
+    z, y, x, c, nx, ny = grid.z, grid.y, grid.x, grid.c, grid.nx, grid.ny
+
+    def device(tz, ty, tx, tc):
+        return (tz * ny + ty, tx * NC + tc)
+
+    def block(dz, dy, dx, tc):
+        place = (z + NZ - dz) % NZ * ny + (y + ny - dy) % ny
+        return w_all.at[place * (nx * NC) + (x + nx - dx) % nx * NC + tc]
+
+    shift_z = lambda d: (z + d) % NZ
+    shift_y = lambda d: (y + d) % ny
+    shift_x = lambda d: (x + d) % nx
+    back = lambda d: (nx - d) % nx
+    other = (c + 1) % NC
+    to = functools.partial(stepped, grid, ZP)
+    greet(
+        [device(shift_z(d), y, x, c) for d in range(1, NZ)]
+        + [device(z, shift_y(d), x, c) for d in range(1, ny)]
+        + [to(*s) for s in around(grid, ZP)]
+    )
+    send = Sender(send_sem)
+    locals_ = [
+        (w_ref, block(0, 0, 0, c)),
+        (rows_ref, rows_all.at[0, 0]),
+        (cot_ref, cot_all.at[0, 0, 0]),
+        (ints_ref, ints_all.at[0, 0, 0]),
+    ]
+    locals_ = [
+        pltpu.make_async_copy(src, dst, local_sem.at[k])
+        for k, (src, dst) in enumerate(locals_)
+    ]
+    for copy in locals_:
+        copy.start()
+    mine = block(0, 0, 0, c)
+    for d in range(1, NZ):
+        send(w_ref, mine, plane_sem.at[d, 0, 0], device(shift_z(d), y, x, c))
+
+    def spread(src, dst, dz):
+        for d in range(1, nx):
+            send(src, dst, plane_sem.at[dz, 0, d], device(z, y, shift_x(d), c))
+        for d in range(1, ny):
+            send(src, dst, plane_sem.at[dz, d, 0], device(z, shift_y(d), x, c))
+        send(src, dst, core_sem.at[dz, 0, 0], device(z, y, x, other))
+
+    spread(w_ref, mine, 0)
+    for d in range(1, nx):
+        send(rows_ref, rows_all.at[back(d), 0], rows_sem.at[back(d), 0], to(0, d, 0))
+    send(rows_ref, rows_all.at[0, 1], rows_sem.at[0, 1], to(0, 0, 1))
+    for a, b, e in around(grid, ZP):
+        mirror = ((ZP - a) % ZP, back(b), e)
+        send(ints_ref, ints_all.at[mirror], ints_sem.at[mirror], to(a, b, e))
+
+    for d in range(1, NZ):
+        here = block(d, 0, 0, c)
+        arrived(here, plane_sem.at[d, 0, 0])
+        spread(here, here, d)
+        if d == 1:
+            for a in range(1, ZP):
+                send(cot_ref, cot_all.at[ZP - a, 0, 0], cot_sem.at[ZP - a, 0, 0, 0], to(a, 0, 0))
+            for b in range(1, nx):
+                send(cot_ref, cot_all.at[0, back(b), 0], cot_sem.at[0, back(b), 0, 0], to(0, b, 0))
+            send(cot_ref, cot_all.at[0, 0, 1], cot_sem.at[0, 0, 1, 0], to(0, 0, 1))
+    for dz in range(NZ):
+        for dx in range(1, nx):
+            here = block(dz, 0, dx, c)
+            arrived(here, plane_sem.at[dz, 0, dx])
+            for d in range(1, ny):
+                send(here, here, plane_sem.at[dz, d, dx], device(z, shift_y(d), x, c))
+            send(here, here, core_sem.at[dz, 0, dx], device(z, y, x, other))
+    for d in range(1, nx):
+        here = rows_all.at[d, 0]
+        arrived(here, rows_sem.at[d, 0])
+        send(here, rows_all.at[d, 1], rows_sem.at[d, 1], to(0, 0, 1))
+    width = cot_ref.shape[1]
+    halves = [
+        (slice(None), pl.ds(0, width // 2)),
+        (slice(None), pl.ds(width // 2, width // 2)),
+    ]
+    for a in range(1, ZP):
+        here = cot_all.at[a, 0, 0]
+        arrived(here, cot_sem.at[a, 0, 0, 0])
+        for b in range(1, nx):
+            send(here.at[halves[0]], cot_all.at[a, back(b), 0].at[halves[0]], cot_sem.at[a, back(b), 0, 0], to(0, b, 0))
+        send(here, cot_all.at[a, 0, 1], cot_sem.at[a, 0, 1, 0], to(0, 0, 1))
+    for b in range(1, nx):
+        here = cot_all.at[0, b, 0]
+        arrived(here, cot_sem.at[0, b, 0, 0])
+        for a in range(1, ZP):
+            send(here.at[halves[1]], cot_all.at[ZP - a, b, 0].at[halves[1]], cot_sem.at[ZP - a, b, 0, 1], to(a, 0, 0))
+        send(here, cot_all.at[0, b, 1], cot_sem.at[0, b, 1, 0], to(0, 0, 1))
+    for dz in range(NZ):
+        for dy in range(1, ny):
+            for dx in range(nx):
+                here = block(dz, dy, dx, c)
+                arrived(here, plane_sem.at[dz, dy, dx])
+                send(here, here, core_sem.at[dz, dy, dx], device(z, y, x, other))
+    for a in range(1, ZP):
+        for b in range(1, nx):
+            here = cot_all.at[a, b, 0]
+            for part in range(2):
+                arrived(here.at[halves[part]], cot_sem.at[a, b, 0, part])
+            send(here, cot_all.at[a, b, 1], cot_sem.at[a, b, 1, 0], to(0, 0, 1))
+    for dx in range(nx):
+        arrived(rows_all.at[dx, 1], rows_sem.at[dx, 1])
+        for a in range(ZP):
+            arrived(cot_all.at[a, dx, 1], cot_sem.at[a, dx, 1, 0])
+    for a, b, e in around(grid, ZP):
+        arrived(ints_all.at[a, b, e], ints_sem.at[a, b, e])
+    for dz in range(NZ):
+        for dy in range(ny):
+            for dx in range(nx):
+                arrived(block(dz, dy, dx, other), core_sem.at[dz, dy, dx])
+    for copy in locals_:
+        copy.wait()
+    send.finish()
+
+
+def gather_first(grid_of, w, rows, cot, ints):
+    grid = grid_of()
+    nx, ny = grid.nx, grid.ny
+    places = NZ * ny * nx * NC
+    octet = ZP * nx * NC
+    sends = (NZ - 1) + NZ * (nx + ny) + 2 * nx + octet * 4 + NZ * nx * ny * (ny + 1)
+    anywhere = pl.BlockSpec(memory_space=pl.ANY)
+    dma = pltpu.SemaphoreType.DMA
+    return pl.pallas_call(
+        functools.partial(gather_kernel, grid_of),
+        out_shape=(
+            jax.ShapeDtypeStruct((places,) + w.shape, w.dtype),
+            jax.ShapeDtypeStruct((nx, NC) + rows.shape, rows.dtype),
+            jax.ShapeDtypeStruct((ZP, nx, NC) + cot.shape, cot.dtype),
+            jax.ShapeDtypeStruct((ZP, nx, NC) + ints.shape, ints.dtype),
+        ),
+        in_specs=[anywhere] * 4,
+        out_specs=(anywhere,) * 4,
+        scratch_shapes=[
+            dma((NZ, ny, nx)),
+            dma((NZ, ny, nx)),
+            dma((nx, NC)),
+            dma((ZP, nx, NC, 2)),
+            dma((ZP, nx, NC)),
+            dma((sends,)),
+            dma((4,)),
+        ],
+        compiler_params=pltpu.CompilerParams(collective_id=0, has_side_effects=True),
+    )(w, rows, cot, ints)
 
 
 def exchange_kernel(grid_of, zp, cut, count, *refs):
@@ -430,20 +417,23 @@
             )
 
 
-def sum_kernel(grid_of, zp, cut, small, parts, *refs):
+def sum_kernel(grid_of, zp, cut, small, jobs, parts, *refs):
     grid = grid_of()
     nx = grid.nx
     if small:
-        pieces, out, pieces_out = refs[:3]
-        refs = refs[3:]
-    else:
-        out = refs[0]
-        refs = refs[1:]
+        pieces, refs = refs[0], refs[1:]
+    job_ins, refs = refs[: len(jobs)], refs[len(jobs) :]
+    out, refs = refs[0], refs[1:]
+    if small:
+        pieces_out, refs = refs[0], refs[1:]
+    job_outs, refs = refs[: len(jobs)], refs[len(jobs) :]
+    refs, (job_send, job_recv) = refs[:-2], refs[-2:]
+    each = functools.partial(each_job, grid, jobs, job_ins, job_outs, job_send, job_recv)
     own, got_c, turn_x, turn_p, got_p, got_x = refs[:6]
     local_sem, c_sem, turn_sem, p_sem, x_sem, small_sem, send_sem = refs[6:]
     send = Sender(send_sem)
     to = functools.partial(stepped, grid, zp)
-    greet([to(*s) for s in around(grid, zp)])
+    greet([to(*s) for s in around(grid, zp)] + job_targets(grid, jobs))
     width = parts.shape[-1]
     h0, h1 = pl.ds(0, cut), pl.ds(cut, width - cut)
     order = (
@@ -469,6 +459,7 @@
         pltpu.make_async_copy(
             pieces.at[0, 0, 0], pieces_out.at[0, 0, 0], small_sem.at[0, 0, 0]
         ).start()
+    each(lambda copy: copy.start())
     rows = 32
 
     def ready(a, b):
@@ -510,10 +501,11 @@
         for a, b, e in [(0, 0, 0)] + around(grid, zp):
             arrived(pieces_out.at[a, b, e], small_sem.at[a, b, e])
     result.wait()
+    each(lambda copy: copy.wait())
     send.finish()
 
 
-def sum_around(grid_of, zp, number, parts, pieces=None):
+def sum_around(grid_of, zp, number, parts, pieces=None, jobs=(), job_arrays=()):
     grid = grid_of()
     nx = grid.nx
     payloads, rows, width = parts.shape[0], parts.shape[-2], parts.shape[-1]
@@ -526,13 +518,16 @@
     if small:
         out_shape.append(jax.ShapeDtypeStruct(pieces.shape, pieces.dtype))
         args.append(pieces)
+    plain = len(out_shape)
+    out_shape += job_shapes(grid, jobs, job_arrays)
+    args += list(job_arrays)
     turns = (max(zp - 1, 1), max(nx - 1, 1))
     vmem = lambda shape: pltpu.VMEM(shape, parts.dtype)
     made = pl.pallas_call(
-        functools.partial(sum_kernel, grid_of, zp, cut, small),
+        functools.partial(sum_kernel, grid_of, zp, cut, small, jobs),
         out_shape=tuple(out_shape),
         in_specs=[anywhere] * len(args),
-        out_specs=(anywhere,) * len(args),
+        out_specs=(anywhere,) * len(out_shape),
         scratch_shapes=[
             vmem((payloads, zp, nx, rows, width)),
             vmem((payloads, zp, nx, rows, width)),
@@ -547,54 +542,517 @@
             dma((turns[1],)),
             dma((zp, nx, NC)),
             dma((zp * nx * 6 + 8,)),
-        ],
+        ]
+        + job_sems(grid, jobs),
         compiler_params=pltpu.CompilerParams(
             collective_id=number,
             has_side_effects=True,
             vmem_limit_bytes=56 * 2**20,
         ),
     )(*args)
-    return made if small else made[0]
+    return made[:plain], made[plain:]
+
+
+def attention_kernel(q_ref, k_ref, v_ref, bias_ref, out_ref):
+    scores = times_transposed(q_ref[...], k_ref[...]) * HD ** (-0.5) + bias_ref[...]
+    weights = jnp.exp(scores - jnp.max(scores, axis=1, keepdims=True))
+    probs = weights * (1.0 / jnp.sum(weights, axis=1, keepdims=True))
+    out_ref[...] = times(probs.astype(bf16), v_ref[...]).astype(bf16)
+
+
+def attention_forward(queries, keys, values, bias):
+    rows, width = queries.shape
+    length = keys.shape[0]
+    by_head = lambda n: pl.BlockSpec((n, HD), lambda h: (0, h))
+    return pl.pallas_call(
+        attention_kernel,
+        grid=(width // HD,),
+        out_shape=jax.ShapeDtypeStruct((rows, width), bf16),
+        in_specs=[
+            by_head(rows),
+            by_head(length),
+            by_head(length),
+            pl.BlockSpec((rows, length), lambda h: (0, 0)),
+        ],
+        out_specs=by_head(rows),
+        compiler_params=pltpu.CompilerParams(vmem_limit_bytes=40 * 2**20),
+        cost_estimate=pl.CostEstimate(
+            flops=4 * rows * length * width,
+            bytes_accessed=4 * (rows + length) * width + 4 * rows * length,
+            transcendentals=rows * length * width // HD,
+        ),
+    )(queries, keys, values, bias)
+
+
+def attention_back_kernel(grid_of, jobs, q_ref, k_ref, v_ref, g_ref, bias_ref, *refs):
+    grid = grid_of()
+    count = len(jobs)
+    dq_ref, parts_ref = refs[count : count + 2]
+    job_send, job_recv = refs[-2:]
+    each = functools.partial(
+        each_job, grid, jobs, refs[:count], refs[count + 2 : -2], job_send, job_recv
+    )
+    if jobs:
+
+        @pl.when(pl.program_id(0) == 0)
+        def _():
+            greet(job_targets(grid, jobs))
+            each(lambda copy: copy.start())
+
+    q, k, g = q_ref[...], k_ref[...], g_ref[...]
+    scores = times_transposed(k, q) * HD ** (-0.5) + bias_ref[...]
+    weights = jnp.exp(scores - jnp.max(scores, axis=0, keepdims=True))
+    probs = weights * (1.0 / jnp.sum(weights, axis=0, keepdims=True))
+    prob_grad = times_transposed(v_ref[...], g)
+    centre = jnp.sum(probs * prob_grad, axis=0, keepdims=True)
+    score_grad = (probs * (prob_grad - centre)).astype(bf16)
+    parts_ref[0] = times(probs.astype(bf16), g).astype(bf16)
+    parts_ref[1] = (times(score_grad, q) * HD ** (-0.5)).astype(bf16)
+    dq_ref[...] = (contract_rows(score_grad, k) * HD ** (-0.5)).astype(bf16)
+    if jobs:
+
+        @pl.when(pl.program_id(0) == pl.num_programs(0) - 1)
+        def _():
+            each(lambda copy: copy.wait())
+
+
+def attention_backward(grid_of, number, queries, keys, values, grads, bias, jobs, job_arrays):
+    grid = grid_of()
+    rows, width = queries.shape
+    length = keys.shape[0]
+    by_head = lambda n: pl.BlockSpec((n, HD), lambda h: (0, h))
+    anywhere = pl.BlockSpec(memory_space=pl.ANY)
+    made = pl.pallas_call(
+        functools.partial(attention_back_kernel, grid_of, jobs),
+        grid=(width // HD,),
+        out_shape=tuple(
+            [
+                jax.ShapeDtypeStruct((rows, width), bf16),
+                jax.ShapeDtypeStruct((2, length, width), bf16),
+            ]
+            + job_shapes(grid, jobs, job_arrays)
+        ),
+        in_specs=[
+            by_head(rows),
+            by_head(length),
+            by_head(length),
+            by_head(rows),
+            pl.BlockSpec((length, rows), lambda h: (0, 0)),
+        ]
+        + [anywhere] * len(jobs),
+        out_specs=(by_head(rows), pl.BlockSpec((2, length, HD), lambda h: (0, 0, h)))
+        + (anywhere,) * len(jobs),
+        scratch_shapes=job_sems(grid, jobs),
+        compiler_params=pltpu.CompilerParams(
+            vmem_limit_bytes=40 * 2**20,
+            **(dict(collective_id=number, has_side_effects=True) if jobs else {}),
+        ),
+        cost_estimate=pl.CostEstimate(
+            flops=10 * rows * length * width,
+            bytes_accessed=6 * rows * width + 8 * length * width + 4 * rows * length,
+            transcendentals=rows * length * width // HD,
+        ),
+    )(queries, keys, values, grads, bias, *job_arrays)
+    return made[0], made[1], made[2:]
+
+
+ROW_SOURCES = 2
+
+
+def expert_kernel(grid_of, capacity, steps, jobs, carry, *refs):
+    grid = grid_of()
+    count = len(jobs)
+    take = lambda n: (refs[:n], refs[n:])
+    (rows_ref, cot_ref, rank_row_ref, rank_col_ref, gate_ref, wg_ref, wu_ref, wd_ref), refs = take(8)
+    before, refs = take(1 if carry else 0)
+    job_ins, refs = take(count)
+    (parts_ref, prob_ref, dg_ref, du_ref, dd_ref), refs = take(5)
+    job_outs, refs = take(count)
+    (x_keep, s_keep, c_keep, h_keep, ag_keep, au_keep, ht_keep), refs = take(7)
+    each = functools.partial(each_job, grid, jobs, job_ins, job_outs, *refs)
+    step = pl.program_id(0)
+    width, hidden = x_keep.shape[1], h_keep.shape[1]
+    tokens = rows_ref.shape[1]
+    size = ROW_SOURCES * capacity
+    strip = 256
+    if jobs:
+
+        @pl.when(step == 0)
+        def _():
+            greet(job_targets(grid, jobs))
+            each(lambda copy: copy.start())
+
+    @pl.when(step < steps)
+    def _():
+        at = pl.ds(pl.multiple_of(step * size, 32), size)
+        picks, columns, gates = [], [], []
+        for s in range(ROW_SOURCES):
+            slots = lax.broadcasted_iota(jnp.int32, (capacity, tokens), 0)
+            hit = slots == rank_row_ref[s]
+            gate = jnp.sum(jnp.where(hit, gate_ref[s], 0.0), axis=1, keepdims=True)
+            pick = hit.astype(f32).astype(bf16)
+            picks.append(hit)
+            gates.append(gate)
+            across = lax.broadcasted_iota(jnp.int32, (tokens, capacity), 1)
+            columns.append((across == rank_col_ref[s]).astype(f32).astype(bf16))
+            to = pl.ds(pl.multiple_of(step * size + s * capacity, 16), capacity)
+            x_keep[to] = times(pick, rows_ref[s]).astype(bf16)
+            cot = times(pick, cot_ref[s])
+            c_keep[pl.ds(s * capacity, capacity)] = cot.astype(bf16)
+            s_keep[to] = (gate * cot).astype(bf16)
+        x, slot = x_keep[at], s_keep[at]
+        for low in range(0, hidden, strip):
+            cut = slice(low, min(low + strip, hidden))
+            gate_act = times(x, wg_ref[0, :, cut])
+            up_act = times(x, wu_ref[0, :, cut])
+            hidden_grad = times_transposed(slot, wd_ref[0, cut])
+            activated, slope = silu_parts(gate_act)
+            h_keep[at, cut] = (activated * up_act).astype(bf16)
+            ag_keep[at, cut] = (hidden_grad * up_act * slope).astype(bf16)
+            au_keep[at, cut] = (hidden_grad * activated).astype(bf16)
+        h, ag, au = h_keep[at], ag_keep[at], au_keep[at]
+        probs = jnp.zeros((size, 1), f32)
+        for low in range(0, width, strip):
+            cut = slice(low, low + strip)
+            made = times(h, wd_ref[0, :, cut]).astype(bf16).astype(f32)
+            probs += jnp.sum(made * c_keep[:, cut].astype(f32), axis=1, keepdims=True)
+            back = (
+                times_transposed(ag, wg_ref[0, cut]) + times_transposed(au, wu_ref[0, cut])
+            ).astype(bf16)
+            for s in range(ROW_SOURCES):
+                mine = slice(s * capacity, (s + 1) * capacity)
+                row = times(columns[s], back[mine])
+                out = times(columns[s], (gates[s] * made[mine]).astype(bf16))
+                if carry:
+                    row += before[0][0, s, :, cut].astype(f32)
+                    out += before[0][1, s, :, cut].astype(f32)
+                parts_ref[0, s, :, cut] = row.astype(bf16)
+                parts_ref[1, s, :, cut] = out.astype(bf16)
+        for s in range(ROW_SOURCES):
+            mine = slice(s * capacity, (s + 1) * capacity)
+            prob_ref[s] = jnp.sum(
+                jnp.where(picks[s], probs[mine], 0.0), axis=0, keepdims=True
+            )
+
+    @pl.when(step == steps)
+    def _():
+        ht_keep[...] = h_keep[...].T
+
+    @pl.when(step >= steps)
+    def _():
+        cut = pl.ds(pl.multiple_of((step - steps) * strip, strip), strip)
+        turned = x_keep[:, cut].T
+        dg_ref[...] = times(turned, ag_keep[...]).astype(bf16)
+        du_ref[...] = times(turned, au_keep[...]).astype(bf16)
+        dd_ref[...] = times(ht_keep[...], s_keep[:, cut]).astype(bf16)
+
+    if jobs:
+
+        @pl.when(step == pl.num_programs(0) - 1)
+        def _():
+            each(lambda copy: copy.wait())
+
+
+def run_expert(grid_of, number, expert, rows, cot, ranks, gates, weights, capacity, before, jobs, job_arrays):
+    grid = grid_of()
+    sources, tokens = ranks.shape
+    width, hidden = weights[0].shape[1:]
+    mine = weights[0].shape[0] // ZP
+    steps = sources // ROW_SOURCES
+    strip = 256
+    strips = width // strip
+    total = sources * capacity
+    turn = lambda s: jnp.minimum(s, steps - 1)
+    later = lambda s: jnp.maximum(s - steps, 0)
+    block = pl.BlockSpec
+    by_source = lambda *rest: block(
+        (ROW_SOURCES,) + rest, lambda s: (turn(s),) + (0,) * len(rest)
+    )
+    held = lambda *rest: block(
+        (1,) + rest,
+        lambda s: (lax.axis_index("wide") // grid.ny % ZP * mine + expert, 0, 0),
+    )
+    parts = block((2, ROW_SOURCES, tokens, width), lambda s: (0, turn(s), 0, 0))
+    anywhere = block(memory_space=pl.ANY)
+    carry = before is not None
+    made = pl.pallas_call(
+        functools.partial(expert_kernel, grid_of, capacity, steps, jobs, carry),
+        grid=(steps + strips,),
+        in_specs=[
+            by_source(tokens, width),
+            by_source(tokens, width),
+            by_source(1, tokens),
+            by_source(tokens, 1),
+            by_source(1, tokens),
+            held(width, hidden),
+            held(width, hidden),
+            held(hidden, width),
+        ]
+        + [parts] * carry
+        + [anywhere] * len(jobs),
+        out_specs=[
+            parts,
+            by_source(1, tokens),
+            block((strip, hidden), lambda s: (later(s), 0)),
+            block((strip, hidden), lambda s: (later(s), 0)),
+            block((hidden, strip), lambda s: (0, later(s))),
+        ]
+        + [anywhere] * len(jobs),
+        scratch_shapes=[
+            pltpu.VMEM((total, width), bf16),
+            pltpu.VMEM((total, width), bf16),
+            pltpu.VMEM((ROW_SOURCES * capacity, width), bf16),
+            pltpu.VMEM((total, hidden), bf16),
+            pltpu.VMEM((total, hidden), bf16),
+            pltpu.VMEM((total, hidden), bf16),
+            pltpu.VMEM((hidden, total), bf16),
+        ]
+        + job_sems(grid, jobs),
+        out_shape=[
+            jax.ShapeDtypeStruct((2, sources, tokens, width), bf16),
+            jax.ShapeDtypeStruct((sources, 1, tokens), f32),
+            jax.ShapeDtypeStruct((width, hidden), bf16),
+            jax.ShapeDtypeStruct((width, hidden), bf16),
+            jax.ShapeDtypeStruct((hidden, width), bf16),
+        ]
+        + job_shapes(grid, jobs, job_arrays),
+        compiler_params=pltpu.CompilerParams(
+            vmem_limit_bytes=58 * 2**20,
+            **(dict(collective_id=number, has_side_effects=True) if jobs else {}),
+        ),
+        cost_estimate=pl.CostEstimate(
+            flops=total * width * hidden * 18,
+            bytes_accessed=width * hidden * 12 + 16 * sources * tokens * width,
+            transcendentals=total * hidden,
+        ),
+    )(
+        rows,
+        cot,
+        ranks[:, None, :],
+        ranks[:, :, None],
+        gates[:, None, :],
+        *weights,
+        *([before] if carry else []),
+        *job_arrays,
+    )
+    return made[:5], made[5:]
+
+
+def jobs_count(grid, jobs):
+    return sum({"y": grid.ny, "z": NZ}[axis] - 1 for axis in jobs)
+
+
+def job_targets(grid, jobs):
+    axes = set(jobs)
+    place = lambda z, y: (z * grid.ny + y, grid.x * NC + grid.c)
+    made = []
+    if "y" in axes:
+        made += [place(grid.z, (grid.y + d) % grid.ny) for d in range(1, grid.ny)]
+    if "z" in axes:
+        made += [place((grid.z + d) % NZ, grid.y) for d in range(1, NZ)]
+    return made
+
+
+def each_job(grid, jobs, ins, outs, send_sem, recv_sem, act):
+    at = 0
+    for axis, src, out in zip(jobs, ins, outs):
+        for d in range(1, {"y": grid.ny, "z": NZ}[axis]):
+            if axis == "y":
+                to = (grid.y + d) % grid.ny
+                piece, target = src.at[:, to], (grid.z * grid.ny + to)
+            else:
+                to = (grid.z + d) % NZ
+                piece, target = src.at[to], (to * grid.ny + grid.y)
+            act(
+                pltpu.make_async_remote_copy(
+                    src_ref=piece,
+                    dst_ref=out.at[d - 1],
+                    send_sem=send_sem.at[at],
+                    recv_sem=recv_sem.at[at],
+                    device_id=(target, grid.x * NC + grid.c),
+                    device_id_type=pl.DeviceIdType.MESH,
+                )
+            )
+            at += 1
+
+
+def job_shapes(grid, jobs, arrays):
+    made = []
+    for axis, v in zip(jobs, arrays):
+        shape = (grid.ny - 1, NZ) + v.shape[2:] if axis == "y" else (NZ - 1,) + v.shape[1:]
+        made.append(jax.ShapeDtypeStruct(shape, v.dtype))
+    return made
+
+
+def job_sems(grid, jobs):
+    count = max(jobs_count(grid, jobs), 1)
+    return [pltpu.SemaphoreType.DMA((count,)), pltpu.SemaphoreType.DMA((count,))]
+
+
+def dense_kernel(grid_of, orders, jobs, *refs):
+    grid = grid_of()
+    z, y, x, c, nx, ny = grid.z, grid.y, grid.x, grid.c, grid.nx, grid.ny
+    count, more = len(orders), len(jobs)
+    take = lambda n: (refs[:n], refs[n:])
+    ins, refs = take(count)
+    job_ins, refs = take(more)
+    outs, refs = take(count)
+    job_outs, refs = take(more)
+    held, refs = take(count)
+    got_c, refs = take(count)
+    got_one, refs = take(count)
+    got_two, refs = take(count)
+    got_z, refs = take(count)
+    local_sem, c_sem, one_sem, two_sem, z_sem, out_sem, send_sem, job_send, job_recv = refs
+    device = lambda tz, ty, tx, tc: (tz * ny + ty, tx * NC + tc)
+    other = (c + 1) % NC
+    greet(
+        [device(z, y, x, other)]
+        + [device(z, y, (x + d) % nx, c) for d in range(1, nx)]
+        + [device(z, (y + d) % ny, x, c) for d in range(1, ny)]
+        + [device((z + d) % NZ, y, x, c) for d in range(1, NZ)]
+    )
+    send = Sender(send_sem)
+    loads = []
+    for k in range(count):
+        send(ins[k].at[:, :, :, other], got_c[k], c_sem.at[k], device(z, y, x, other))
+        load = pltpu.make_async_copy(ins[k].at[:, :, :, c], held[k], local_sem.at[k])
+        load.start()
+        loads.append(load)
+    each_job(grid, jobs, job_ins, job_outs, job_send, job_recv, lambda copy: copy.start())
+
+    def add(dst, src):
+        lead = dst.shape[:-2]
+        total = 1
+        for n in lead:
+            total *= n
+
+        @pl.loop(0, total)
+        def _(i):
+            index = []
+            for n in reversed(lead):
+                index.insert(0, i % n)
+                i = i // n
+            index = tuple(index)
+            dst[index] = (dst[index].astype(f32) + src[index].astype(f32)).astype(dst.dtype)
+
+    def first(k):
+        loads[k].wait()
+        arrived(got_c[k], c_sem.at[k])
+        add(held[k], got_c[k])
+        if orders[k] == "xy":
+            for d in range(1, nx):
+                to = (x + d) % nx
+                send(held[k].at[:, :, to], got_one[k].at[d - 1], one_sem.at[k, d - 1], device(z, y, to, c))
+        else:
+            for d in range(1, ny):
+                to = (y + d) % ny
+                send(held[k].at[:, to], got_one[k].at[d - 1], one_sem.at[k, d - 1], device(z, to, x, c))
+
+    def second(k):
+        mine = held[k].at[:, :, x] if orders[k] == "xy" else held[k].at[:, y]
+        for d in range(1, nx if orders[k] == "xy" else ny):
+            arrived(got_one[k].at[d - 1], one_sem.at[k, d - 1])
+            add(mine, got_one[k].at[d - 1])
+        if orders[k] == "xy":
+            for d in range(1, ny):
+                to = (y + d) % ny
+                send(held[k].at[:, to, x], got_two[k].at[d - 1], two_sem.at[k, d - 1], device(z, to, x, c))
+        else:
+            for d in range(1, nx):
+                to = (x + d) % nx
+                send(held[k].at[:, y, to], got_two[k].at[d - 1], two_sem.at[k, d - 1], device(z, y, to, c))
+
+    results = []
+
+    def third(k):
+        mine = held[k].at[:, y, x]
+        for d in range(1, ny if orders[k] == "xy" else nx):
+            arrived(got_two[k].at[d - 1], two_sem.at[k, d - 1])
+            add(mine, got_two[k].at[d - 1])
+        near = z // ZP * ZP + (z + 1) % ZP
+        for n in range(NZ // ZP):
+            to = (z + 1) % ZP + n * ZP
+            send(held[k].at[to, y, x], got_z[k].at[n], z_sem.at[k, n], device(near, y, x, c))
+
+    def fourth(k):
+        for n in range(NZ // ZP):
+            arrived(got_z[k].at[n], z_sem.at[k, n])
+            at = (z % ZP + n * ZP, y, x)
+            held[k][at] = (held[k][at].astype(f32) + got_z[k][n].astype(f32)).astype(held[k].dtype)
+        for n in range(1, NZ // ZP):
+            to = (z + n * ZP) % NZ
+            send(held[k].at[to, y, x], outs[k].at[n], z_sem.at[k, NZ // ZP + n - 1], device(to, y, x, c))
+        result = pltpu.make_async_copy(held[k].at[z, y, x], outs[k].at[0], out_sem.at[k])
+        result.start()
+        results.append(result)
+
+    for t in range(count + 6):
+        for stage, late in ((first, 0), (second, 2), (third, 4), (fourth, 6)):
+            if 0 <= t - late < count:
+                stage(t - late)
+    for k in range(count):
+        for n in range(1, NZ // ZP):
+            arrived(outs[k].at[n], z_sem.at[k, NZ // ZP + n - 1])
+        results[k].wait()
+    each_job(grid, jobs, job_ins, job_outs, job_send, job_recv, lambda copy: copy.wait())
+    send.finish()
+
+
+def reduce_dense(grid_of, number, arrays, orders, jobs, job_arrays):
+    grid = grid_of()
+    nx, ny = grid.nx, grid.ny
+    count = len(arrays)
+    anywhere = pl.BlockSpec(memory_space=pl.ANY)
+    dma = pltpu.SemaphoreType.DMA
+    block = [v.shape[4:] for v in arrays]
+    kind = [v.dtype for v in arrays]
+    far = max(nx, ny)
+    held = [pltpu.VMEM((NZ, ny, nx) + b, t) for b, t in zip(block, kind)]
+    one = [
+        pltpu.VMEM((nx - 1, NZ, ny) + b if o == "xy" else (ny - 1, NZ, nx) + b, t)
+        for b, t, o in zip(block, kind, orders)
+    ]
+    two = [
+        pltpu.VMEM(((ny if o == "xy" else nx) - 1, NZ) + b, t)
+        for b, t, o in zip(block, kind, orders)
+    ]
+    made = pl.pallas_call(
+        functools.partial(dense_kernel, grid_of, orders, jobs),
+        out_shape=tuple(
+            [jax.ShapeDtypeStruct((NZ // ZP,) + b, t) for b, t in zip(block, kind)]
+            + job_shapes(grid, jobs, job_arrays)
+        ),
+        in_specs=[anywhere] * (count + len(jobs)),
+        out_specs=(anywhere,) * (count + len(jobs)),
+        scratch_shapes=held
+        + held
+        + one
+        + two
+        + [pltpu.VMEM((NZ // ZP,) + b, t) for b, t in zip(block, kind)]
+        + [
+            dma((count,)),
+            dma((count,)),
+            dma((count, far)),
+            dma((count, far)),
+            dma((count, NZ - 1)),
+            dma((count,)),
+            dma((count * (1 + nx + ny + NZ),)),
+        ]
+        + job_sems(grid, jobs),
+        compiler_params=pltpu.CompilerParams(
+            collective_id=number,
+            has_side_effects=True,
+            vmem_limit_bytes=60 * 2**20,
+        ),
+    )(*arrays, *job_arrays)
+    return made[:count], made[count:]
 
 
 def attention_bias(segment, labels_all, query_places, key_places):
     same_doc = segment[:, None] == labels_all[None, :]
     allowed = same_doc & (query_places[:, None] >= key_places[None, :])
     return jnp.where(allowed, 0.0, masked_value).astype(f32)
-
-
-def make_probs(query_heads, key_heads, bias):
-    scores = (
-        jnp.einsum("qhd,khd->hqk", query_heads, key_heads, preferred_element_type=f32)
-        * HD ** (-0.5)
-    )
-    scores = scores + bias[None]
-    largest = jnp.max(scores, axis=-1, keepdims=True)
-    weights = jnp.exp(scores - largest)
-    return weights * (1.0 / jnp.sum(weights, axis=-1, keepdims=True))
-
-
-def reduce_dense(grid, value, order):
-    names = ["z", "y", "x", "c"]
-    for axis in order:
-        at = names.index(axis)
-        value = grid.scatter_absolute(value, axis, at)
-        names.pop(at)
-    return value
-
-
-def reduce_experts(grid, value):
-    mine, rows, columns = value.shape
-    value = value.reshape(mine, NZ, grid.ny, rows // (NZ * grid.ny), columns)
-    value = grid.scatter_absolute(value, "y", 2)
-    take = lambda i: lax.dynamic_index_in_dim(value, i, 1, keepdims=False)
-    sums = [take(grid.z).astype(f32), None]
-    for d in range(1, NZ):
-        got = grid.send(take((grid.z + d) % NZ), "z", d).astype(f32)
-        sums[d % ZP] = got if sums[d % ZP] is None else sums[d % ZP] + got
-    first = jnp.where(grid.zm == 0, sums[0], sums[1])
-    second = jnp.where(grid.zm == 0, sums[1], sums[0])
-    return jnp.concatenate([first, second], axis=0)
 
 
 def body(
@@ -645,11 +1103,10 @@
         axis=1,
     )
     integers = jnp.concatenate([routes.T, segment[None, :]], axis=0)
-    bundle_all, group_rows, integers_all = gather_first(
-        grid_of, bundle, activations, integers
-    )
-    group_rows = group_rows.at[0, 0].set(activations).reshape(-1, width)
-    integers_all = integers_all.at[0, 0, 0].set(integers)
+    bundle_all, group_rows, cot_all, integers_all = gather_first(
+        grid_of, bundle, activations, cotangent, integers
+    )
+    group_rows = group_rows.reshape(-1, width)
     integers_all = integers_all.reshape(sources, top_count + 1, tok_rows)
     bundle_all = bundle_all.reshape(width, bundle.shape[1])
     w_query, w_key, w_value, w_out = (
@@ -681,22 +1138,12 @@
     key_places = (block_places[:, None] * tok_rows + steps[None, :]).reshape(-1)
     query_places = (grid.x * NC + grid.c) * tok_rows + steps
     bias = attention_bias(segment, labels_all, query_places, key_places)
-    query_heads = queries.reshape(-1, heads, HD)
-    key_heads = keys_all.reshape(-1, heads, HD)
-    value_heads = values_all.reshape(-1, heads, HD)
-    probs = make_probs(query_heads, key_heads, bias)
-    attended = (
-        jnp.einsum(
-            "hqk,khd->qhd", probs.astype(bf16), value_heads, preferred_element_type=f32
-        )
-        .reshape(tok_rows, width)
-        .astype(bf16)
-    )
+    attended = attention_forward(queries, keys_all, values_all, bias)
     middle = inputs + times(attended, w_out)
     inverse_two = norm_scale(middle)
     normed_two = (middle * inverse_two * gain_two).astype(bf16)
 
-    rows_all, cot_all = exchange(grid_of, ZP, 1, normed_two, cotangent)
+    (rows_all,) = exchange(grid_of, ZP, 1, normed_two)
     rows_all = rows_all.reshape(sources, tok_rows, width)
     cot_all = cot_all.reshape(sources, tok_rows, width)
     router_probs_all = jax.nn.softmax(
@@ -714,69 +1161,65 @@
     ranks = jnp.einsum(
         "irt,tu->iru", marks.astype(bf16), earlier, preferred_element_type=f32
     ).astype(jnp.int32)
-    slots = jnp.arange(capacity, dtype=jnp.int32)
-    chosen = marks[:, :, None, :] & (ranks[:, :, None, :] == slots[None, None, :, None])
-    picks = chosen.astype(bf16)
+    ranks = jnp.where(marks, ranks, -1)
     gates_mine = jnp.moveaxis(
         lax.dynamic_slice_in_dim(router_probs_all, first_expert, mine, axis=2), 2, 0
     )
-    gate_rows = jnp.sum(
-        jnp.where(chosen, gates_mine[:, :, None, :], 0.0), axis=-1
-    ).reshape(mine, sources * capacity, 1)
-    out_parts = 0.0
-    row_parts = 0.0
+    def by_wide(v):
+        return v.reshape(NZ, ny, v.shape[0] // wide, v.shape[1])
+
+    names = [(i, k) for i in range(mine) for k in range(3)]
+    grads, along_y, along_z = {}, {}, {}
+
+    def jobs_of(which_y, which_z):
+        tags = tuple("y" for _ in which_y) + tuple("z" for _ in which_z)
+        return tags, [grads[n] for n in which_y] + [column[n] for n in which_z]
+
+    def landed(which_y, which_z, moved):
+        along_y.update(zip(which_y, moved))
+        along_z.update(zip(which_z, moved[len(which_y) :]))
+
+    def summed(name):
+        total = lax.dynamic_index_in_dim(grads[name], grid.y, 1, keepdims=False).astype(f32)
+        for d in range(ny - 1):
+            total = total + along_y[name][d].astype(f32)
+        return total.astype(bf16)
+
+    column = {}
+    both_parts = None
     prob_parts = []
-    gate_w_grads, up_w_grads, down_w_grads = [], [], []
-    w_gates = lax.dynamic_slice_in_dim(expert_gate, grid.zm * mine, mine, axis=0)
-    w_ups = lax.dynamic_slice_in_dim(expert_up, grid.zm * mine, mine, axis=0)
-    w_downs = lax.dynamic_slice_in_dim(expert_down, grid.zm * mine, mine, axis=0)
     for i in range(mine):
-        pick = lambda v: (
-            jnp.einsum("rst,rtd->rsd", picks[i], v, preferred_element_type=f32)
-            .astype(bf16)
-            .reshape(sources * capacity, width)
+        behind = (names[3 * i - 3 : 3 * i - 1], []) if i else ([], [])
+        (both_parts, probs_here, *made), moved = run_expert(
+            grid_of,
+            5 + i,
+            i,
+            rows_all,
+            cot_all,
+            ranks[i],
+            gates_mine[i],
+            (expert_gate, expert_up, expert_down),
+            capacity,
+            both_parts,
+            *jobs_of(*behind),
         )
-        unpick = lambda v: jnp.einsum(
-            "rst,rsd->rtd",
-            picks[i],
-            v.reshape(sources, capacity, width),
-            preferred_element_type=f32,
-        )
-        rows_here = pick(rows_all)
-        cot_here = pick(cot_all).astype(f32)
-        slot_here = (gate_rows[i] * cot_here).astype(bf16)
-        gate_act = times(rows_here, w_gates[i])
-        up_act = times(rows_here, w_ups[i])
-        activated, slope = silu_parts(gate_act)
-        hidden = (activated * up_act).astype(bf16)
-        produced = times(hidden, w_downs[i]).astype(bf16).astype(f32)
-        row_probs = jnp.sum(produced * cot_here, axis=-1).reshape(sources, capacity, 1)
-        prob_parts.append(jnp.sum(jnp.where(chosen[i], row_probs, 0.0), axis=1))
-        out_parts = out_parts + unpick((gate_rows[i] * produced).astype(bf16))
-        hidden_grad = times_transposed(slot_here, w_downs[i])
-        act_gate = (hidden_grad * up_act * slope).astype(bf16)
-        act_up = (hidden_grad * activated).astype(bf16)
-        down_w_grads.append(contract_rows(hidden, slot_here).astype(bf16))
-        gate_w_grads.append(contract_rows(rows_here, act_gate).astype(bf16))
-        up_w_grads.append(contract_rows(rows_here, act_up).astype(bf16))
-        row_grad = (
-            times_transposed(act_gate, w_gates[i]) + times_transposed(act_up, w_ups[i])
-        ).astype(bf16)
-        row_parts = row_parts + unpick(row_grad)
-
-    both_parts = jnp.stack([row_parts.astype(bf16), out_parts.astype(bf16)])
-    sums, sent = sum_around(
+        landed(*behind, moved)
+        prob_parts.append(probs_here[:, 0])
+        grads.update({(i, k): by_wide(v) for k, v in enumerate(made)})
+    column.update({name: summed(name) for name in along_y})
+    behind = (names[2:4], names[:1])
+    (sums, sent), moved = sum_around(
         grid_of,
         ZP,
         2,
         both_parts.reshape(2, ZP, nx, NC, tok_rows, width),
         jnp.stack(prob_parts, axis=1).reshape(ZP, nx, NC, mine, tok_rows),
-    )
+        *jobs_of(*behind),
+    )
+    landed(*behind, moved)
+    column.update({name: summed(name) for name in behind[0]})
     routed_grad = sums[0].astype(f32)
     routed = sums[1].astype(f32)
-    expert_down_grad = reduce_experts(grid, jnp.stack(down_w_grads))
-    expert_gate_grad = reduce_experts(grid, jnp.stack(gate_w_grads))
-    expert_up_grad = reduce_experts(grid, jnp.stack(up_w_grads))
     dz = (grid.zm + jnp.arange(ZP, dtype=jnp.int32)) % ZP
     owner = block_places.reshape(1, nx, NC, 1) * local_experts
     owner = owner + dz[:, None, None, None] * mine + jnp.arange(mine, dtype=jnp.int32)
@@ -833,32 +1276,30 @@
     output_weight_grad = contract_rows(attended, branch_grad)
     attended_grad = times_transposed(branch_grad, w_out).astype(bf16)
 
-    grad_heads = attended_grad.reshape(tok_rows, heads, HD)
-    prob_grad_att = jnp.einsum(
-        "qhd,khd->hqk", grad_heads, value_heads, preferred_element_type=f32
-    )
-    centre = jnp.sum(probs * prob_grad_att, axis=-1, keepdims=True)
-    score_grad = (probs * (prob_grad_att - centre)).astype(bf16)
-    query_act_grad = (
-        (
-            jnp.einsum("hqk,khd->qhd", score_grad, key_heads, preferred_element_type=f32)
-            * HD ** (-0.5)
-        )
-        .reshape(tok_rows, width)
-        .astype(bf16)
-    )
-    key_part = (
-        jnp.einsum("hqk,qhd->khd", score_grad, query_heads, preferred_element_type=f32)
-        * HD ** (-0.5)
-    )
-    value_part = jnp.einsum(
-        "hqk,qhd->khd", probs.astype(bf16), grad_heads, preferred_element_type=f32
-    )
-
-    parts = jnp.stack([value_part.astype(bf16), key_part.astype(bf16)])
-    value_act_grad, key_act_grad = sum_around(
-        grid_of, 1, 3, parts.reshape(2, 1, nx, NC, tok_rows, width)
-    )
+    behind = (names[4:5], names[1:2])
+    query_act_grad, parts, moved = attention_backward(
+        grid_of,
+        1 + 8,
+        queries,
+        keys_all,
+        values_all,
+        attended_grad,
+        bias.T,
+        *jobs_of(*behind),
+    )
+    landed(*behind, moved)
+    behind = (names[5:], names[2:4])
+    ((value_key,), moved) = sum_around(
+        grid_of,
+        1,
+        3,
+        parts.reshape(2, 1, nx, NC, tok_rows, width),
+        None,
+        *jobs_of(*behind),
+    )
+    value_act_grad, key_act_grad = value_key
+    landed(*behind, moved)
+    column.update({name: summed(name) for name in names[4:]})
     query_w_grad = contract_rows(normed_one, query_act_grad)
     key_w_grad = contract_rows(normed_one, key_act_grad)
     value_w_grad = contract_rows(normed_one, value_act_grad)
@@ -875,16 +1316,6 @@
     def by_place(v):
         return v.reshape((NZ, ny, nx, NC, v.shape[0] // (wide * ep)) + v.shape[1:])
 
-    def reduce_all(v, order):
-        return reduce_dense(grid, by_place(v.astype(bf16)), order).astype(f32)
-
-    output_weight_sum = reduce_all(output_weight_grad, "cxyz")
-    shared_gate_sum = reduce_all(shared_gate_grad, "cyxz")
-    shared_up_sum = reduce_all(shared_up_grad, "cxyz")
-    shared_down_sum = reduce_all(shared_down_grad, "cyxz")
-    query_sum = reduce_all(query_w_grad, "cxyz")
-    key_sum = reduce_all(key_w_grad, "cyxz")
-    value_sum = reduce_all(value_w_grad, "cxyz")
     counts = jnp.sum(
         (routes[:, :, None] == jnp.arange(experts, dtype=jnp.int32)).astype(f32),
         axis=(0, 1),
@@ -906,9 +1337,53 @@
     extras = jnp.concatenate(
         [extras, count_block, jnp.zeros((wide, ep, 7, 128), f32)], axis=2
     )
-    extra_sum = reduce_dense(
-        grid, extras.reshape(NZ, ny, nx, NC, share + 8, 128), "cxyz"
-    )
+    dense = [
+        output_weight_grad,
+        shared_down_grad,
+        shared_gate_grad,
+        shared_up_grad,
+        query_w_grad,
+        key_w_grad,
+        value_w_grad,
+    ]
+    terms, moved = reduce_dense(
+        grid_of,
+        4,
+        [by_place(v.astype(bf16)) for v in dense]
+        + [extras.reshape(NZ, ny, nx, NC, share + 8, 128)],
+        ("xy", "yx", "xy", "yx", "xy", "yx", "xy", "xy"),
+        *jobs_of([], names[4:]),
+    )
+    landed([], names[4:], moved)
+    (
+        output_weight_sum,
+        shared_down_sum,
+        shared_gate_sum,
+        shared_up_sum,
+        query_sum,
+        key_sum,
+        value_sum,
+        extra_sum,
+    ) = (jnp.sum(v.astype(f32), axis=0) for v in terms)
+
+    def expert_sum(kind):
+        halves = [[], []]
+        for i in range(mine):
+            name = (i, kind)
+            same = lax.dynamic_index_in_dim(column[name], grid.z, 0, keepdims=False)
+            same = same.astype(f32)
+            far = 0.0
+            for d in range(1, NZ):
+                got = along_z[name][d - 1].astype(f32)
+                if d % ZP == 0:
+                    same = same + got
+                else:
+                    far = far + got
+            halves[0].append(jnp.where(grid.zm == 0, same, far))
+            halves[1].append(jnp.where(grid.zm == 0, far, same))
+        return jnp.stack(halves[0] + halves[1])
+
+    expert_gate_grad, expert_up_grad, expert_down_grad = (expert_sum(k) for k in range(3))
     return (
         block_out,
         input_grad,

time: 997 us -> 714 us (0.72)
  Pallas kernels: 227 us -> 526 us
  matrix products: 276 us -> 75.1 us
  waiting for transfers between devices: 183 us -> 0.7 us
  starting transfers between devices: 117 us -> 0.08 us
  local copies, waits for them, and re-layouts: 95 us -> 33.2 us
  other arithmetic: 72.5 us -> 54.4 us
    pallas_call x3 -> x8, Pallas kernels: 178 us -> 497 us  [the longest x1 127 us: reduce_dense(): pl.pallas_call(functools.partial(dense_kernel, grid_of, orders, jobs), ou...]
    ppermute x60 -> x0, waiting for transfers between devices: 183 us -> none  [send(): return lax.ppermute(value, BOTH, self.pairs(moves[axis]))]
    ppermute x60 -> x0, starting transfers between devices: 117 us -> none  [send(): return lax.ppermute(value, BOTH, self.pairs(moves[axis]))]
    dot_general x13 -> x0, matrix products: 63.9 us -> none  [the longest x4 21.4 us: body(): jnp.einsum('rst,rsd->rtd', picks[i], v.reshape(sources, capacity, width),...]
    dot_general x13 -> x7, matrix products: 72 us -> 18.4 us  [times_transposed(): lax.dot_general(left, right, (((1,), (1,)), ((), ())), preferred_element_...]
    dot_general x13 -> x7, matrix products: 82.1 us -> 30.2 us  [times(): return jnp.dot(left, right, preferred_element_type=f32)]
    dot_general x13 -> x7, matrix products: 40.7 us -> 17.5 us  [contract_rows(): lax.dot_general(left, right, (((0,), (0,)), ((), ())), preferred_element_...]
    another operation x6 -> x4, local copies, waits for them, and re-layouts: 26 us -> 3.98 us  [the longest x3 3.36 us: run_expert(): ranks[:, :, None]]
  transfers between devices with their start and end apart: 62 -> 2, of which waited for: 26 -> 0; matrix products, arithmetic and copies ran while one was open for 34% -> 10% of each run, Pallas kernels for 19% -> 46%
where the time goes in v3:
time: 714 us; the launch traced here: 705 us
  Pallas kernels  526 us (74%)
  matrix products  75.1 us (11%)
  other arithmetic  54.4 us (8%)
  local copies, waits for them, and re-layouts  33.2 us (5%)
  between operations  15.4 us (2%)
    pallas_call x1, Pallas kernels, reduce_dense(): pl.pallas_call(functools.partial(dense_kernel, grid_of, orders, jobs), ou...  127 us
    pallas_call x2, Pallas kernels, sum_around(): pl.pallas_call(functools.partial(sum_kernel, grid_of, zp, cut, small, job...  122 us
    pallas_call x2, Pallas kernels, run_expert(): pl.pallas_call(functools.partial(expert_kernel, grid_of, capacity, steps,...  106 us
    pallas_call x1, Pallas kernels, gather_first(): pl.pallas_call(functools.partial(gather_kernel, grid_of), out_shape=(jax....  104 us
    dot_general x7, matrix products, times(): return jnp.dot(left, right, preferred_element_type=f32)  30.2 us
    pallas_call x1, Pallas kernels, exchange(): pl.pallas_call(functools.partial(exchange_kernel, grid_of, zp, arrays[0]....  29.1 us
    pallas_call x1, Pallas kernels, attention_backward(): pl.pallas_call(functools.partial(attention_back_kernel, grid_of, jobs), g...  28.3 us
    dot_general x7, matrix products, times_transposed(): lax.dot_general(left, right, (((1,), (1,)), ((), ())), preferred_element_...  18.4 us
  transfers between devices with their start and end apart: 2, of which 0 were waited for; matrix products, arithmetic and copies ran while one was open for 10% of the time, Pallas kernels for 46%

profile of v3, /device:TPU:0, one launch (start us, length us, event | category | flops | bytes accessed | tf_op | source)
XLA Modules:
  0.0 704.9 jit_solution(6203382209047080064)
XLA Ops:
  15.1 104.4 %shard_map.288 = (bf16[32,40,5248]{2,1,0:T(8,128)(2,1)}, bf16[2,2,256,1280]{3,2,1,0:T(8,128)(2,1)}, bf16[2,2,2,256,1280]{4,3,2,1,0:T(8,128)(2,1)}, s32[2,2,2,8,256]{4,3,2,1,0:T(8,128)}) custom-call(bf16[40,5248]{1,0:T(8,128)(2,1)} %concatenate.22.w_ref, bf16[256,1280]{1,0:T(8,128)(2,1)} %rows_ref.1, bf16[256,1280]{1,0:T(8,128)(2,1)} %cot_ref.1, ...), custom_call_target="tpu_custom_call" | custom-call | tf_op jit(solution)/shard_map/pallas_call | solution.py:307
  124.9 6.6 convolution_convert_fusion.4.v_ref
  131.5 6.8 convolution_convert_fusion.5.k_ref
  138.3 3.8 fusion.28.q_ref
  146.1 9.0 %shard_map.289 = bf16[256,1280]{1,0:T(8,128)(2,1)S(1)} custom-call(bf16[256,1280]{1,0:T(8,128)(2,1)S(1)} %copy-done.6, bf16[1024,1280]{1,0:T(8,128)(2,1)S(1)} %copy-done, bf16[1024,1280]{1,0:T(8,128)(2,1)S(1)} %convolution_convert_fusion.4.v_ref, f32[256,1024]{1,0:T(8,128)S(1)} %and_select_fusion.1.bias_ref), custom_call_target="tpu_custom_call" | custom-call | flops 1342177280 | bytes 7602176 | tf_op jit(solution)/shard_map/pallas_call | solution.py:567
  155.2 4.0 multiply_reduce_fusion.3
  163.3 29.1 %shard_map.290 = bf16[2,2,2,256,1280]{4,3,2,1,0:T(8,128)(2,1)} custom-call(bf16[256,1280]{1,0:T(8,128)(2,1)} %multiply_convert_fusion.refs_0_), custom_call_target="tpu_custom_call" | custom-call | tf_op jit(solution)/shard_map/pallas_call | solution.py:388
  192.4 4.6 fusion.105
  202.1 46.2 %shard_map.291 = (bf16[2,8,256,1280]{3,2,1,0:T(8,128)(2,1)}, f32[8,1,256]{2,1,0:T(1,128)}, bf16[1280,896]{1,0:T(8,128)(2,1)}, bf16[1280,896]{1,0:T(8,128)(2,1)}, bf16[896,1280]{1,0:T(8,128)(2,1)}) custom-call(bf16[8,256,1280]{2,1,0:T(8,128)(2,1)} %bitcast.180, bf16[8,256,1280]{2,1,0:T(8,128)(2,1)} %bitcast.224, s32[8,1,256]{2,1,0:T(1,128)} %get-tuple-element.169.refs_2_, ...), custom_call_target="tpu_custom_call" | custom-call | flops 26424115200 | bytes 55705600 | tf_op jit(solution)/shard_map/pallas_call | solution.py:778
  248.3 59.8 %shard_map.292 = (bf16[2,8,256,1280]{3,2,1,0:T(8,128)(2,1)}, f32[8,1,256]{2,1,0:T(1,128)}, bf16[1280,896]{1,0:T(8,128)(2,1)}, bf16[1280,896]{1,0:T(8,128)(2,1)},...) custom-call(bf16[8,256,1280]{2,1,0:T(8,128)(2,1)} %bitcast.181, ...), custom_call_target="tpu_custom_call" | custom-call | flops 26424115200 | bytes 55705600 | tf_op jit(solution)/shard_map/pallas_call | solution.py:778
  312.0 73.2 %shard_map.293 = (bf16[2,256,1280]{2,1,0:T(8,128)(2,1)}, f32[2,2,2,2,256]{4,3,2,1,0:T(2,128)}, bf16[1,4,112,1280]{3,2,1,0:T(8,128)(2,1)}, bf16[1,4,160,896]{3,2,1,0:T(8,128)(2,1)}, bf16[3,160,896]{2,1,0:T(8,128)(2,1)}) custom-call(bf16[2,2,2,2,256,1280]{5,4,3,2,1,0:T(8,128)(2,1)} %bitcast.182, f32[2,2,2,2,256]{4,3,2,1,0:T(2,128)} %bitcast.214, ...), custom_call_target="tpu_custom_call" | custom-call | tf_op jit(solution)/shard_map/pallas_call | solution.py:526
  400.6 4.1 reshape.429
  418.0 3.6 fusion.31.g_ref
  422.2 28.3 %shard_map.294 = (bf16[256,1280]{1,0:T(8,128)(2,1)S(1)}, bf16[2,1024,1280]{2,1,0:T(8,128)(2,1)}, bf16[1,4,160,896]{3,2,1,0:T(8,128)(2,1)S(1)}, bf16[3,160,896]{2,1,0:T(8,128)(2,1)S(1)}) custom-call(bf16[256,1280]{1,0:T(8,128)(2,1)S(1)} %copy-done.7, bf16[1024,1280]{1,0:T(8,128)(2,1)S(1)} %copy-done.1, ...), custom_call_target="tpu_custom_call" | custom-call | flops 3355443200 | bytes 13500416 | tf_op jit(solution)/shard_map/pallas_call | solution.py:625
  451.5 48.5 %shard_map.295 = (bf16[2,256,1280]{2,1,0:T(8,128)(2,1)}, bf16[1,4,112,1280]{3,2,1,0:T(8,128)(2,1)}, bf16[3,112,1280]{2,1,0:T(8,128)(2,1)}, bf16[3,160,896]{2,1,0:T(8,128)(2,1)}) custom-call(bf16[2,1,2,2,256,1280]{5,4,3,2,1,0:T(8,128)(2,1)} %bitcast.185, bf16[4,2,112,1280]{3,2,1,0:T(8,128)(2,1)} %bitcast.190, bf16[4,112,1280]{2,1,0:T(8,128)(2,1)} %fusion.38.refs_1_, ...), custom_call_target="tpu_custom_call" | custom-call | tf_op jit(solution)/shard_map/pallas_call | solution.py:526
  500.0 3.3 fusion.10
  503.4 2.8 convolution_convert_fusion
  518.8 2.8 convolution_convert_fusion.2
  521.6 3.1 fusion.19
  524.8 4.8 fusion.54
  536.3 2.8 fusion.58
  539.1 127.4 %shard_map.296 = (bf16[2,40,1280]{2,1,0:T(8,128)(2,1)}, bf16[2,28,1280]{2,1,0:T(8,128)(2,1)}, bf16[2,40,896]{2,1,0:T(8,128)(2,1)}, bf16[2,40,896]{2,1,0:T(8,128)...) custom-call(bf16[4,2,2,2,40,1280]{5,4,3,2,1,0:T(8,128)(2,1)} %bitcas, ...), custom_call_target="tpu_custom_call" | custom-call | tf_op jit(solution)/shard_map/pallas_call | solution.py:1020
  668.5 3.5 fusion.34
  688.4 2.8 fusion.51
  (278 shorter events, 104.0 us)
Async XLA Ops:
  7.2 393.4 %all-gather.6.cloned.1.call-start = ((), (), s32[]{:S(2)}) async-start(), calls=%async_computation.1 | async-start | bytes 2703360 | tf_op jit(solution)/shard_map/all_gather | solution.py:1116
  7.9 396.7 %all-gather.4.cloned.1.call-start = ((), (), s32[]{:S(2)}) async-start(), calls=%async_computation | async-start | bytes 4730880 | tf_op jit(solution)/shard_map/all_gather | solution.py:1116
  124.9 13.4 %copy-start.14 = (bf16[1024,1280]{1,0:T(8,128)(2,1)}, bf16[1024,1280]{1,0:T(8,128)(2,1)S(1)}, u32[]{:S(2)}) copy-start(bf16[1024,1280]{1,0:T(8,128)(2,1)S(1)} %fusion.2) | copy-start | bytes 7864324
  143.0 12.2 %copy-start.64 = (s32[1,2,4,128]{3,1,2,0:T(2,128)}, s32[1,2,4,128]{3,1,2,0:T(2,128)S(1)}, u32[]{:S(2)}) copy-start(s32[1,2,4,128]{3,1,2,0:T(2,128)S(1)} %copy.142) | copy-start | bytes 12292
  143.0 12.2 %copy-start.80 = (s32[256]{0:T(256)}, s32[256]{0:T(256)S(1)}, u32[]{:S(2)}) copy-start(s32[256]{0:T(256)S(1)} %iota_add_fusion.1) | copy-start | bytes 3076
  143.0 12.2 %copy-start.66 = (s32[4,1,256]{2,1,0:T(1,128)}, s32[4,1,256]{2,1,0:T(1,128)S(1)}, u32[]{:S(2)}) copy-start(s32[4,1,256]{2,1,0:T(1,128)S(1)} %slice.173) | copy-start | bytes 12292
  146.1 9.1 %copy-start.21 = (bf16[256,1280]{1,0:T(8,128)(2,1)S(1)}, bf16[256,1280]{1,0:T(8,128)(2,1)}, u32[]{:S(2)}) copy-start(bf16[256,1280]{1,0:T(8,128)(2,1)} %rows_ref.1) | copy-start | bytes 1966084
  159.7 32.7 %copy-start.70 = (f32[256]{0:T(256)}, f32[256]{0:T(256)S(1)}, u32[]{:S(2)}) copy-start(f32[256]{0:T(256)S(1)} %get-tuple-element.174) | copy-start | bytes 3076
  248.3 59.8 %copy-start.75 = (f32[8,1,256]{2,1,0:T(1,128)S(1)}, f32[8,1,256]{2,1,0:T(1,128)}, u32[]{:S(2)}) copy-start(f32[8,1,256]{2,1,0:T(1,128)} %get-tuple-element.63) | copy-start | bytes 24580
  248.3 61.2 %copy-start.52 = (bf16[1280,896]{1,0:T(8,128)(2,1)S(1)}, bf16[1280,896]{1,0:T(8,128)(2,1)}, u32[]{:S(2)}) copy-start(bf16[1280,896]{1,0:T(8,128)(2,1)} %get-tuple-element.60) | copy-start | bytes 6881284
  312.0 74.0 %copy-start.79 = (s32[2,2]{1,0:T(2,128)S(1)}, s32[2,2]{1,0:T(2,128)}, u32[]{:S(2)}) copy-start(s32[2,2]{1,0:T(2,128)} %get-tuple-element.175) | copy-start | bytes 52
  312.0 74.2 %copy-start.69 = (s32[256,7]{0,1:T(8,128)S(1)}, s32[256,7]{0,1:T(8,128)}, u32[]{:S(2)}) copy-start(s32[256,7]{0,1:T(8,128)} %param.19) | copy-start | bytes 21508
  312.0 78.4 %copy-start.65 = (s32[1,2,4,128]{3,1,2,0:T(2,128)S(1)}, s32[1,2,4,128]{3,1,2,0:T(2,128)}, u32[]{:S(2)}) copy-start(s32[1,2,4,128]{3,1,2,0:T(2,128)} %copy-done.64) | copy-start | bytes 12292
  312.0 78.4 %copy-start.67 = (s32[4,1,256]{2,1,0:T(1,128)S(1)}, s32[4,1,256]{2,1,0:T(1,128)}, u32[]{:S(2)}) copy-start(s32[4,1,256]{2,1,0:T(1,128)} %copy-done.66) | copy-start | bytes 12292
  312.0 78.4 %copy-start.73 = (s32[256]{0:T(256)S(1)}, s32[256]{0:T(256)}, u32[]{:S(2)}) copy-start(s32[256]{0:T(256)} %param.18) | copy-start | bytes 3076
  312.0 78.4 %copy-start.81 = (s32[256]{0:T(256)S(1)}, s32[256]{0:T(256)}, u32[]{:S(2)}) copy-start(s32[256]{0:T(256)} %copy-done.80) | copy-start | bytes 3076
  387.0 6.4 copy-start.48
  524.7 6.1 copy-start.68
  524.8 7.4 %copy-start.39 = (bf16[256,896]{1,0:T(8,128)(2,1)S(1)}, bf16[256,896]{1,0:T(8,128)(2,1)}, u32[]{:S(2)}) copy-start(bf16[256,896]{1,0:T(8,128)(2,1)} %get-tuple-element.164) | copy-start | bytes 1376260
  539.1 129.4 %copy-start.10 = (f32[256,1280]{1,0:T(8,128)S(1)}, f32[256,1280]{1,0:T(8,128)}, u32[]{:S(2)}) copy-start(f32[256,1280]{1,0:T(8,128)} %get-tuple-element.178) | copy-start | bytes 3932164
  677.8 5.9 copy-start.56
  680.0 6.5 copy-start.60
  680.0 8.4 %copy-start.18 = (f32[256,1280]{1,0:T(8,128)S(1)}, f32[256,1280]{1,0:T(8,128)}, u32[]{:S(2)}) copy-start(f32[256,1280]{1,0:T(8,128)} %copy-done.16) | copy-start | bytes 3932164
  680.0 8.4 %copy-start.76 = (f32[256]{0:T(256)S(1)}, f32[256]{0:T(256)}, u32[]{:S(2)}) copy-start(f32[256]{0:T(256)} %get-tuple-element.171) | copy-start | bytes 3076
  (63 other events, 191.9 us)
Sparse Core Ops, SparseCore 0:
  10.8 83.6 all-gather.5
  98.0 62.4 all-gather.3

commit v4 on v3

--- a/solution.py
+++ b/solution.py
@@ -177,6 +177,11 @@
     ints_sem,
     send_sem,
     local_sem,
+    z_in,
+    z_out,
+    x_out,
+    y_out,
+    c_out,
 ):
     grid = grid_of()
     z, y, x, c, nx, ny = grid.z, grid.y, grid.x, grid.c, grid.nx, grid.ny
@@ -212,42 +217,74 @@
     ]
     for copy in locals_:
         copy.start()
-    mine = block(0, 0, 0, c)
-    for d in range(1, NZ):
-        send(w_ref, mine, plane_sem.at[d, 0, 0], device(shift_z(d), y, x, c))
-
-    def spread(src, dst, dz):
-        for d in range(1, nx):
-            send(src, dst, plane_sem.at[dz, 0, d], device(z, y, shift_x(d), c))
-        for d in range(1, ny):
-            send(src, dst, plane_sem.at[dz, d, 0], device(z, shift_y(d), x, c))
-        send(src, dst, core_sem.at[dz, 0, 0], device(z, y, x, other))
-
-    spread(w_ref, mine, 0)
-    for d in range(1, nx):
-        send(rows_ref, rows_all.at[back(d), 0], rows_sem.at[back(d), 0], to(0, d, 0))
-    send(rows_ref, rows_all.at[0, 1], rows_sem.at[0, 1], to(0, 0, 1))
+    def start(src, dst, out_sem, in_sem, target):
+        pltpu.make_async_remote_copy(
+            src_ref=src,
+            dst_ref=dst,
+            send_sem=out_sem,
+            recv_sem=in_sem,
+            device_id=target,
+            device_id_type=pl.DeviceIdType.MESH,
+        ).start()
+
+    def each_source(act, least=0, most=NZ - 1):
+        for d in range(least, most + 1):
+            for way in range(2):
+                there = z - d >= 0 if way == 0 else z + d <= NZ - 1
+                pl.when(there)(
+                    functools.partial(act, way, d, d if way == 0 else (NZ - d) % NZ)
+                )
+
+    def pass_on(way, d, dz):
+        here = block(dz, 0, 0, c)
+        src = here if d else w_ref
+        if d:
+            arrived(here, z_in.at[way, d])
+        if d < NZ - 1:
+
+            @pl.when(z < NZ - 1 if way == 0 else z > 0)
+            def _():
+                start(
+                    src,
+                    here,
+                    z_out.at[way, d],
+                    z_in.at[way, d + 1],
+                    device(z + 1 if way == 0 else z - 1, y, x, c),
+                )
+
+        if d or way == 0:
+            for b in range(1, nx):
+                start(src, here, x_out.at[dz, b], plane_sem.at[dz, 0, b], device(z, y, shift_x(b), c))
+            for b in range(1, ny):
+                start(src, here, y_out.at[dz, 0, b], plane_sem.at[dz, b, 0], device(z, shift_y(b), x, c))
+            start(src, here, c_out.at[dz, 0], core_sem.at[dz, 0, 0], device(z, y, x, other))
+
+    def turn(way, d, dz):
+        if d == 0 and way == 1:
+            return
+        for dx in range(1, nx):
+            here = block(dz, 0, dx, c)
+            arrived(here, plane_sem.at[dz, 0, dx])
+            for b in range(1, ny):
+                start(here, here, y_out.at[dz, dx, b], plane_sem.at[dz, b, dx], device(z, shift_y(b), x, c))
+            start(here, here, c_out.at[dz, dx], core_sem.at[dz, 0, dx], device(z, y, x, other))
+
     for a, b, e in around(grid, ZP):
         mirror = ((ZP - a) % ZP, back(b), e)
         send(ints_ref, ints_all.at[mirror], ints_sem.at[mirror], to(a, b, e))
-
+    each_source(pass_on, 0, 0)
     for d in range(1, NZ):
-        here = block(d, 0, 0, c)
-        arrived(here, plane_sem.at[d, 0, 0])
-        spread(here, here, d)
-        if d == 1:
+        each_source(pass_on, d, d)
+        if d == NZ - 1:
             for a in range(1, ZP):
                 send(cot_ref, cot_all.at[ZP - a, 0, 0], cot_sem.at[ZP - a, 0, 0, 0], to(a, 0, 0))
             for b in range(1, nx):
                 send(cot_ref, cot_all.at[0, back(b), 0], cot_sem.at[0, back(b), 0, 0], to(0, b, 0))
-            send(cot_ref, cot_all.at[0, 0, 1], cot_sem.at[0, 0, 1, 0], to(0, 0, 1))
-    for dz in range(NZ):
-        for dx in range(1, nx):
-            here = block(dz, 0, dx, c)
-            arrived(here, plane_sem.at[dz, 0, dx])
-            for d in range(1, ny):
-                send(here, here, plane_sem.at[dz, d, dx], device(z, shift_y(d), x, c))
-            send(here, here, core_sem.at[dz, 0, dx], device(z, y, x, other))
+                send(rows_ref, rows_all.at[back(b), 0], rows_sem.at[back(b), 0], to(0, b, 0))
+        each_source(turn, d - 1, d - 1)
+    each_source(turn, NZ - 1, NZ - 1)
+    send(cot_ref, cot_all.at[0, 0, 1], cot_sem.at[0, 0, 1, 0], to(0, 0, 1))
+    send(rows_ref, rows_all.at[0, 1], rows_sem.at[0, 1], to(0, 0, 1))
     for d in range(1, nx):
         here = rows_all.at[d, 0]
         arrived(here, rows_sem.at[d, 0])
@@ -295,6 +332,22 @@
         copy.wait()
     send.finish()
 
+    def sent(way, d, dz):
+        if d < NZ - 1:
+
+            @pl.when(z < NZ - 1 if way == 0 else z > 0)
+            def _():
+                arrived(w_ref, z_out.at[way, d])
+
+    each_source(sent)
+    for dz in range(NZ):
+        for b in range(1, nx):
+            arrived(w_ref, x_out.at[dz, b])
+        for dx in range(nx):
+            for b in range(1, ny):
+                arrived(w_ref, y_out.at[dz, dx, b])
+            arrived(w_ref, c_out.at[dz, dx])
+
 
 def gather_first(grid_of, w, rows, cot, ints):
     grid = grid_of()
@@ -322,88 +375,99 @@
             dma((ZP, nx, NC)),
             dma((sends,)),
             dma((4,)),
+            dma((2, NZ)),
+            dma((2, NZ)),
+            dma((NZ, nx)),
+            dma((NZ, nx, ny)),
+            dma((NZ, nx)),
         ],
         compiler_params=pltpu.CompilerParams(collective_id=0, has_side_effects=True),
     )(w, rows, cot, ints)
 
 
-def exchange_kernel(grid_of, zp, cut, count, *refs):
+def shared_compute(n2, cot, w_in, w_down, out, back, dg, du, dd, h, ag, au):
+    hidden, width = w_down.shape
+    strip = 256
+    for low in range(0, hidden, strip):
+        cut = slice(low, min(low + strip, hidden))
+        up_cut = slice(hidden + cut.start, hidden + cut.stop)
+        gate_act = times(n2[...], w_in[:, cut])
+        up_act = times(n2[...], w_in[:, up_cut])
+        hidden_grad = times_transposed(cot[...], w_down[cut])
+        activated, slope = silu_parts(gate_act)
+        h[:, cut] = (activated * up_act).astype(bf16)
+        ag[:, cut] = (hidden_grad * up_act * slope).astype(bf16)
+        au[:, cut] = (hidden_grad * activated).astype(bf16)
+    turned = h[...].T
+    for low in range(0, width, strip):
+        cut = slice(low, low + strip)
+        out[:, cut] = times(h[...], w_down[:, cut])
+        back[:, cut] = times_transposed(ag[...], w_in[cut, :hidden]) + times_transposed(
+            au[...], w_in[cut, hidden:]
+        )
+        rows = n2[:, cut].T
+        dg[cut] = times(rows, ag[...]).astype(bf16)
+        du[cut] = times(rows, au[...]).astype(bf16)
+        dd[:, cut] = times(turned, cot[:, cut]).astype(bf16)
+
+
+def exchange_kernel(grid_of, zp, cut, src, out, plane_sem, core_sem, local_sem, send_sem):
     grid = grid_of()
     nx = grid.nx
-    ins, outs = refs[:count], refs[count : 2 * count]
-    plane_sem, core_sem, local_sem, send_sem = refs[2 * count :]
     send = Sender(send_sem)
     to = functools.partial(stepped, grid, zp)
     greet([to(*s) for s in around(grid, zp)])
     back = lambda d: (nx - d) % nx
-    for k in range(count):
-        src, out = ins[k], outs[k]
+    for a in range(1, zp):
+        send(src, out.at[zp - a, 0, 0], plane_sem.at[zp - a, 0, 0], to(a, 0, 0))
+    for b in range(1, nx):
+        send(src, out.at[0, back(b), 0], plane_sem.at[0, back(b), 0], to(0, b, 0))
+    send(src, out.at[0, 0, 1], core_sem.at[0, 0], to(0, 0, 1))
+    keep = pltpu.make_async_copy(src, out.at[0, 0, 0], local_sem)
+    keep.start()
+    h0 = (slice(None), pl.ds(0, cut))
+    h1 = (slice(None), pl.ds(cut, src.shape[1] - cut))
+    for a in range(1, zp):
+        here = out.at[a, 0, 0]
+        arrived(here, plane_sem.at[a, 0, 0])
+        for b in range(1, nx):
+            send(here.at[h0], out.at[a, back(b), 0].at[h0], plane_sem.at[a, back(b), 0], to(0, b, 0))
+        send(here, out.at[a, 0, 1], core_sem.at[a, 0], to(0, 0, 1))
+    for b in range(1, nx):
+        here = out.at[0, b, 0]
+        arrived(here, plane_sem.at[0, b, 0])
         for a in range(1, zp):
-            send(src, out.at[zp - a, 0, 0], plane_sem.at[k, zp - a, 0, 0], to(a, 0, 0))
+            send(here.at[h1], out.at[zp - a, b, 0].at[h1], plane_sem.at[zp - a, b, 1], to(a, 0, 0))
+        send(here, out.at[0, b, 1], core_sem.at[0, b], to(0, 0, 1))
+    for a in range(1, zp):
         for b in range(1, nx):
-            send(src, out.at[0, back(b), 0], plane_sem.at[k, 0, back(b), 0], to(0, b, 0))
-        send(src, out.at[0, 0, 1], core_sem.at[k, 0, 0], to(0, 0, 1))
-        pltpu.make_async_copy(src, out.at[0, 0, 0], local_sem.at[k]).start()
-    for k in range(count):
-        out = outs[k]
-        h0 = (slice(None), pl.ds(0, cut))
-        h1 = (slice(None), pl.ds(cut, ins[k].shape[1] - cut))
-        for a in range(1, zp):
-            here = out.at[a, 0, 0]
-            arrived(here, plane_sem.at[k, a, 0, 0])
-            for b in range(1, nx):
-                send(here.at[h0], out.at[a, back(b), 0].at[h0], plane_sem.at[k, a, back(b), 0], to(0, b, 0))
-            send(here, out.at[a, 0, 1], core_sem.at[k, a, 0], to(0, 0, 1))
-        for b in range(1, nx):
-            here = out.at[0, b, 0]
-            arrived(here, plane_sem.at[k, 0, b, 0])
-            for a in range(1, zp):
-                send(here.at[h1], out.at[zp - a, b, 0].at[h1], plane_sem.at[k, zp - a, b, 1], to(a, 0, 0))
-            send(here, out.at[0, b, 1], core_sem.at[k, 0, b], to(0, 0, 1))
-    for k in range(count):
-        out = outs[k]
-        h0 = (slice(None), pl.ds(0, cut))
-        h1 = (slice(None), pl.ds(cut, ins[k].shape[1] - cut))
-        for a in range(1, zp):
-            for b in range(1, nx):
-                here = out.at[a, b, 0]
-                arrived(here.at[h0], plane_sem.at[k, a, b, 0])
-                arrived(here.at[h1], plane_sem.at[k, a, b, 1])
-                send(here, out.at[a, b, 1], core_sem.at[k, a, b], to(0, 0, 1))
-    for k in range(count):
-        for a in range(zp):
-            for b in range(nx):
-                arrived(outs[k].at[a, b, 1], core_sem.at[k, a, b])
-        pltpu.make_async_copy(ins[k], outs[k].at[0, 0, 0], local_sem.at[k]).wait()
+            here = out.at[a, b, 0]
+            arrived(here.at[h0], plane_sem.at[a, b, 0])
+            arrived(here.at[h1], plane_sem.at[a, b, 1])
+            send(here, out.at[a, b, 1], core_sem.at[a, b], to(0, 0, 1))
+    for a in range(zp):
+        for b in range(nx):
+            arrived(out.at[a, b, 1], core_sem.at[a, b])
+    keep.wait()
     send.finish()
 
 
-def exchange(grid_of, zp, number, *arrays):
+def exchange(grid_of, zp, number, rows):
     grid = grid_of()
     nx = grid.nx
-    count = len(arrays)
-    sends = count * (zp * nx * 2 + zp * nx * nx * 2)
+    sends = zp * nx * 2 + zp * nx * nx * 2
     anywhere = pl.BlockSpec(memory_space=pl.ANY)
     dma = pltpu.SemaphoreType.DMA
     return pl.pallas_call(
-        functools.partial(
-            exchange_kernel, grid_of, zp, arrays[0].shape[1] // 256 * 128, count
-        ),
-        out_shape=tuple(
-            jax.ShapeDtypeStruct((zp, nx, NC) + v.shape, v.dtype) for v in arrays
-        ),
-        in_specs=[anywhere] * count,
-        out_specs=(anywhere,) * count,
-        scratch_shapes=[
-            dma((count, zp, nx, 2)),
-            dma((count, zp, nx)),
-            dma((count,)),
-            dma((sends,)),
-        ],
+        functools.partial(exchange_kernel, grid_of, zp, rows.shape[1] // 256 * 128),
+        out_shape=jax.ShapeDtypeStruct((zp, nx, NC) + rows.shape, rows.dtype),
+        in_specs=[anywhere],
+        out_specs=anywhere,
+        scratch_shapes=[dma((zp, nx, 2)), dma((zp, nx)), dma, dma((sends,))],
         compiler_params=pltpu.CompilerParams(
             collective_id=number, has_side_effects=True
         ),
-    )(*arrays)
+    )(rows)
 
 
 def add_into(dst, src, rows):
@@ -422,12 +486,20 @@
     nx = grid.nx
     if small:
         pieces, refs = refs[0], refs[1:]
+        shared_ins, refs = refs[:4], refs[4:]
     job_ins, refs = refs[: len(jobs)], refs[len(jobs) :]
     out, refs = refs[0], refs[1:]
     if small:
         pieces_out, refs = refs[0], refs[1:]
+        shared_outs, refs = refs[:5], refs[5:]
     job_outs, refs = refs[: len(jobs)], refs[len(jobs) :]
     refs, (job_send, job_recv) = refs[:-2], refs[-2:]
+    if small:
+        shared_held, load_sem, refs = refs[-8:-1], refs[-1], refs[:-8]
+        loads = [
+            pltpu.make_async_copy(a, b, load_sem.at[k])
+            for k, (a, b) in enumerate(zip(shared_ins, shared_held))
+        ]
     each = functools.partial(each_job, grid, jobs, job_ins, job_outs, job_send, job_recv)
     own, got_c, turn_x, turn_p, got_p, got_x = refs[:6]
     local_sem, c_sem, turn_sem, p_sem, x_sem, small_sem, send_sem = refs[6:]
@@ -460,6 +532,9 @@
             pieces.at[0, 0, 0], pieces_out.at[0, 0, 0], small_sem.at[0, 0, 0]
         ).start()
     each(lambda copy: copy.start())
+    if small:
+        for load in loads:
+            load.start()
     rows = 32
 
     def ready(a, b):
@@ -489,6 +564,10 @@
             add_into(own.at[:, 0, b, :, h1], turn_p.at[:, a - 1, b - 1], rows)
         send(own.at[:, 0, b], got_x.at[:, b - 1], x_sem.at[b - 1], to(0, b, 0))
     ready(0, 0)
+    if small:
+        for load in loads:
+            load.wait()
+        shared_compute(*shared_held[:4], *shared_outs, *shared_held[4:])
     for a in range(1, zp):
         arrived(got_p.at[:, a - 1], p_sem.at[a - 1])
         add_into(own.at[:, 0, 0], got_p.at[:, a - 1], rows)
@@ -505,11 +584,11 @@
     send.finish()
 
 
-def sum_around(grid_of, zp, number, parts, pieces=None, jobs=(), job_arrays=()):
+def sum_around(grid_of, zp, number, parts, pieces=None, shared=(), jobs=(), job_arrays=()):
     grid = grid_of()
     nx = grid.nx
     payloads, rows, width = parts.shape[0], parts.shape[-2], parts.shape[-1]
-    cut = width // 256 * 128
+    cut = width // 640 * 512
     anywhere = pl.BlockSpec(memory_space=pl.ANY)
     dma = pltpu.SemaphoreType.DMA
     small = pieces is not None
@@ -517,7 +596,11 @@
     args = [parts]
     if small:
         out_shape.append(jax.ShapeDtypeStruct(pieces.shape, pieces.dtype))
-        args.append(pieces)
+        args += [pieces, *shared]
+        tokens, hidden = shared[0].shape[0], shared[3].shape[0]
+        out_shape += [jax.ShapeDtypeStruct((tokens, width), f32)] * 2
+        out_shape += [jax.ShapeDtypeStruct((width, hidden), bf16)] * 2
+        out_shape.append(jax.ShapeDtypeStruct((hidden, width), bf16))
     plain = len(out_shape)
     out_shape += job_shapes(grid, jobs, job_arrays)
     args += list(job_arrays)
@@ -527,7 +610,10 @@
         functools.partial(sum_kernel, grid_of, zp, cut, small, jobs),
         out_shape=tuple(out_shape),
         in_specs=[anywhere] * len(args),
-        out_specs=(anywhere,) * len(out_shape),
+        out_specs=tuple(
+            pl.BlockSpec(memory_space=pltpu.VMEM) if 2 <= n < plain else anywhere
+            for n in range(len(out_shape))
+        ),
         scratch_shapes=[
             vmem((payloads, zp, nx, rows, width)),
             vmem((payloads, zp, nx, rows, width)),
@@ -543,6 +629,13 @@
             dma((zp, nx, NC)),
             dma((zp * nx * 6 + 8,)),
         ]
+        + (
+            [pltpu.VMEM(v.shape, bf16) for v in shared]
+            + [pltpu.VMEM((tokens, hidden), bf16)] * 3
+            + [dma((4,))]
+            if small
+            else []
+        )
         + job_sems(grid, jobs),
         compiler_params=pltpu.CompilerParams(
             collective_id=number,
@@ -889,15 +982,19 @@
     return [pltpu.SemaphoreType.DMA((count,)), pltpu.SemaphoreType.DMA((count,))]
 
 
-def dense_kernel(grid_of, orders, jobs, *refs):
+def dense_kernel(grid_of, orders, jobs, items, *refs):
     grid = grid_of()
     z, y, x, c, nx, ny = grid.z, grid.y, grid.x, grid.c, grid.nx, grid.ny
     count, more = len(orders), len(jobs)
+    wholes = items[-1][0] + 1
     take = lambda n: (refs[:n], refs[n:])
-    ins, refs = take(count)
+    ins, refs = take(wholes)
     job_ins, refs = take(more)
-    outs, refs = take(count)
+    outs, refs = take(wholes)
     job_outs, refs = take(more)
+    strip = lambda v, low, wide: v.at[(slice(None),) * (len(v.shape) - 1) + (pl.ds(low, wide),)]
+    ins = [strip(ins[k], low, wide) for k, low, wide in items]
+    outs = [strip(outs[k], low, wide) for k, low, wide in items]
     held, refs = take(count)
     got_c, refs = take(count)
     got_one, refs = take(count)
@@ -914,11 +1011,15 @@
     )
     send = Sender(send_sem)
     loads = []
-    for k in range(count):
+
+    def begin(k):
         send(ins[k].at[:, :, :, other], got_c[k], c_sem.at[k], device(z, y, x, other))
         load = pltpu.make_async_copy(ins[k].at[:, :, :, c], held[k], local_sem.at[k])
         load.start()
         loads.append(load)
+
+    for k in range(min(3, count)):
+        begin(k)
     each_job(grid, jobs, job_ins, job_outs, job_send, job_recv, lambda copy: copy.start())
 
     def add(dst, src):
@@ -937,6 +1038,8 @@
             dst[index] = (dst[index].astype(f32) + src[index].astype(f32)).astype(dst.dtype)
 
     def first(k):
+        if k + 3 < count:
+            begin(k + 3)
         loads[k].wait()
         arrived(got_c[k], c_sem.at[k])
         add(held[k], got_c[k])
@@ -999,14 +1102,20 @@
     send.finish()
 
 
-def reduce_dense(grid_of, number, arrays, orders, jobs, job_arrays):
+def reduce_dense(grid_of, number, arrays, jobs, job_arrays):
     grid = grid_of()
     nx, ny = grid.nx, grid.ny
-    count = len(arrays)
+    items = []
+    for k, v in enumerate(arrays):
+        wide = v.shape[5]
+        low = wide // 2 if wide % 256 == 0 else wide
+        items += [(k, at, low) for at in range(0, wide, low)]
+    orders = ["xy" if n % 2 == 0 else "yx" for n in range(len(items))]
+    count = len(items)
     anywhere = pl.BlockSpec(memory_space=pl.ANY)
     dma = pltpu.SemaphoreType.DMA
-    block = [v.shape[4:] for v in arrays]
-    kind = [v.dtype for v in arrays]
+    block = [(arrays[k].shape[4], wide) for k, _, wide in items]
+    kind = [arrays[k].dtype for k, _, _ in items]
     far = max(nx, ny)
     held = [pltpu.VMEM((NZ, ny, nx) + b, t) for b, t in zip(block, kind)]
     one = [
@@ -1018,13 +1127,13 @@
         for b, t, o in zip(block, kind, orders)
     ]
     made = pl.pallas_call(
-        functools.partial(dense_kernel, grid_of, orders, jobs),
+        functools.partial(dense_kernel, grid_of, orders, jobs, items),
         out_shape=tuple(
-            [jax.ShapeDtypeStruct((NZ // ZP,) + b, t) for b, t in zip(block, kind)]
+            [jax.ShapeDtypeStruct((NZ // ZP,) + v.shape[4:], v.dtype) for v in arrays]
             + job_shapes(grid, jobs, job_arrays)
         ),
-        in_specs=[anywhere] * (count + len(jobs)),
-        out_specs=(anywhere,) * (count + len(jobs)),
+        in_specs=[anywhere] * (len(arrays) + len(jobs)),
+        out_specs=(anywhere,) * (len(arrays) + len(jobs)),
         scratch_shapes=held
         + held
         + one
@@ -1046,7 +1155,53 @@
             vmem_limit_bytes=60 * 2**20,
         ),
     )(*arrays, *job_arrays)
-    return made[:count], made[count:]
+    return made[: len(arrays)], made[len(arrays) :]
+
+
+def finish_kernel(grid_of, mine, dense, *refs):
+    grid = grid_of()
+    kinds = 3
+    names = mine * kinds
+    own, far = refs[:names], refs[names : 2 * names]
+    terms = refs[2 * names : 2 * names + dense]
+    outs = refs[2 * names + dense :]
+    for n in range(names):
+        i, kind = n // kinds, n % kinds
+        sums = [own[n][0].astype(f32), None]
+        for d in range(1, NZ):
+            got = far[n][d - 1].astype(f32)
+            sums[d % ZP] = got if sums[d % ZP] is None else sums[d % ZP] + got
+        outs[kind][grid.zm, i] = sums[0]
+        outs[kind][1 - grid.zm, i] = sums[1]
+    for n in range(dense):
+        total = terms[n][0].astype(f32)
+        for d in range(1, terms[n].shape[0]):
+            total = total + terms[n][d].astype(f32)
+        outs[kinds + n][...] = total
+
+
+def finish(grid_of, mine, columns, far, terms):
+    grid = grid_of()
+    whole = lambda v: pl.BlockSpec(v.shape, lambda _: (0,) * len(v.shape))
+    out_shape = [
+        jax.ShapeDtypeStruct((ZP, mine) + columns[k].shape[1:], f32) for k in range(3)
+    ] + [jax.ShapeDtypeStruct(v.shape[1:], f32) for v in terms]
+    return pl.pallas_call(
+        functools.partial(finish_kernel, grid_of, mine, len(terms)),
+        grid=(1,),
+        out_shape=out_shape,
+        in_specs=[
+            pl.BlockSpec(
+                (1,) + v.shape[1:],
+                lambda _: (lax.axis_index("wide") // grid.ny, 0, 0),
+            )
+            for v in columns
+        ]
+        + [whole(v) for v in far]
+        + [whole(v) for v in terms],
+        out_specs=[whole(v) for v in out_shape],
+        compiler_params=pltpu.CompilerParams(vmem_limit_bytes=62 * 2**20),
+    )(*columns, *far, *terms)
 
 
 def attention_bias(segment, labels_all, query_places, key_places):
@@ -1114,9 +1269,15 @@
     )
     small_all = bundle_all[:, 4 * width :]
     gather_all = lambda v: lax.all_gather(v, BOTH, axis=0, tiled=True)
-    s_both = gather_all(jnp.concatenate([shared_gate, shared_up], axis=1))
-    s_gate, s_up = s_both[:, :hidden_width], s_both[:, hidden_width:]
-    s_down = gather_all(shared_down)
+    shared_in, shared_out_in, integers_all = lax.optimization_barrier(
+        (
+            jnp.concatenate([shared_gate, shared_up], axis=1),
+            shared_down,
+            integers_all,
+        )
+    )
+    s_both = gather_all(shared_in)
+    s_down = gather_all(shared_out_in)
     w_router = small_all[:, :experts]
     gain_one = small_all[:, experts].astype(f32)
     gain_two = small_all[:, experts + 1].astype(f32)
@@ -1143,7 +1304,7 @@
     inverse_two = norm_scale(middle)
     normed_two = (middle * inverse_two * gain_two).astype(bf16)
 
-    (rows_all,) = exchange(grid_of, ZP, 1, normed_two)
+    rows_all = exchange(grid_of, ZP, 1, normed_two)
     rows_all = rows_all.reshape(sources, tok_rows, width)
     cot_all = cot_all.reshape(sources, tok_rows, width)
     router_probs_all = jax.nn.softmax(
@@ -1208,12 +1369,21 @@
         grads.update({(i, k): by_wide(v) for k, v in enumerate(made)})
     column.update({name: summed(name) for name in along_y})
     behind = (names[2:4], names[:1])
-    (sums, sent), moved = sum_around(
+    (
+        sums,
+        sent,
+        shared_out,
+        shared_back,
+        shared_gate_grad,
+        shared_up_grad,
+        shared_down_grad,
+    ), moved = sum_around(
         grid_of,
         ZP,
         2,
         both_parts.reshape(2, ZP, nx, NC, tok_rows, width),
         jnp.stack(prob_parts, axis=1).reshape(ZP, nx, NC, mine, tok_rows),
+        (normed_two, cotangent, s_both, s_down),
         *jobs_of(*behind),
     )
     landed(*behind, moved)
@@ -1228,23 +1398,7 @@
         jnp.where(same[:, :, None], sent.reshape(1, experts, tok_rows), 0.0), axis=1
     ).T
 
-    shared_gate_act = times(normed_two, s_gate)
-    shared_up_act = times(normed_two, s_up)
-    shared_act, shared_slope = silu_parts(shared_gate_act)
-    shared_hidden = (shared_act * shared_up_act).astype(bf16)
-    shared_out = times(shared_hidden, s_down)
     out_grad = cotangent.astype(f32)
-    shared_down_grad = contract_rows(shared_hidden, cotangent)
-    shared_hidden_grad = times_transposed(cotangent, s_down)
-    shared_gate_act_grad = (shared_hidden_grad * shared_up_act * shared_slope).astype(
-        bf16
-    )
-    shared_up_act_grad = (shared_hidden_grad * shared_act).astype(bf16)
-    shared_gate_grad = contract_rows(normed_two, shared_gate_act_grad)
-    shared_up_grad = contract_rows(normed_two, shared_up_act_grad)
-    normed_two_grad = times_transposed(shared_gate_act_grad, s_gate) + times_transposed(
-        shared_up_act_grad, s_up
-    )
     block_out = (middle + shared_out + routed).astype(bf16)
 
     logit_grad = router_probs * (
@@ -1258,7 +1412,7 @@
         preferred_element_type=f32,
     )
     normed_two_grad = (
-        normed_two_grad
+        shared_back
         + routed_grad
         + lax.dot_general(
             logit_grad,
@@ -1295,6 +1449,7 @@
         3,
         parts.reshape(2, 1, nx, NC, tok_rows, width),
         None,
+        (),
         *jobs_of(*behind),
     )
     value_act_grad, key_act_grad = value_key
@@ -1351,11 +1506,13 @@
         4,
         [by_place(v.astype(bf16)) for v in dense]
         + [extras.reshape(NZ, ny, nx, NC, share + 8, 128)],
-        ("xy", "yx", "xy", "yx", "xy", "yx", "xy", "xy"),
         *jobs_of([], names[4:]),
     )
     landed([], names[4:], moved)
     (
+        expert_gate_grad,
+        expert_up_grad,
+        expert_down_grad,
         output_weight_sum,
         shared_down_sum,
         shared_gate_sum,
@@ -1364,26 +1521,13 @@
         key_sum,
         value_sum,
         extra_sum,
-    ) = (jnp.sum(v.astype(f32), axis=0) for v in terms)
-
-    def expert_sum(kind):
-        halves = [[], []]
-        for i in range(mine):
-            name = (i, kind)
-            same = lax.dynamic_index_in_dim(column[name], grid.z, 0, keepdims=False)
-            same = same.astype(f32)
-            far = 0.0
-            for d in range(1, NZ):
-                got = along_z[name][d - 1].astype(f32)
-                if d % ZP == 0:
-                    same = same + got
-                else:
-                    far = far + got
-            halves[0].append(jnp.where(grid.zm == 0, same, far))
-            halves[1].append(jnp.where(grid.zm == 0, far, same))
-        return jnp.stack(halves[0] + halves[1])
-
-    expert_gate_grad, expert_up_grad, expert_down_grad = (expert_sum(k) for k in range(3))
+    ) = finish(
+        grid_of, mine, [column[n] for n in names], [along_z[n] for n in names], terms
+    )
+    expert_gate_grad, expert_up_grad, expert_down_grad = (
+        v.reshape((local_experts,) + v.shape[2:])
+        for v in (expert_gate_grad, expert_up_grad, expert_down_grad)
+    )
     return (
         block_out,
         input_grad,

time: 714 us -> 640 us (0.90)
  Pallas kernels: 526 us -> 500 us
  other arithmetic: 54.4 us -> 28.7 us
  matrix products: 75.1 us -> 55.8 us
    pallas_call x1, Pallas kernels: 104 us -> 87.8 us  [gather_first(): pl.pallas_call(functools.partial(gather_kernel, grid_of), out_shape=(jax....]
    select_n x6 -> x0, other arithmetic: 12.2 us -> none  [expert_sum(): halves[0].append(jnp.where(grid.zm == 0, same, far))]
    dot_general x7 -> x4, matrix products: 30.2 us -> 21.3 us  [times(): return jnp.dot(left, right, preferred_element_type=f32)]
    dot_general x7 -> x4, matrix products: 17.5 us -> 11.1 us  [contract_rows(): lax.dot_general(left, right, (((0,), (0,)), ((), ())), preferred_element_...]
    dot_general x7 -> x4, matrix products: 18.4 us -> 14.1 us  [times_transposed(): lax.dot_general(left, right, (((1,), (1,)), ((), ())), preferred_element_...]
    unnamed x177 -> x89, local copies, waits for them, and re-layouts: 15.2 us -> 11.8 us
    pallas_call x2 -> x3, Pallas kernels: 157 us -> 153 us  [the longest x1 112 us: reduce_dense(): pl.pallas_call(functools.partial(dense_kernel, grid_of, orders, jobs, ite...]
  transfers between devices with their start and end apart: 2 -> 2, of which waited for: 0 -> 0; matrix products, arithmetic and copies ran while one was open for 10% -> 7% of each run, Pallas kernels for 46% -> 24%
where the time goes in v4:
time: 640 us; the launch traced here: 632 us
  Pallas kernels  500 us (78%)
  matrix products  55.8 us (9%)
  local copies, waits for them, and re-layouts  31.4 us (5%)
  other arithmetic  28.7 us (4%)
  between operations  15.2 us (2%)
    pallas_call x2, Pallas kernels, sum_around(): pl.pallas_call(functools.partial(sum_kernel, grid_of, zp, cut, small, job...  115 us
    pallas_call x1, Pallas kernels, reduce_dense(): pl.pallas_call(functools.partial(dense_kernel, grid_of, orders, jobs, ite...  112 us
    pallas_call x2, Pallas kernels, run_expert(): pl.pallas_call(functools.partial(expert_kernel, grid_of, capacity, steps,...  106 us
    pallas_call x1, Pallas kernels, gather_first(): pl.pallas_call(functools.partial(gather_kernel, grid_of), out_shape=(jax....  87.8 us
    pallas_call x1, Pallas kernels, exchange(): pl.pallas_call(functools.partial(exchange_kernel, grid_of, zp, rows.shape...  34.6 us
    pallas_call x1, Pallas kernels, attention_backward(): pl.pallas_call(functools.partial(attention_back_kernel, grid_of, jobs), g...  29.2 us
    dot_general x4, matrix products, times(): return jnp.dot(left, right, preferred_element_type=f32)  21.3 us
    dot_general x4, matrix products, times_transposed(): lax.dot_general(left, right, (((1,), (1,)), ((), ())), preferred_element_...  14.1 us
  transfers between devices with their start and end apart: 2, of which 0 were waited for; matrix products, arithmetic and copies ran while one was open for 7% of the time, Pallas kernels for 24%

profile of v4, /device:TPU:0, one launch (start us, length us, event | category | flops | bytes accessed | tf_op | source)
XLA Modules:
  0.0 632.1 jit_solution(1882716597050895983)
XLA Ops:
  14.3 87.8 %shard_map.288 = (bf16[32,40,5248]{2,1,0:T(8,128)(2,1)}, bf16[2,2,256,1280]{3,2,1,0:T(8,128)(2,1)}, bf16[2,2,2,256,1280]{4,3,2,1,0:T(8,128)(2,1)}, s32[2,2,2,8,256]{4,3,2,1,0:T(8,128)}) custom-call(bf16[40,5248]{1,0:T(8,128)(2,1)} %concatenate.22.w_ref, bf16[256,1280]{1,0:T(8,128)(2,1)} %rows_ref.1, bf16[256,1280]{1,0:T(8,128)(2,1)} %refs_2_.1, ...), custom_call_target="tpu_custom_call" | custom-call | tf_op jit(solution)/shard_map/pallas_call | solution.py:360
  108.2 6.7 %convolution_convert_fusion.4.v_ref = bf16[1024,1280]{1,0:T(8,128)(2,1)S(1)} fusion(bf16[1024,1280]{1,0:T(8,128)(2,1)S(1)} %fusion.2, bf16[1280,5248]{1,0:T(8,128)(2,1)} %bitcast.188), kind=kOutput, calls=%fused_computation.9 | convolution fusion | flops 3356753920 | bytes 8519680 | tf_op jit(solution)/shard_map/dot_general | solution.py:34
  114.9 7.7 %convolution_convert_fusion.5.k_ref = bf16[1024,1280]{1,0:T(8,128)(2,1)} fusion(bf16[1024,1280]{1,0:T(8,128)(2,1)S(1)} %fusion.2, bf16[1280,5248]{1,0:T(8,128)(2,1)} %bitcast.189), kind=kOutput, calls=%fused_computation.10 | convolution fusion | flops 3356753920 | bytes 8519680 | tf_op jit(solution)/shard_map/dot_general | solution.py:34
  122.6 3.8 fusion.26.q_ref
  129.8 9.1 %shard_map.289 = bf16[256,1280]{1,0:T(8,128)(2,1)S(1)} custom-call(bf16[256,1280]{1,0:T(8,128)(2,1)S(1)} %copy-done.9, bf16[1024,1280]{1,0:T(8,128)(2,1)S(1)} %copy-done.3, bf16[1024,1280]{1,0:T(8,128)(2,1)S(1)} %convolution_convert_fusion.4.v_ref, f32[256,1024]{1,0:T(8,128)S(1)} %and_select_fusion.1.bias_ref), custom_call_target="tpu_custom_call" | custom-call | flops 1342177280 | bytes 7602176 | tf_op jit(solution)/shard_map/pallas_call | solution.py:660
  138.9 3.1 multiply_reduce_fusion.3
  143.2 34.6 %shard_map.290 = bf16[2,2,2,256,1280]{4,3,2,1,0:T(8,128)(2,1)} custom-call(bf16[256,1280]{1,0:T(8,128)(2,1)} %multiply_convert_fusion.src.refs_1_), custom_call_target="tpu_custom_call" | custom-call | tf_op jit(solution)/shard_map/pallas_call | solution.py:461
  182.1 4.1 fusion.82
  186.8 46.4 %shard_map.291 = (bf16[2,8,256,1280]{3,2,1,0:T(8,128)(2,1)}, f32[8,1,256]{2,1,0:T(1,128)}, bf16[1280,896]{1,0:T(8,128)(2,1)}, bf16[1280,896]{1,0:T(8,128)(2,1)}, bf16[896,1280]{1,0:T(8,128)(2,1)}) custom-call(bf16[8,256,1280]{2,1,0:T(8,128)(2,1)} %bitcast.169, bf16[8,256,1280]{2,1,0:T(8,128)(2,1)} %bitcast.211, s32[8,1,256]{2,1,0:T(1,128)} %get-tuple-element.210.refs_2_, ...), custom_call_target="tpu_custom_call" | custom-call | flops 26424115200 | bytes 55705600 | tf_op jit(solution)/shard_map/pallas_call | solution.py:871
  233.2 59.3 %shard_map.292 = (bf16[2,8,256,1280]{3,2,1,0:T(8,128)(2,1)}, f32[8,1,256]{2,1,0:T(1,128)}, bf16[1280,896]{1,0:T(8,128)(2,1)}, bf16[1280,896]{1,0:T(8,128)(2,1)},...) custom-call(bf16[8,256,1280]{2,1,0:T(8,128)(2,1)} %bitcast.170, ...), custom_call_target="tpu_custom_call" | custom-call | flops 26424115200 | bytes 55705600 | tf_op jit(solution)/shard_map/pallas_call | solution.py:871
  298.5 4.5 reshape.441.refs_4_
  303.0 66.5 %shard_map.293 = (bf16[2,256,1280]{2,1,0:T(8,128)(2,1)}, f32[2,2,2,2,256]{4,3,2,1,0:T(2,128)}, f32[256,1280]{1,0:T(8,128)}, f32[256,1280]{1,0:T(8,128)}, bf16[12...) custom-call(bf16[2,2,2,2,256,1280]{5,4,3,2,1,0:T(8,128)(2,1)} %bitca, ...), custom_call_target="tpu_custom_call" | custom-call | tf_op jit(solution)/shard_map/pallas_call | solution.py:609
  370.4 2.9 fusion.73
  373.3 2.9 fusion.34.refs_2_.refs_3_
  382.0 3.5 fusion.29.g_ref
  386.3 29.2 %shard_map.294 = (bf16[256,1280]{1,0:T(8,128)(2,1)S(1)}, bf16[2,1024,1280]{2,1,0:T(8,128)(2,1)}, bf16[1,4,160,896]{3,2,1,0:T(8,128)(2,1)S(1)}, bf16[3,160,896]{2,1,0:T(8,128)(2,1)S(1)}) custom-call(bf16[256,1280]{1,0:T(8,128)(2,1)S(1)} %copy-done.10, bf16[1024,1280]{1,0:T(8,128)(2,1)S(1)} %copy-done.4, bf16[1024,1280]{1,0:T(8,128)(2,1)S(1)} %copy-done.2, ...), custom_call_target="tpu_custom_call" | custom-call | flops 3355443200 | bytes 13500416 | tf_op jit(solution)/shard_map/pallas_call | solution.py:718
  416.5 48.5 %shard_map.295 = (bf16[2,256,1280]{2,1,0:T(8,128)(2,1)}, bf16[1,4,112,1280]{3,2,1,0:T(8,128)(2,1)}, bf16[3,112,1280]{2,1,0:T(8,128)(2,1)}, bf16[3,160,896]{2,1,0:T(8,128)(2,1)}) custom-call(bf16[2,1,2,2,256,1280]{5,4,3,2,1,0:T(8,128)(2,1)} %bitcast.172, bf16[4,2,112,1280]{3,2,1,0:T(8,128)(2,1)} %bitcast.173, bf16[4,112,1280]{2,1,0:T(8,128)(2,1)} %fusion.35.refs_1_.refs_2_, ...), custom_call_target="tpu_custom_call" | custom-call | tf_op jit(solution)/shard_map/pallas_call | solution.py:609
  465.0 3.3 fusion.10
  479.5 3.1 fusion.17
  482.5 4.2 fusion.44
  489.4 2.9 fusion.32.refs_9_.refs_5_
  493.5 4.2 reshape.413.refs_1_
  499.1 111.7 %shard_map.296 = (bf16[2,40,1280]{2,1,0:T(8,128)(2,1)}, bf16[2,28,1280]{2,1,0:T(8,128)(2,1)}, bf16[2,40,896]{2,1,0:T(8,128)(2,1)}, bf16[2,40,896]{2,1,0:T(8,128)...) custom-call(bf16[4,2,2,2,40,1280]{5,4,3,2,1,0:T(8,128)(2,1)} %bitcas, ...), custom_call_target="tpu_custom_call" | custom-call | tf_op jit(solution)/shard_map/pallas_call | solution.py:1129
  610.9 7.1 %shard_map.297 = (f32[2,2,160,896]{3,2,1,0:T(8,128)}, f32[2,2,160,896]{3,2,1,0:T(8,128)}, f32[2,2,112,1280]{3,2,1,0:T(8,128)}, f32[40,1280]{1,0:T(8,128)}, f32[2...) custom-call(bf16[4,160,896]{2,1,0:T(8,128)(2,1)} %fusion.37.refs_7_., ...), custom_call_target="tpu_custom_call" | custom-call | tf_op jit(solution)/shard_map/pallas_call | solution.py:1189
  (164 shorter events, 60.0 us)
Async XLA Ops:
  7.2 291.3 %all-gather.6.cloned.1.call-start = ((), (), s32[]{:S(2)}) async-start(), calls=%async_computation.1 | async-start | bytes 2703360 | tf_op jit(solution)/shard_map/all_gather | solution.py:1271
  102.1 5.4 copy-start.18
  102.2 200.8 %all-gather.4.cloned.1.call-start = ((), (), s32[]{:S(2)}) async-start(), calls=%async_computation | async-start | bytes 4730880 | tf_op jit(solution)/shard_map/all_gather | solution.py:1271
  108.2 14.4 %copy-start.13 = (bf16[1024,1280]{1,0:T(8,128)(2,1)}, bf16[1024,1280]{1,0:T(8,128)(2,1)S(1)}, u32[]{:S(2)}) copy-start(bf16[1024,1280]{1,0:T(8,128)(2,1)S(1)} %fusion.2) | copy-start | bytes 7864324
  114.9 12.1 %copy-start.1 = (bf16[1024,1280]{1,0:T(8,128)(2,1)}, bf16[1024,1280]{1,0:T(8,128)(2,1)S(1)}, u32[]{:S(2)}) copy-start(bf16[1024,1280]{1,0:T(8,128)(2,1)S(1)} %convolution_convert_fusion.4.v_ref) | copy-start | bytes 7864324
  122.6 4.1 copy-start.39
  129.8 9.1 %copy-start.19 = (bf16[256,1280]{1,0:T(8,128)(2,1)S(1)}, bf16[256,1280]{1,0:T(8,128)(2,1)}, u32[]{:S(2)}) copy-start(bf16[256,1280]{1,0:T(8,128)(2,1)} %rows_ref.1) | copy-start | bytes 1966084
  233.2 59.4 %copy-start.40 = (f32[8,1,256]{2,1,0:T(1,128)S(1)}, f32[8,1,256]{2,1,0:T(1,128)}, u32[]{:S(2)}) copy-start(f32[8,1,256]{2,1,0:T(1,128)} %get-tuple-element.83) | copy-start | bytes 24580
  233.2 60.8 %copy-start.20 = (bf16[256,1280]{1,0:T(8,128)(2,1)S(1)}, bf16[256,1280]{1,0:T(8,128)(2,1)}, u32[]{:S(2)}) copy-start(bf16[256,1280]{1,0:T(8,128)(2,1)} %rows_ref.1) | copy-start | bytes 1966084
  298.5 87.1 %copy-start = (bf16[4,160,896]{2,1,0:T(8,128)(2,1)}, bf16[4,160,896]{2,1,0:T(8,128)(2,1)S(1)}, u32[]{:S(2)}) copy-start(bf16[4,160,896]{2,1,0:T(8,128)(2,1)S(1)} %fusion.36.refs_1_) | copy-start | bytes 3440644
  370.4 5.8 copy-start.24
  370.4 5.8 copy-start.35
  380.7 4.9 copy-start.7
  380.7 4.9 copy-start.11
  382.0 4.2 copy-start.4
  382.0 4.3 copy-start.10
  416.5 48.5 %copy-start.8 = (bf16[3,160,896]{2,1,0:T(8,128)(2,1)}, bf16[3,160,896]{2,1,0:T(8,128)(2,1)S(1)}, u32[]{:S(2)}) copy-start(bf16[3,160,896]{2,1,0:T(8,128)(2,1)S(1)} %get-tuple-element.105.refs_7_) | copy-start | bytes 2580484
  486.7 5.5 copy-start.6
  486.7 5.5 copy-start.12
  493.5 4.2 copy-start.25
  493.5 4.2 copy-start.26
  493.5 4.3 copy-start.27
  610.8 11.3 %copy-start.17 = (f32[256,1280]{1,0:T(8,128)S(1)}, f32[256,1280]{1,0:T(8,128)}, u32[]{:S(2)}) copy-start(f32[256,1280]{1,0:T(8,128)} %copy-done.15) | copy-start | bytes 3932164
  610.8 11.3 %copy-start.22 = (bf16[256,1280]{1,0:T(8,128)(2,1)S(1)}, bf16[256,1280]{1,0:T(8,128)(2,1)}, u32[]{:S(2)}) copy-start(bf16[256,1280]{1,0:T(8,128)(2,1)} %rows_ref.1) | copy-start | bytes 1966084
  (19 other events, 53.8 us)
Sparse Core Ops, SparseCore 0:
  102.3 60.3 all-gather.5
  166.1 63.8 all-gather.3

commit v5 on v4

--- a/solution.py
+++ b/solution.py
@@ -49,7 +49,7 @@
 
 
 def silu_parts(gate_act):
-    logistic = jax.nn.sigmoid(gate_act)
+    logistic = 0.5 * jnp.tanh(0.5 * gate_act) + 0.5
     return (gate_act * logistic, logistic * (1.0 + gate_act * (1.0 - logistic)))
 
 
@@ -646,6 +646,79 @@
     return made[:plain], made[plain:]
 
 
+def project_kernel(rows_ref, wq_ref, wk_ref, wv_ref, q_ref, k_ref, v_ref):
+    rows = rows_ref[...]
+    q_ref[...] = times(rows[: q_ref.shape[0]], wq_ref[...]).astype(bf16)
+    k_ref[...] = times(rows, wk_ref[...]).astype(bf16)
+    v_ref[...] = times(rows, wv_ref[...]).astype(bf16)
+
+
+def project(rows, weights, tokens):
+    length, width = rows.shape
+    strip = 256
+    strips = width // strip
+    block = pl.BlockSpec
+    weight = lambda k: block((width, strip), lambda s: (0, k * strips + s))
+    return pl.pallas_call(
+        project_kernel,
+        grid=(strips,),
+        in_specs=[block((length, width), lambda s: (0, 0)), weight(0), weight(1), weight(2)],
+        out_specs=[
+            block((tokens, strip), lambda s: (0, s)),
+            block((length, strip), lambda s: (0, s)),
+            block((length, strip), lambda s: (0, s)),
+        ],
+        out_shape=[
+            jax.ShapeDtypeStruct((n, width), bf16) for n in (tokens, length, length)
+        ],
+        compiler_params=pltpu.CompilerParams(vmem_limit_bytes=48 * 2**20),
+        cost_estimate=pl.CostEstimate(
+            flops=2 * (tokens + 2 * length) * width * width,
+            bytes_accessed=6 * width * width + 6 * length * width,
+            transcendentals=0,
+        ),
+    )(rows, weights, weights, weights)
+
+
+def project_back_kernel(rows_ref, gq_ref, gvk_ref, w_ref, dq_ref, dk_ref, dv_ref, back_ref):
+    turned = rows_ref[...].T
+    width = gq_ref.shape[1]
+    total = None
+    for k, (grad, out) in enumerate(
+        ((gq_ref[...], dq_ref), (gvk_ref[1], dk_ref), (gvk_ref[0], dv_ref))
+    ):
+        out[...] = times(turned, grad).astype(bf16)
+        part = times_transposed(grad, w_ref[:, k * width : (k + 1) * width])
+        total = part if total is None else total + part
+    back_ref[...] = total
+
+
+def project_back(rows, gq, gvk, weights):
+    tokens, width = rows.shape
+    strip = 256
+    block = pl.BlockSpec
+    return pl.pallas_call(
+        project_back_kernel,
+        grid=(width // strip,),
+        in_specs=[
+            block((tokens, strip), lambda s: (0, s)),
+            block((tokens, width), lambda s: (0, 0)),
+            block((2, tokens, width), lambda s: (0, 0, 0)),
+            block((strip, 3 * width), lambda s: (s, 0)),
+        ],
+        out_specs=[block((strip, width), lambda s: (s, 0))] * 3
+        + [block((tokens, strip), lambda s: (0, s))],
+        out_shape=[jax.ShapeDtypeStruct((width, width), bf16)] * 3
+        + [jax.ShapeDtypeStruct((tokens, width), f32)],
+        compiler_params=pltpu.CompilerParams(vmem_limit_bytes=48 * 2**20),
+        cost_estimate=pl.CostEstimate(
+            flops=12 * tokens * width * width,
+            bytes_accessed=12 * width * width + 12 * tokens * width,
+            transcendentals=0,
+        ),
+    )(rows, gq, gvk, weights)
+
+
 def attention_kernel(q_ref, k_ref, v_ref, bias_ref, out_ref):
     scores = times_transposed(q_ref[...], k_ref[...]) * HD ** (-0.5) + bias_ref[...]
     weights = jnp.exp(scores - jnp.max(scores, axis=1, keepdims=True))
@@ -1264,9 +1337,7 @@
     group_rows = group_rows.reshape(-1, width)
     integers_all = integers_all.reshape(sources, top_count + 1, tok_rows)
     bundle_all = bundle_all.reshape(width, bundle.shape[1])
-    w_query, w_key, w_value, w_out = (
-        bundle_all[:, i * width : (i + 1) * width] for i in range(4)
-    )
+    w_out = bundle_all[:, 3 * width : 4 * width]
     small_all = bundle_all[:, 4 * width :]
     gather_all = lambda v: lax.all_gather(v, BOTH, axis=0, tiled=True)
     shared_in, shared_out_in, integers_all = lax.optimization_barrier(
@@ -1287,9 +1358,7 @@
     group_inputs = group_rows.astype(f32)
     normed_group = (group_inputs * norm_scale(group_inputs) * gain_one).astype(bf16)
     normed_one = normed_group[:tok_rows]
-    queries = times(normed_one, w_query).astype(bf16)
-    keys_all = times(normed_group, w_key).astype(bf16)
-    values_all = times(normed_group, w_value).astype(bf16)
+    queries, keys_all, values_all = project(normed_group, bundle_all, tok_rows)
     labels_all = integers_all[: nx * NC, top_count].reshape(-1)
     steps = jnp.arange(tok_rows, dtype=jnp.int32)
     block_places = (
@@ -1350,7 +1419,7 @@
     both_parts = None
     prob_parts = []
     for i in range(mine):
-        behind = (names[3 * i - 3 : 3 * i - 1], []) if i else ([], [])
+        behind = (names[:1], []) if i else ([], [])
         (both_parts, probs_here, *made), moved = run_expert(
             grid_of,
             5 + i,
@@ -1368,7 +1437,7 @@
         prob_parts.append(probs_here[:, 0])
         grads.update({(i, k): by_wide(v) for k, v in enumerate(made)})
     column.update({name: summed(name) for name in along_y})
-    behind = (names[2:4], names[:1])
+    behind = (names[1:3], names[:1])
     (
         sums,
         sent,
@@ -1430,7 +1499,7 @@
     output_weight_grad = contract_rows(attended, branch_grad)
     attended_grad = times_transposed(branch_grad, w_out).astype(bf16)
 
-    behind = (names[4:5], names[1:2])
+    behind = (names[3:4], names[1:2])
     query_act_grad, parts, moved = attention_backward(
         grid_of,
         1 + 8,
@@ -1442,7 +1511,8 @@
         *jobs_of(*behind),
     )
     landed(*behind, moved)
-    behind = (names[5:], names[2:4])
+    behind = (names[4:], names[2:4])
+    column.update({name: summed(name) for name in names[3:4]})
     ((value_key,), moved) = sum_around(
         grid_of,
         1,
@@ -1452,16 +1522,10 @@
         (),
         *jobs_of(*behind),
     )
-    value_act_grad, key_act_grad = value_key
     landed(*behind, moved)
     column.update({name: summed(name) for name in names[4:]})
-    query_w_grad = contract_rows(normed_one, query_act_grad)
-    key_w_grad = contract_rows(normed_one, key_act_grad)
-    value_w_grad = contract_rows(normed_one, value_act_grad)
-    normed_one_grad = (
-        times_transposed(query_act_grad, w_query)
-        + times_transposed(key_act_grad, w_key)
-        + times_transposed(value_act_grad, w_value)
+    query_w_grad, key_w_grad, value_w_grad, normed_one_grad = project_back(
+        normed_one, query_act_grad, value_key, bundle_all
     )
     gain_one_grad, input_part = norm_backward(
         inputs, inverse_one, gain_one, normed_one_grad

time: 640 us -> 622 us (0.972)
  matrix products: 55.8 us -> 20.4 us
  Pallas kernels: 500 us -> 512 us
    pallas_call x0 -> x2, Pallas kernels: none -> 21.3 us  [the longest x1 11.5 us: project(): pl.pallas_call(project_kernel, grid=(strips,), in_specs=[block((length, w...]
    dot_general x4 -> x1, matrix products: 21.3 us -> 3.03 us  [times(): return jnp.dot(left, right, preferred_element_type=f32)]
    pallas_call x2, Pallas kernels: 106 us -> 95 us  [run_expert(): pl.pallas_call(functools.partial(expert_kernel, grid_of, capacity, steps,...]
    dot_general x4 -> x1, matrix products: 14.1 us -> 3.44 us  [times_transposed(): lax.dot_general(left, right, (((1,), (1,)), ((), ())), preferred_element_...]
    dot_general x4 -> x1, matrix products: 11.1 us -> 2.8 us  [contract_rows(): lax.dot_general(left, right, (((0,), (0,)), ((), ())), preferred_element_...]
  transfers between devices with their start and end apart: 2 -> 2, of which waited for: 0 -> 0; matrix products, arithmetic and copies ran while one was open for 7% -> 6% of each run, Pallas kernels for 24% -> 25%
where the time goes in v5:
time: 622 us; the launch traced here: 615 us
  Pallas kernels  512 us (82%)
  other arithmetic  33.9 us (5%)
  local copies, waits for them, and re-layouts  32.9 us (5%)
  matrix products  20.4 us (3%)
  between operations  15.2 us (2%)
    pallas_call x2, Pallas kernels, sum_around(): pl.pallas_call(functools.partial(sum_kernel, grid_of, zp, cut, small, job...  119 us
    pallas_call x1, Pallas kernels, reduce_dense(): pl.pallas_call(functools.partial(dense_kernel, grid_of, orders, jobs, ite...  106 us
    pallas_call x2, Pallas kernels, run_expert(): pl.pallas_call(functools.partial(expert_kernel, grid_of, capacity, steps,...  95 us
    pallas_call x1, Pallas kernels, gather_first(): pl.pallas_call(functools.partial(gather_kernel, grid_of), out_shape=(jax....  87.8 us
    pallas_call x1, Pallas kernels, exchange(): pl.pallas_call(functools.partial(exchange_kernel, grid_of, zp, rows.shape...  36.7 us
    pallas_call x1, Pallas kernels, attention_backward(): pl.pallas_call(functools.partial(attention_back_kernel, grid_of, jobs), g...  29.7 us
  transfers between devices with their start and end apart: 2, of which 0 were waited for; matrix products, arithmetic and copies ran while one was open for 6% of the time, Pallas kernels for 25%

profile of v5, /device:TPU:0, one launch (start us, length us, event | category | flops | bytes accessed | tf_op | source)
XLA Modules:
  0.0 615.3 jit_solution(11456478417254087986)
XLA Ops:
  14.3 87.8 %shard_map.288 = (bf16[32,40,5248]{2,1,0:T(8,128)(2,1)}, bf16[2,2,256,1280]{3,2,1,0:T(8,128)(2,1)}, bf16[2,2,2,256,1280]{4,3,2,1,0:T(8,128)(2,1)}, s32[2,2,2,8,256]{4,3,2,1,0:T(8,128)}) custom-call(bf16[40,5248]{1,0:T(8,128)(2,1)} %concatenate.22.w_ref, bf16[256,1280]{1,0:T(8,128)(2,1)} %rows_ref.1, bf16[256,1280]{1,0:T(8,128)(2,1)} %refs_2_.1, ...), custom_call_target="tpu_custom_call" | custom-call | tf_op jit(solution)/shard_map/pallas_call | solution.py:360
  105.6 2.5 multiply_reduce_fusion
  110.3 11.5 %shard_map.289 = (bf16[256,1280]{1,0:T(8,128)(2,1)S(1)}, bf16[1024,1280]{1,0:T(8,128)(2,1)S(1)}, bf16[1024,1280]{1,0:T(8,128)(2,1)S(1)}) custom-call(bf16[1024,1280]{1,0:T(8,128)(2,1)} %fusion.2.rows_ref, bf16[1280,5248]{1,0:T(8,128)(2,1)} %bitcast.148, bf16[1280,5248]{1,0:T(8,128)(2,1)} %bitcast.149, bf16[1280,5248]{1,0:T(8,128)(2,1)} %bitcast.150), custom_call_target="tpu_custom_call" | custom-call | flops 7549747200 | bytes 17694720 | tf_op jit(solution)/shard_map/pallas_call | solution.py:662
  122.1 9.1 %shard_map.290 = bf16[256,1280]{1,0:T(8,128)(2,1)S(1)} custom-call(bf16[256,1280]{1,0:T(8,128)(2,1)S(1)} %get-tuple-element.83.q_ref, bf16[1024,1280]{1,0:T(8,128)(2,1)S(1)} %get-tuple-element.84.k_ref, bf16[1024,1280]{1,0:T(8,128)(2,1)S(1)} %get-tuple-element.85.v_ref, f32[256,1024]{1,0:T(8,128)S(1)} %and_select_fusion.1.bias_ref), custom_call_target="tpu_custom_call" | custom-call | flops 1342177280 | bytes 7602176 | tf_op jit(solution)/shard_map/pallas_call | solution.py:733
  131.2 3.0 multiply_reduce_fusion.3
  138.3 36.7 %shard_map.291 = bf16[2,2,2,256,1280]{4,3,2,1,0:T(8,128)(2,1)} custom-call(bf16[256,1280]{1,0:T(8,128)(2,1)} %multiply_convert_fusion.src.refs_1_), custom_call_target="tpu_custom_call" | custom-call | tf_op jit(solution)/shard_map/pallas_call | solution.py:461
  181.5 4.6 fusion.50
  187.5 46.4 %shard_map.292 = (bf16[2,8,256,1280]{3,2,1,0:T(8,128)(2,1)}, f32[8,1,256]{2,1,0:T(1,128)}, bf16[1280,896]{1,0:T(8,128)(2,1)}, bf16[1280,896]{1,0:T(8,128)(2,1)}, bf16[896,1280]{1,0:T(8,128)(2,1)}) custom-call(bf16[8,256,1280]{2,1,0:T(8,128)(2,1)} %bitcast.158, bf16[8,256,1280]{2,1,0:T(8,128)(2,1)} %bitcast.192, s32[8,1,256]{2,1,0:T(1,128)} %get-tuple-element.224.refs_2_, ...), custom_call_target="tpu_custom_call" | custom-call | flops 26424115200 | bytes 55705600 | tf_op jit(solution)/shard_map/pallas_call | solution.py:944
  233.9 48.6 %shard_map.293 = (bf16[2,8,256,1280]{3,2,1,0:T(8,128)(2,1)}, f32[8,1,256]{2,1,0:T(1,128)}, bf16[1280,896]{1,0:T(8,128)(2,1)}, bf16[1280,896]{1,0:T(8,128)(2,1)},...) custom-call(bf16[8,256,1280]{2,1,0:T(8,128)(2,1)} %bitcast.159, bf16[8,256,1280]{2,1,0:T(8,128)(2,1)} %bitcast.193, ...), custom_call_target="tpu_custom_call" | custom-call | flops 26424115200 | bytes 55705600 | tf_op jit(solution)/shard_map/pallas_call | solution.py:944
  286.1 2.5 fusion.18.refs_7_.refs_0_
  288.6 4.1 reshape.441.refs_4_
  292.7 66.0 %shard_map.294 = (bf16[2,256,1280]{2,1,0:T(8,128)(2,1)}, f32[2,2,2,2,256]{4,3,2,1,0:T(2,128)}, f32[256,1280]{1,0:T(8,128)}, f32[256,1280]{1,0:T(8,128)}, bf16[12...) custom-call(bf16[2,2,2,2,256,1280]{5,4,3,2,1,0:T(8,128)(2,1)} %bitca, ...), custom_call_target="tpu_custom_call" | custom-call | tf_op jit(solution)/shard_map/pallas_call | solution.py:609
  359.6 2.8 fusion.42
  362.5 3.5 multiply_reduce_fusion.1
  367.4 3.4 fusion.10.g_ref
  370.9 2.8 convolution_convert_fusion
  376.3 29.7 %shard_map.295 = (bf16[256,1280]{1,0:T(8,128)(2,1)S(1)}, bf16[2,1024,1280]{2,1,0:T(8,128)(2,1)}, bf16[1,4,160,896]{3,2,1,0:T(8,128)(2,1)S(1)}, bf16[3,160,896]{2,1,0:T(8,128)(2,1)S(1)}) custom-call(bf16[256,1280]{1,0:T(8,128)(2,1)S(1)} %copy-done.7, bf16[1024,1280]{1,0:T(8,128)(2,1)S(1)} %get-tuple-element.84.k_ref, bf16[1024,1280]{1,0:T(8,128)(2,1)S(1)} %copy-done.2, ...), custom_call_target="tpu_custom_call" | custom-call | flops 3355443200 | bytes 13500416 | tf_op jit(solution)/shard_map/pallas_call | solution.py:791
  410.1 53.3 %shard_map.296 = (bf16[2,256,1280]{2,1,0:T(8,128)(2,1)}, bf16[1,4,160,896]{3,2,1,0:T(8,128)(2,1)}, bf16[1,4,112,1280]{3,2,1,0:T(8,128)(2,1)}, bf16[3,112,1280]{2,1,0:T(8,128)(2,1)}, bf16[3,160,896]{2,1,0:T(8,128)(2,1)}) custom-call(bf16[2,1,2,2,256,1280]{5,4,3,2,1,0:T(8,128)(2,1)} %bitcast.161, bf16[4,2,160,896]{3,2,1,0:T(8,128)(2,1)} %bitcast.162, ...), custom_call_target="tpu_custom_call" | custom-call | tf_op jit(solution)/shard_map/pallas_call | solution.py:609
  464.8 9.8 %shard_map.297 = (bf16[1280,1280]{1,0:T(8,128)(2,1)}, bf16[1280,1280]{1,0:T(8,128)(2,1)}, bf16[1280,1280]{1,0:T(8,128)(2,1)}, f32[256,1280]{1,0:T(8,128)S(1)}) custom-call(bf16[256,1280]{1,0:T(8,128)(2,1)S(1)} %copy-done.5, bf16[256,1280]{1,0:T(8,128)(2,1)S(1)} %get-tuple-element.105.gq_ref, bf16[2,256,1280]{2,1,0:T(8,128)(2,1)S(1)} %copy-done.9, ...), custom_call_target="tpu_custom_call" | custom-call | flops 5033164800 | bytes 23592960 | tf_op jit(solution)/shard_map/pallas_call | solution.py:700
  476.9 3.1 fusion.13.refs_9_.refs_5_
  481.2 4.1 reshape.413.refs_1_
  487.8 106.3 %shard_map.298 = (bf16[2,40,1280]{2,1,0:T(8,128)(2,1)}, bf16[2,28,1280]{2,1,0:T(8,128)(2,1)}, bf16[2,40,896]{2,1,0:T(8,128)(2,1)}, bf16[2,40,896]{2,1,0:T(8,128)...) custom-call(bf16[4,2,2,2,40,1280]{5,4,3,2,1,0:T(8,128)(2,1)} %bitcas, ...), custom_call_target="tpu_custom_call" | custom-call | tf_op jit(solution)/shard_map/pallas_call | solution.py:1202
  594.1 7.0 %shard_map.299 = (f32[2,2,160,896]{3,2,1,0:T(8,128)}, f32[2,2,160,896]{3,2,1,0:T(8,128)}, f32[2,2,112,1280]{3,2,1,0:T(8,128)}, f32[40,1280]{1,0:T(8,128)}, f32[2...) custom-call(bf16[4,160,896]{2,1,0:T(8,128)(2,1)} %fusion.18.refs_7_., ...), custom_call_target="tpu_custom_call" | custom-call | tf_op jit(solution)/shard_map/pallas_call | solution.py:1262
  605.3 2.7 fusion.22
  (171 shorter events, 48.7 us)
Async XLA Ops:
  7.2 281.5 %all-gather.6.cloned.1.call-start = ((), (), s32[]{:S(2)}) async-start(), calls=%async_computation.1 | async-start | bytes 2703360 | tf_op jit(solution)/shard_map/all_gather | solution.py:1342
  102.2 190.5 %all-gather.4.cloned.1.call-start = ((), (), s32[]{:S(2)}) async-start(), calls=%async_computation | async-start | bytes 4730880 | tf_op jit(solution)/shard_map/all_gather | solution.py:1342
  103.2 18.6 %copy-start.30 = (s32[1,2,4,128]{3,1,2,0:T(2,128)}, s32[1,2,4,128]{3,1,2,0:T(2,128)S(1)}, u32[]{:S(2)}) copy-start(s32[1,2,4,128]{3,1,2,0:T(2,128)S(1)} %copy.116) | copy-start | bytes 12292
  103.2 18.6 %copy-start.45 = (s32[256]{0:T(256)}, s32[256]{0:T(256)S(1)}, u32[]{:S(2)}) copy-start(s32[256]{0:T(256)S(1)} %iota_add_fusion.1) | copy-start | bytes 3076
  104.0 17.8 %copy-start.32 = (s32[4,1,256]{2,1,0:T(1,128)}, s32[4,1,256]{2,1,0:T(1,128)S(1)}, u32[]{:S(2)}) copy-start(s32[4,1,256]{2,1,0:T(1,128)S(1)} %slice.59) | copy-start | bytes 12292
  110.3 11.6 %copy-start.39 = (s32[256]{0:T(256)S(1)}, s32[256]{0:T(256)}, u32[]{:S(2)}) copy-start(s32[256]{0:T(256)} %param.18) | copy-start | bytes 3076
  121.8 9.4 %copy-start.1 = (bf16[1024,1280]{1,0:T(8,128)(2,1)}, bf16[1024,1280]{1,0:T(8,128)(2,1)S(1)}, u32[]{:S(2)}) copy-start(bf16[1024,1280]{1,0:T(8,128)(2,1)S(1)} %get-tuple-element.85.v_ref) | copy-start | bytes 7864324
  121.8 9.4 %copy-start.6 = (bf16[256,1280]{1,0:T(8,128)(2,1)}, bf16[256,1280]{1,0:T(8,128)(2,1)S(1)}, u32[]{:S(2)}) copy-start(bf16[256,1280]{1,0:T(8,128)(2,1)S(1)} %get-tuple-element.83.q_ref) | copy-start | bytes 1966084
  122.1 9.1 %copy-start.13 = (bf16[256,1280]{1,0:T(8,128)(2,1)S(1)}, bf16[256,1280]{1,0:T(8,128)(2,1)}, u32[]{:S(2)}) copy-start(bf16[256,1280]{1,0:T(8,128)(2,1)} %rows_ref.1) | copy-start | bytes 1966084
  138.3 36.7 %copy-start.29 = (s32[2,2,2,8,256]{4,3,2,1,0:T(8,128)S(1)}, s32[2,2,2,8,256]{4,3,2,1,0:T(8,128)}, u32[]{:S(2)}) copy-start(s32[2,2,2,8,256]{4,3,2,1,0:T(8,128)} %get-tuple-element.86) | copy-start | bytes 196612
  175.0 4.4 copy-start.35
  233.9 48.7 %copy-start.42 = (f32[8,1,256]{2,1,0:T(1,128)S(1)}, f32[8,1,256]{2,1,0:T(1,128)}, u32[]{:S(2)}) copy-start(f32[8,1,256]{2,1,0:T(1,128)} %get-tuple-element.92) | copy-start | bytes 24580
  233.9 50.1 %copy-start.14 = (bf16[256,1280]{1,0:T(8,128)(2,1)S(1)}, bf16[256,1280]{1,0:T(8,128)(2,1)}, u32[]{:S(2)}) copy-start(bf16[256,1280]{1,0:T(8,128)(2,1)} %rows_ref.1) | copy-start | bytes 1966084
  233.9 50.3 %copy-start.47 = (s32[16]{0:T(128)S(1)}, s32[16]{0:T(128)}, u32[]{:S(2)}) copy-start(s32[16]{0:T(128)} %add.313) | copy-start | bytes 196
  233.9 50.9 %copy-start.31 = (s32[1,2,4,128]{3,1,2,0:T(2,128)S(1)}, s32[1,2,4,128]{3,1,2,0:T(2,128)}, u32[]{:S(2)}) copy-start(s32[1,2,4,128]{3,1,2,0:T(2,128)} %copy-done.30) | copy-start | bytes 12292
  233.9 50.8 %copy-start.33 = (s32[4,1,256]{2,1,0:T(1,128)S(1)}, s32[4,1,256]{2,1,0:T(1,128)}, u32[]{:S(2)}) copy-start(s32[4,1,256]{2,1,0:T(1,128)} %copy-done.32) | copy-start | bytes 12292
  233.9 50.8 %copy-start.40 = (s32[256]{0:T(256)S(1)}, s32[256]{0:T(256)}, u32[]{:S(2)}) copy-start(s32[256]{0:T(256)} %param.18) | copy-start | bytes 3076
  233.9 50.8 %copy-start.46 = (s32[256]{0:T(256)S(1)}, s32[256]{0:T(256)}, u32[]{:S(2)}) copy-start(s32[256]{0:T(256)} %copy-done.45) | copy-start | bytes 3076
  374.0 32.1 %copy-start = (bf16[4,160,896]{2,1,0:T(8,128)(2,1)}, bf16[4,160,896]{2,1,0:T(8,128)(2,1)S(1)}, u32[]{:S(2)}) copy-start(bf16[4,160,896]{2,1,0:T(8,128)(2,1)S(1)} %fusion.17.refs_1_) | copy-start | bytes 3440644
  410.1 53.3 %copy-start.5 = (bf16[256,1280]{1,0:T(8,128)(2,1)S(1)}, bf16[256,1280]{1,0:T(8,128)(2,1)}, u32[]{:S(2)}) copy-start(bf16[256,1280]{1,0:T(8,128)(2,1)} %slice.85.rows_ref) | copy-start | bytes 1966084
  464.8 9.8 %copy-start.15 = (bf16[256,1280]{1,0:T(8,128)(2,1)S(1)}, bf16[256,1280]{1,0:T(8,128)(2,1)}, u32[]{:S(2)}) copy-start(bf16[256,1280]{1,0:T(8,128)(2,1)} %rows_ref.1) | copy-start | bytes 1966084
  464.8 9.8 %copy-start.38 = (f32[256]{0:T(256)S(1)}, f32[256]{0:T(256)}, u32[]{:S(2)}) copy-start(f32[256]{0:T(256)} %get-tuple-element.227) | copy-start | bytes 3076
  481.2 4.2 copy-start.48
  594.1 11.1 %copy-start.44 = (f32[256]{0:T(256)S(1)}, f32[256]{0:T(256)}, u32[]{:S(2)}) copy-start(f32[256]{0:T(256)} %get-tuple-element.226) | copy-start | bytes 3076
  (27 other events, 78.5 us)
Sparse Core Ops, SparseCore 0:
  102.3 60.4 all-gather.5
  166.2 63.6 all-gather.3

commit v6 on v5

--- a/solution.py
+++ b/solution.py
@@ -694,7 +694,7 @@
 
 
 def project_back(rows, gq, gvk, weights):
-    tokens, width = rows.shape
+    tokens, width = gq.shape
     strip = 256
     block = pl.BlockSpec
     return pl.pallas_call(
@@ -750,13 +750,15 @@
     )(queries, keys, values, bias)
 
 
-def attention_back_kernel(grid_of, jobs, q_ref, k_ref, v_ref, g_ref, bias_ref, *refs):
+def attention_back_kernel(
+    grid_of, jobs, q_ref, k_ref, v_ref, branch_ref, wo_ref, out_ref, bias_ref, *refs
+):
     grid = grid_of()
     count = len(jobs)
-    dq_ref, parts_ref = refs[count : count + 2]
+    dq_ref, parts_ref, dwo_ref = refs[count : count + 3]
     job_send, job_recv = refs[-2:]
     each = functools.partial(
-        each_job, grid, jobs, refs[:count], refs[count + 2 : -2], job_send, job_recv
+        each_job, grid, jobs, refs[:count], refs[count + 3 : -2], job_send, job_recv
     )
     if jobs:
 
@@ -765,7 +767,9 @@
             greet(job_targets(grid, jobs))
             each(lambda copy: copy.start())
 
-    q, k, g = q_ref[...], k_ref[...], g_ref[...]
+    q, k, branch = q_ref[...], k_ref[...], branch_ref[...]
+    g = times_transposed(branch, wo_ref[...]).astype(bf16)
+    dwo_ref[...] = times(out_ref[...].T, branch).astype(bf16)
     scores = times_transposed(k, q) * HD ** (-0.5) + bias_ref[...]
     weights = jnp.exp(scores - jnp.max(scores, axis=0, keepdims=True))
     probs = weights * (1.0 / jnp.sum(weights, axis=0, keepdims=True))
@@ -782,11 +786,14 @@
             each(lambda copy: copy.wait())
 
 
-def attention_backward(grid_of, number, queries, keys, values, grads, bias, jobs, job_arrays):
+def attention_backward(
+    grid_of, number, queries, keys, values, branch, weights, attended, bias, jobs, job_arrays
+):
     grid = grid_of()
     rows, width = queries.shape
     length = keys.shape[0]
     by_head = lambda n: pl.BlockSpec((n, HD), lambda h: (0, h))
+    whole = lambda *shape: pl.BlockSpec(shape, lambda h: (0, 0))
     anywhere = pl.BlockSpec(memory_space=pl.ANY)
     made = pl.pallas_call(
         functools.partial(attention_back_kernel, grid_of, jobs),
@@ -795,6 +802,7 @@
             [
                 jax.ShapeDtypeStruct((rows, width), bf16),
                 jax.ShapeDtypeStruct((2, length, width), bf16),
+                jax.ShapeDtypeStruct((width, width), bf16),
             ]
             + job_shapes(grid, jobs, job_arrays)
         ),
@@ -802,11 +810,17 @@
             by_head(rows),
             by_head(length),
             by_head(length),
+            whole(rows, width),
+            pl.BlockSpec((HD, width), lambda h: (h, 3)),
             by_head(rows),
-            pl.BlockSpec((length, rows), lambda h: (0, 0)),
+            whole(length, rows),
         ]
         + [anywhere] * len(jobs),
-        out_specs=(by_head(rows), pl.BlockSpec((2, length, HD), lambda h: (0, 0, h)))
+        out_specs=(
+            by_head(rows),
+            pl.BlockSpec((2, length, HD), lambda h: (0, 0, h)),
+            pl.BlockSpec((HD, width), lambda h: (h, 0)),
+        )
         + (anywhere,) * len(jobs),
         scratch_shapes=job_sems(grid, jobs),
         compiler_params=pltpu.CompilerParams(
@@ -814,12 +828,12 @@
             **(dict(collective_id=number, has_side_effects=True) if jobs else {}),
         ),
         cost_estimate=pl.CostEstimate(
-            flops=10 * rows * length * width,
-            bytes_accessed=6 * rows * width + 8 * length * width + 4 * rows * length,
+            flops=10 * rows * length * width + 4 * rows * width * width,
+            bytes_accessed=8 * rows * width + 8 * length * width + 4 * rows * length,
             transcendentals=rows * length * width // HD,
         ),
-    )(queries, keys, values, grads, bias, *job_arrays)
-    return made[0], made[1], made[2:]
+    )(queries, keys, values, branch, weights, attended, bias, *job_arrays)
+    return made[0], made[1], made[2], made[3:]
 
 
 ROW_SOURCES = 2
@@ -1496,17 +1510,17 @@
     )
     middle_grad = out_grad + middle_part
     branch_grad = middle_grad.astype(bf16)
-    output_weight_grad = contract_rows(attended, branch_grad)
-    attended_grad = times_transposed(branch_grad, w_out).astype(bf16)
 
     behind = (names[3:4], names[1:2])
-    query_act_grad, parts, moved = attention_backward(
+    query_act_grad, parts, output_weight_grad, moved = attention_backward(
         grid_of,
         1 + 8,
         queries,
         keys_all,
         values_all,
-        attended_grad,
+        branch_grad,
+        bundle_all,
+        attended,
         bias.T,
         *jobs_of(*behind),
     )
@@ -1525,7 +1539,7 @@
     landed(*behind, moved)
     column.update({name: summed(name) for name in names[4:]})
     query_w_grad, key_w_grad, value_w_grad, normed_one_grad = project_back(
-        normed_one, query_act_grad, value_key, bundle_all
+        normed_group, query_act_grad, value_key, bundle_all
     )
     gain_one_grad, input_part = norm_backward(
         inputs, inverse_one, gain_one, normed_one_grad

time: 622 us -> 616 us (level)
  matrix products: 20.4 us -> 13.7 us
    dot_general x2 -> x0, matrix products: 6.25 us -> none  [the longest x1 3.44 us: times_transposed(): lax.dot_general(left, right, (((1,), (1,)), ((), ())), preferred_element_...]
where the time goes in v6:
time: 616 us; the launch traced here: 609 us
  Pallas kernels  513 us (83%)
  other arithmetic  36.1 us (6%)
  local copies, waits for them, and re-layouts  30.5 us (5%)
  between operations  14.9 us (2%)
  matrix products  13.7 us (2%)
    pallas_call x2, Pallas kernels, sum_around(): pl.pallas_call(functools.partial(sum_kernel, grid_of, zp, cut, small, job...  119 us
    pallas_call x1, Pallas kernels, reduce_dense(): pl.pallas_call(functools.partial(dense_kernel, grid_of, orders, jobs, ite...  106 us
    pallas_call x2, Pallas kernels, run_expert(): pl.pallas_call(functools.partial(expert_kernel, grid_of, capacity, steps,...  95.2 us
    pallas_call x1, Pallas kernels, gather_first(): pl.pallas_call(functools.partial(gather_kernel, grid_of), out_shape=(jax....  87.8 us
    pallas_call x1, Pallas kernels, exchange(): pl.pallas_call(functools.partial(exchange_kernel, grid_of, zp, rows.shape...  36.6 us
    pallas_call x1, Pallas kernels, attention_backward(): pl.pallas_call(functools.partial(attention_back_kernel, grid_of, jobs), g...  30.2 us
  transfers between devices with their start and end apart: 2, of which 0 were waited for; matrix products, arithmetic and copies ran while one was open for 6% of the time, Pallas kernels for 25%

profile of v6, /device:TPU:0, one launch (start us, length us, event | category | flops | bytes accessed | tf_op | source)
XLA Modules:
  0.0 608.8 jit_solution(13684308260904882457)
XLA Ops:
  14.3 87.8 %shard_map.288 = (bf16[32,40,5248]{2,1,0:T(8,128)(2,1)}, bf16[2,2,256,1280]{3,2,1,0:T(8,128)(2,1)}, bf16[2,2,2,256,1280]{4,3,2,1,0:T(8,128)(2,1)}, s32[2,2,2,8,256]{4,3,2,1,0:T(8,128)}) custom-call(bf16[40,5248]{1,0:T(8,128)(2,1)} %concatenate.22.w_ref, bf16[256,1280]{1,0:T(8,128)(2,1)} %rows_ref.1, bf16[256,1280]{1,0:T(8,128)(2,1)} %refs_2_.1, ...), custom_call_target="tpu_custom_call" | custom-call | tf_op jit(solution)/shard_map/pallas_call | solution.py:360
  105.6 2.5 multiply_reduce_fusion
  108.1 2.1 fusion.2.rows_ref
  110.2 11.5 %shard_map.289 = (bf16[256,1280]{1,0:T(8,128)(2,1)S(1)}, bf16[1024,1280]{1,0:T(8,128)(2,1)S(1)}, bf16[1024,1280]{1,0:T(8,128)(2,1)S(1)}) custom-call(bf16[1024,1280]{1,0:T(8,128)(2,1)} %fusion.2.rows_ref, bf16[1280,5248]{1,0:T(8,128)(2,1)} %bitcast.147, bf16[1280,5248]{1,0:T(8,128)(2,1)} %bitcast.148, bf16[1280,5248]{1,0:T(8,128)(2,1)} %bitcast.149), custom_call_target="tpu_custom_call" | custom-call | flops 7549747200 | bytes 17694720 | tf_op jit(solution)/shard_map/pallas_call | solution.py:662
  122.0 9.1 %shard_map.290.out_ref = bf16[256,1280]{1,0:T(8,128)(2,1)S(1)} custom-call(bf16[256,1280]{1,0:T(8,128)(2,1)S(1)} %get-tuple-element.84.q_ref, bf16[1024,1280]{1,0:T(8,128)(2,1)S(1)} %get-tuple-element.85.k_ref, bf16[1024,1280]{1,0:T(8,128)(2,1)S(1)} %get-tuple-element.86.v_ref, f32[256,1024]{1,0:T(8,128)S(1)} %and_select_fusion.1.bias_ref), custom_call_target="tpu_custom_call" | custom-call | flops 1342177280 | bytes 7602176 | tf_op jit(solution)/shard_map/pallas_call | solution.py:733
  131.1 3.3 multiply_reduce_fusion.3
  136.4 36.6 %shard_map.291 = bf16[2,2,2,256,1280]{4,3,2,1,0:T(8,128)(2,1)} custom-call(bf16[256,1280]{1,0:T(8,128)(2,1)} %multiply_convert_fusion.src.refs_1_), custom_call_target="tpu_custom_call" | custom-call | tf_op jit(solution)/shard_map/pallas_call | solution.py:461
  179.6 4.6 fusion.44
  185.6 46.2 %shard_map.292 = (bf16[2,8,256,1280]{3,2,1,0:T(8,128)(2,1)}, f32[8,1,256]{2,1,0:T(1,128)}, bf16[1280,896]{1,0:T(8,128)(2,1)}, bf16[1280,896]{1,0:T(8,128)(2,1)}, bf16[896,1280]{1,0:T(8,128)(2,1)}) custom-call(bf16[8,256,1280]{2,1,0:T(8,128)(2,1)} %bitcast.156, bf16[8,256,1280]{2,1,0:T(8,128)(2,1)} %bitcast.191, s32[8,1,256]{2,1,0:T(1,128)} %get-tuple-element.227.refs_2_, ...), custom_call_target="tpu_custom_call" | custom-call | flops 26424115200 | bytes 55705600 | tf_op jit(solution)/shard_map/pallas_call | solution.py:958
  231.9 49.0 %shard_map.293 = (bf16[2,8,256,1280]{3,2,1,0:T(8,128)(2,1)}, f32[8,1,256]{2,1,0:T(1,128)}, bf16[1280,896]{1,0:T(8,128)(2,1)}, bf16[1280,896]{1,0:T(8,128)(2,1)},...) custom-call(bf16[8,256,1280]{2,1,0:T(8,128)(2,1)} %bitcast.157, bf16[8,256,1280]{2,1,0:T(8,128)(2,1)} %bitcast.192, ...), custom_call_target="tpu_custom_call" | custom-call | flops 26424115200 | bytes 55705600 | tf_op jit(solution)/shard_map/pallas_call | solution.py:958
  284.6 2.5 fusion.13.refs_7_.refs_0_
  287.1 4.1 reshape.441.refs_4_
  291.2 65.8 %shard_map.294 = (bf16[2,256,1280]{2,1,0:T(8,128)(2,1)}, f32[2,2,2,2,256]{4,3,2,1,0:T(2,128)}, f32[256,1280]{1,0:T(8,128)}, f32[256,1280]{1,0:T(8,128)}, bf16[12...) custom-call(bf16[2,2,2,2,256,1280]{5,4,3,2,1,0:T(8,128)(2,1)} %bitca, ...), custom_call_target="tpu_custom_call" | custom-call | tf_op jit(solution)/shard_map/pallas_call | solution.py:609
  357.9 2.8 fusion.35
  363.1 2.8 multiply_reduce_fusion.1
  369.6 30.2 %shard_map.295 = (bf16[256,1280]{1,0:T(8,128)(2,1)S(1)}, bf16[2,1024,1280]{2,1,0:T(8,128)(2,1)}, bf16[1280,1280]{1,0:T(8,128)(2,1)}, bf16[1,4,160,896]{3,2,1,0:T(8,128)(2,1)S(1)}, bf16[3,160,896]{2,1,0:T(8,128)(2,1)S(1)}) custom-call(bf16[256,1280]{1,0:T(8,128)(2,1)S(1)} %get-tuple-element.84.q_ref, bf16[1024,1280]{1,0:T(8,128)(2,1)S(1)} %get-tuple-element.85.k_ref, ...), custom_call_target="tpu_custom_call" | custom-call | flops 5033164800 | bytes 14155776 | tf_op jit(solution)/shard_map/pallas_call | solution.py:798
  403.7 53.5 %shard_map.296 = (bf16[2,256,1280]{2,1,0:T(8,128)(2,1)}, bf16[1,4,160,896]{3,2,1,0:T(8,128)(2,1)}, bf16[1,4,112,1280]{3,2,1,0:T(8,128)(2,1)}, bf16[3,112,1280]{2,1,0:T(8,128)(2,1)}, bf16[3,160,896]{2,1,0:T(8,128)(2,1)}) custom-call(bf16[2,1,2,2,256,1280]{5,4,3,2,1,0:T(8,128)(2,1)} %bitcast.159, bf16[4,2,160,896]{3,2,1,0:T(8,128)(2,1)} %bitcast.160, ...), custom_call_target="tpu_custom_call" | custom-call | tf_op jit(solution)/shard_map/pallas_call | solution.py:609
  458.5 10.0 %shard_map.297 = (bf16[1280,1280]{1,0:T(8,128)(2,1)}, bf16[1280,1280]{1,0:T(8,128)(2,1)}, bf16[1280,1280]{1,0:T(8,128)(2,1)}, f32[256,1280]{1,0:T(8,128)S(1)}) custom-call(bf16[1024,1280]{1,0:T(8,128)(2,1)S(1)} %copy-done.2, bf16[256,1280]{1,0:T(8,128)(2,1)S(1)} %get-tuple-element.106.gq_ref, bf16[2,256,1280]{2,1,0:T(8,128)(2,1)S(1)} %copy-done.9, ...), custom_call_target="tpu_custom_call" | custom-call | flops 5033164800 | bytes 23592960 | tf_op jit(solution)/shard_map/pallas_call | solution.py:700
  470.8 3.0 fusion.8.refs_9_.refs_5_
  475.1 4.2 reshape.413.refs_1_
  479.3 2.4 fusion.24
  481.7 106.1 %shard_map.298 = (bf16[2,40,1280]{2,1,0:T(8,128)(2,1)}, bf16[2,28,1280]{2,1,0:T(8,128)(2,1)}, bf16[2,40,896]{2,1,0:T(8,128)(2,1)}, bf16[2,40,896]{2,1,0:T(8,128)...) custom-call(bf16[4,2,2,2,40,1280]{5,4,3,2,1,0:T(8,128)(2,1)} %bitcas, ...), custom_call_target="tpu_custom_call" | custom-call | tf_op jit(solution)/shard_map/pallas_call | solution.py:1216
  587.9 7.0 %shard_map.299 = (f32[2,2,160,896]{3,2,1,0:T(8,128)}, f32[2,2,160,896]{3,2,1,0:T(8,128)}, f32[2,2,112,1280]{3,2,1,0:T(8,128)}, f32[40,1280]{1,0:T(8,128)}, f32[2...) custom-call(bf16[4,160,896]{2,1,0:T(8,128)(2,1)} %fusion.13.refs_7_., ...), custom_call_target="tpu_custom_call" | custom-call | tf_op jit(solution)/shard_map/pallas_call | solution.py:1276
  599.0 2.7 fusion.17
  (164 shorter events, 44.0 us)
Async XLA Ops:
  7.2 280.0 %all-gather.6.cloned.1.call-start = ((), (), s32[]{:S(2)}) async-start(), calls=%async_computation.1 | async-start | bytes 2703360 | tf_op jit(solution)/shard_map/all_gather | solution.py:1356
  102.2 189.0 %all-gather.4.cloned.1.call-start = ((), (), s32[]{:S(2)}) async-start(), calls=%async_computation | async-start | bytes 4730880 | tf_op jit(solution)/shard_map/all_gather | solution.py:1356
  103.2 18.5 %copy-start.28 = (s32[1,2,4,128]{3,1,2,0:T(2,128)}, s32[1,2,4,128]{3,1,2,0:T(2,128)S(1)}, u32[]{:S(2)}) copy-start(s32[1,2,4,128]{3,1,2,0:T(2,128)S(1)} %copy.116) | copy-start | bytes 12292
  103.2 18.5 %copy-start.42 = (s32[256]{0:T(256)}, s32[256]{0:T(256)S(1)}, u32[]{:S(2)}) copy-start(s32[256]{0:T(256)S(1)} %iota_add_fusion.1) | copy-start | bytes 3076
  104.0 17.8 %copy-start.30 = (s32[4,1,256]{2,1,0:T(1,128)}, s32[4,1,256]{2,1,0:T(1,128)S(1)}, u32[]{:S(2)}) copy-start(s32[4,1,256]{2,1,0:T(1,128)S(1)} %slice.56) | copy-start | bytes 12292
  110.2 11.5 %copy-start.37 = (s32[256]{0:T(256)S(1)}, s32[256]{0:T(256)}, u32[]{:S(2)}) copy-start(s32[256]{0:T(256)} %param.18) | copy-start | bytes 3076
  121.7 9.3 %copy-start = (bf16[1024,1280]{1,0:T(8,128)(2,1)}, bf16[1024,1280]{1,0:T(8,128)(2,1)S(1)}, u32[]{:S(2)}) copy-start(bf16[1024,1280]{1,0:T(8,128)(2,1)S(1)} %get-tuple-element.86.v_ref) | copy-start | bytes 7864324
  122.0 9.1 %copy-start.12 = (bf16[256,1280]{1,0:T(8,128)(2,1)S(1)}, bf16[256,1280]{1,0:T(8,128)(2,1)}, u32[]{:S(2)}) copy-start(bf16[256,1280]{1,0:T(8,128)(2,1)} %rows_ref.1) | copy-start | bytes 1966084
  136.4 36.7 %copy-start.27 = (s32[2,2,2,8,256]{4,3,2,1,0:T(8,128)S(1)}, s32[2,2,2,8,256]{4,3,2,1,0:T(8,128)}, u32[]{:S(2)}) copy-start(s32[2,2,2,8,256]{4,3,2,1,0:T(8,128)} %get-tuple-element.87) | copy-start | bytes 196612
  173.1 4.4 copy-start.33
  231.9 49.1 %copy-start.40 = (f32[8,1,256]{2,1,0:T(1,128)S(1)}, f32[8,1,256]{2,1,0:T(1,128)}, u32[]{:S(2)}) copy-start(f32[8,1,256]{2,1,0:T(1,128)} %get-tuple-element.93) | copy-start | bytes 24580
  231.9 50.5 %copy-start.13 = (bf16[256,1280]{1,0:T(8,128)(2,1)S(1)}, bf16[256,1280]{1,0:T(8,128)(2,1)}, u32[]{:S(2)}) copy-start(bf16[256,1280]{1,0:T(8,128)(2,1)} %rows_ref.1) | copy-start | bytes 1966084
  231.9 50.7 %copy-start.45 = (s32[16]{0:T(128)S(1)}, s32[16]{0:T(128)}, u32[]{:S(2)}) copy-start(s32[16]{0:T(128)} %add.313) | copy-start | bytes 196
  231.9 51.3 %copy-start.29 = (s32[1,2,4,128]{3,1,2,0:T(2,128)S(1)}, s32[1,2,4,128]{3,1,2,0:T(2,128)}, u32[]{:S(2)}) copy-start(s32[1,2,4,128]{3,1,2,0:T(2,128)} %copy-done.28) | copy-start | bytes 12292
  231.9 51.3 %copy-start.31 = (s32[4,1,256]{2,1,0:T(1,128)S(1)}, s32[4,1,256]{2,1,0:T(1,128)}, u32[]{:S(2)}) copy-start(s32[4,1,256]{2,1,0:T(1,128)} %copy-done.30) | copy-start | bytes 12292
  231.9 51.3 %copy-start.38 = (s32[256]{0:T(256)S(1)}, s32[256]{0:T(256)}, u32[]{:S(2)}) copy-start(s32[256]{0:T(256)} %param.18) | copy-start | bytes 3076
  231.9 51.3 %copy-start.43 = (s32[256]{0:T(256)S(1)}, s32[256]{0:T(256)}, u32[]{:S(2)}) copy-start(s32[256]{0:T(256)} %copy-done.42) | copy-start | bytes 3076
  357.9 4.9 copy-start.21
  362.8 5.0 copy-start.3
  403.7 53.5 %copy-start.2 = (bf16[1024,1280]{1,0:T(8,128)(2,1)S(1)}, bf16[1024,1280]{1,0:T(8,128)(2,1)}, u32[]{:S(2)}) copy-start(bf16[1024,1280]{1,0:T(8,128)(2,1)} %fusion.2.rows_ref) | copy-start | bytes 7864324
  458.5 10.0 %copy-start.14 = (bf16[256,1280]{1,0:T(8,128)(2,1)S(1)}, bf16[256,1280]{1,0:T(8,128)(2,1)}, u32[]{:S(2)}) copy-start(bf16[256,1280]{1,0:T(8,128)(2,1)} %rows_ref.1) | copy-start | bytes 1966084
  458.5 10.0 %copy-start.36 = (f32[256]{0:T(256)S(1)}, f32[256]{0:T(256)}, u32[]{:S(2)}) copy-start(f32[256]{0:T(256)} %get-tuple-element.230) | copy-start | bytes 3076
  475.1 4.2 copy-start.46
  587.8 11.1 %copy-start.41 = (f32[256]{0:T(256)S(1)}, f32[256]{0:T(256)}, u32[]{:S(2)}) copy-start(f32[256]{0:T(256)} %get-tuple-element.229) | copy-start | bytes 3076
  (25 other events, 67.0 us)
Sparse Core Ops, SparseCore 0:
  102.3 60.5 all-gather.5
  166.3 62.7 all-gather.3

commit v7 on v6

--- a/solution.py
+++ b/solution.py
@@ -162,7 +162,11 @@
 
 def gather_kernel(
     grid_of,
-    w_ref,
+    wq_ref,
+    wk_ref,
+    wv_ref,
+    wo_ref,
+    rest_ref,
     rows_ref,
     cot_ref,
     ints_ref,
@@ -182,6 +186,7 @@
     x_out,
     y_out,
     c_out,
+    piece_sem,
 ):
     grid = grid_of()
     z, y, x, c, nx, ny = grid.z, grid.y, grid.x, grid.c, grid.nx, grid.ny
@@ -199,6 +204,16 @@
     back = lambda d: (nx - d) % nx
     other = (c + 1) % NC
     to = functools.partial(stepped, grid, ZP)
+    mine = block(0, 0, 0, c)
+    pieces, low = [], 0
+    for n, piece in enumerate((wq_ref, wk_ref, wv_ref, wo_ref, rest_ref)):
+        wide = piece.shape[1]
+        pieces.append(
+            pltpu.make_async_copy(piece, mine.at[:, pl.ds(low, wide)], piece_sem.at[n])
+        )
+        low += wide
+    for copy in pieces:
+        copy.start()
     greet(
         [device(shift_z(d), y, x, c) for d in range(1, NZ)]
         + [device(z, shift_y(d), x, c) for d in range(1, ny)]
@@ -206,7 +221,6 @@
     )
     send = Sender(send_sem)
     locals_ = [
-        (w_ref, block(0, 0, 0, c)),
         (rows_ref, rows_all.at[0, 0]),
         (cot_ref, cot_all.at[0, 0, 0]),
         (ints_ref, ints_all.at[0, 0, 0]),
@@ -217,6 +231,8 @@
     ]
     for copy in locals_:
         copy.start()
+    for copy in pieces:
+        copy.wait()
     def start(src, dst, out_sem, in_sem, target):
         pltpu.make_async_remote_copy(
             src_ref=src,
@@ -237,7 +253,7 @@
 
     def pass_on(way, d, dz):
         here = block(dz, 0, 0, c)
-        src = here if d else w_ref
+        src = here
         if d:
             arrived(here, z_in.at[way, d])
         if d < NZ - 1:
@@ -337,35 +353,38 @@
 
             @pl.when(z < NZ - 1 if way == 0 else z > 0)
             def _():
-                arrived(w_ref, z_out.at[way, d])
+                arrived(mine, z_out.at[way, d])
 
     each_source(sent)
     for dz in range(NZ):
         for b in range(1, nx):
-            arrived(w_ref, x_out.at[dz, b])
+            arrived(mine, x_out.at[dz, b])
         for dx in range(nx):
             for b in range(1, ny):
-                arrived(w_ref, y_out.at[dz, dx, b])
-            arrived(w_ref, c_out.at[dz, dx])
-
-
-def gather_first(grid_of, w, rows, cot, ints):
+                arrived(mine, y_out.at[dz, dx, b])
+            arrived(mine, c_out.at[dz, dx])
+
+
+def gather_first(grid_of, weights, rows, cot, ints):
     grid = grid_of()
     nx, ny = grid.nx, grid.ny
     places = NZ * ny * nx * NC
     octet = ZP * nx * NC
+    rest = weights[0].shape[0]
     sends = (NZ - 1) + NZ * (nx + ny) + 2 * nx + octet * 4 + NZ * nx * ny * (ny + 1)
     anywhere = pl.BlockSpec(memory_space=pl.ANY)
     dma = pltpu.SemaphoreType.DMA
     return pl.pallas_call(
         functools.partial(gather_kernel, grid_of),
         out_shape=(
-            jax.ShapeDtypeStruct((places,) + w.shape, w.dtype),
+            jax.ShapeDtypeStruct(
+                (places, rest, sum(w.shape[1] for w in weights)), weights[0].dtype
+            ),
             jax.ShapeDtypeStruct((nx, NC) + rows.shape, rows.dtype),
             jax.ShapeDtypeStruct((ZP, nx, NC) + cot.shape, cot.dtype),
             jax.ShapeDtypeStruct((ZP, nx, NC) + ints.shape, ints.dtype),
         ),
-        in_specs=[anywhere] * 4,
+        in_specs=[anywhere] * 8,
         out_specs=(anywhere,) * 4,
         scratch_shapes=[
             dma((NZ, ny, nx)),
@@ -380,9 +399,10 @@
             dma((NZ, nx)),
             dma((NZ, nx, ny)),
             dma((NZ, nx)),
+            dma((5,)),
         ],
         compiler_params=pltpu.CompilerParams(collective_id=0, has_side_effects=True),
-    )(w, rows, cot, ints)
+    )(*weights, rows, cot, ints)
 
 
 def shared_compute(n2, cot, w_in, w_down, out, back, dg, du, dd, h, ag, au):
@@ -1331,12 +1351,8 @@
     sources = ZP * nx * NC
     capacity = min((tok_rows * top_count * 10 // (7 * experts) + 7) // 8 * 8, tok_rows)
 
-    bundle = jnp.concatenate(
+    rest = jnp.concatenate(
         [
-            query_weight,
-            key_weight,
-            value_weight,
-            output_weight,
             router_weight,
             gain_attention[:, None],
             gain_experts[:, None],
@@ -1344,13 +1360,14 @@
         ],
         axis=1,
     )
+    bundle = (query_weight, key_weight, value_weight, output_weight, rest)
     integers = jnp.concatenate([routes.T, segment[None, :]], axis=0)
     bundle_all, group_rows, cot_all, integers_all = gather_first(
         grid_of, bundle, activations, cotangent, integers
     )
     group_rows = group_rows.reshape(-1, width)
     integers_all = integers_all.reshape(sources, top_count + 1, tok_rows)
-    bundle_all = bundle_all.reshape(width, bundle.shape[1])
+    bundle_all = bundle_all.reshape(width, bundle_all.shape[2])
     w_out = bundle_all[:, 3 * width : 4 * width]
     small_all = bundle_all[:, 4 * width :]
     gather_all = lambda v: lax.all_gather(v, BOTH, axis=0, tiled=True)

time: 616 us -> 627 us (1.018)
  Pallas kernels: 513 us -> 525 us
    pallas_call x1, Pallas kernels: 87.8 us -> 100 us  [gather_first(): pl.pallas_call(functools.partial(gather_kernel, grid_of), out_shape=(jax....]
where the time goes in v7:
time: 627 us; the launch traced here: 620 us
  Pallas kernels  525 us (84%)
  other arithmetic  36.8 us (6%)
  local copies, waits for them, and re-layouts  28.7 us (5%)
  between operations  14.9 us (2%)
  matrix products  13.7 us (2%)
    pallas_call x2, Pallas kernels, sum_around(): pl.pallas_call(functools.partial(sum_kernel, grid_of, zp, cut, small, job...  119 us
    pallas_call x1, Pallas kernels, reduce_dense(): pl.pallas_call(functools.partial(dense_kernel, grid_of, orders, jobs, ite...  107 us
    pallas_call x1, Pallas kernels, gather_first(): pl.pallas_call(functools.partial(gather_kernel, grid_of), out_shape=(jax....  100 us
    pallas_call x2, Pallas kernels, run_expert(): pl.pallas_call(functools.partial(expert_kernel, grid_of, capacity, steps,...  95.5 us
    pallas_call x1, Pallas kernels, exchange(): pl.pallas_call(functools.partial(exchange_kernel, grid_of, zp, rows.shape...  36.1 us
    pallas_call x1, Pallas kernels, attention_backward(): pl.pallas_call(functools.partial(attention_back_kernel, grid_of, jobs), g...  29.8 us
  transfers between devices with their start and end apart: 2, of which 0 were waited for; matrix products, arithmetic and copies ran while one was open for 6% of the time, Pallas kernels for 25%

profile of v7, /device:TPU:0, one launch (start us, length us, event | category | flops | bytes accessed | tf_op | source)
XLA Modules:
  0.0 620.2 jit_solution(1648821206579911816)
XLA Ops:
  13.2 100.4 %shard_map.288 = (bf16[32,40,5248]{2,1,0:T(8,128)(2,1)}, bf16[2,2,256,1280]{3,2,1,0:T(8,128)(2,1)}, bf16[2,2,2,256,1280]{4,3,2,1,0:T(8,128)(2,1)}, s32[2,2,2,8,256]{4,3,2,1,0:T(8,128)}) custom-call(bf16[40,1280]{1,0:T(8,128)(2,1)} %wq_ref.1, bf16[40,1280]{1,0:T(8,128)(2,1)} %wk_ref.1, bf16[40,1280]{1,0:T(8,128)(2,1)} %wv_ref.1, bf16[40,1280]{1,0:T(8,128)(2,1)} %wo_ref.1, ...), custom_call_target="tpu_custom_call" | custom-call | tf_op jit(solution)/shard_map/pallas_call | solution.py:377
  117.0 2.5 multiply_reduce_fusion
  119.6 2.1 fusion.2.rows_ref
  121.7 11.5 %shard_map.289 = (bf16[256,1280]{1,0:T(8,128)(2,1)S(1)}, bf16[1024,1280]{1,0:T(8,128)(2,1)S(1)}, bf16[1024,1280]{1,0:T(8,128)(2,1)S(1)}) custom-call(bf16[1024,1280]{1,0:T(8,128)(2,1)} %fusion.2.rows_ref, bf16[1280,5248]{1,0:T(8,128)(2,1)} %bitcast.147, bf16[1280,5248]{1,0:T(8,128)(2,1)} %bitcast.148, bf16[1280,5248]{1,0:T(8,128)(2,1)} %bitcast.149), custom_call_target="tpu_custom_call" | custom-call | flops 7549747200 | bytes 17694720 | tf_op jit(solution)/shard_map/pallas_call | solution.py:682
  133.5 9.1 %shard_map.290.out_ref = bf16[256,1280]{1,0:T(8,128)(2,1)S(1)} custom-call(bf16[256,1280]{1,0:T(8,128)(2,1)S(1)} %get-tuple-element.84.q_ref, bf16[1024,1280]{1,0:T(8,128)(2,1)S(1)} %get-tuple-element.85.k_ref, bf16[1024,1280]{1,0:T(8,128)(2,1)S(1)} %get-tuple-element.86.v_ref, f32[256,1024]{1,0:T(8,128)S(1)} %and_select_fusion.1.bias_ref), custom_call_target="tpu_custom_call" | custom-call | flops 1342177280 | bytes 7602176 | tf_op jit(solution)/shard_map/pallas_call | solution.py:753
  142.6 3.3 multiply_reduce_fusion.3
  148.0 36.1 %shard_map.291 = bf16[2,2,2,256,1280]{4,3,2,1,0:T(8,128)(2,1)} custom-call(bf16[256,1280]{1,0:T(8,128)(2,1)} %multiply_convert_fusion.src.refs_1_), custom_call_target="tpu_custom_call" | custom-call | tf_op jit(solution)/shard_map/pallas_call | solution.py:481
  190.6 4.6 fusion.44
  196.6 46.2 %shard_map.292 = (bf16[2,8,256,1280]{3,2,1,0:T(8,128)(2,1)}, f32[8,1,256]{2,1,0:T(1,128)}, bf16[1280,896]{1,0:T(8,128)(2,1)}, bf16[1280,896]{1,0:T(8,128)(2,1)}, bf16[896,1280]{1,0:T(8,128)(2,1)}) custom-call(bf16[8,256,1280]{2,1,0:T(8,128)(2,1)} %bitcast.156, bf16[8,256,1280]{2,1,0:T(8,128)(2,1)} %bitcast.191, s32[8,1,256]{2,1,0:T(1,128)} %get-tuple-element.227.refs_2_, ...), custom_call_target="tpu_custom_call" | custom-call | flops 26424115200 | bytes 55705600 | tf_op jit(solution)/shard_map/pallas_call | solution.py:978
  242.9 49.2 %shard_map.293 = (bf16[2,8,256,1280]{3,2,1,0:T(8,128)(2,1)}, f32[8,1,256]{2,1,0:T(1,128)}, bf16[1280,896]{1,0:T(8,128)(2,1)}, bf16[1280,896]{1,0:T(8,128)(2,1)},...) custom-call(bf16[8,256,1280]{2,1,0:T(8,128)(2,1)} %bitcast.157, bf16[8,256,1280]{2,1,0:T(8,128)(2,1)} %bitcast.192, ...), custom_call_target="tpu_custom_call" | custom-call | flops 26424115200 | bytes 55705600 | tf_op jit(solution)/shard_map/pallas_call | solution.py:978
  295.8 2.5 fusion.13.refs_7_.refs_0_
  298.4 4.1 reshape.441.refs_4_
  302.4 65.7 %shard_map.294 = (bf16[2,256,1280]{2,1,0:T(8,128)(2,1)}, f32[2,2,2,2,256]{4,3,2,1,0:T(2,128)}, f32[256,1280]{1,0:T(8,128)}, f32[256,1280]{1,0:T(8,128)}, bf16[12...) custom-call(bf16[2,2,2,2,256,1280]{5,4,3,2,1,0:T(8,128)(2,1)} %bitca, ...), custom_call_target="tpu_custom_call" | custom-call | tf_op jit(solution)/shard_map/pallas_call | solution.py:629
  369.0 2.8 fusion.35
  374.3 2.8 multiply_reduce_fusion.1
  380.7 29.8 %shard_map.295 = (bf16[256,1280]{1,0:T(8,128)(2,1)S(1)}, bf16[2,1024,1280]{2,1,0:T(8,128)(2,1)}, bf16[1280,1280]{1,0:T(8,128)(2,1)}, bf16[1,4,160,896]{3,2,1,0:T(8,128)(2,1)S(1)}, bf16[3,160,896]{2,1,0:T(8,128)(2,1)S(1)}) custom-call(bf16[256,1280]{1,0:T(8,128)(2,1)S(1)} %get-tuple-element.84.q_ref, bf16[1024,1280]{1,0:T(8,128)(2,1)S(1)} %get-tuple-element.85.k_ref, ...), custom_call_target="tpu_custom_call" | custom-call | flops 5033164800 | bytes 14155776 | tf_op jit(solution)/shard_map/pallas_call | solution.py:818
  414.5 53.4 %shard_map.296 = (bf16[2,256,1280]{2,1,0:T(8,128)(2,1)}, bf16[1,4,160,896]{3,2,1,0:T(8,128)(2,1)}, bf16[1,4,112,1280]{3,2,1,0:T(8,128)(2,1)}, bf16[3,112,1280]{2,1,0:T(8,128)(2,1)}, bf16[3,160,896]{2,1,0:T(8,128)(2,1)}) custom-call(bf16[2,1,2,2,256,1280]{5,4,3,2,1,0:T(8,128)(2,1)} %bitcast.159, bf16[4,2,160,896]{3,2,1,0:T(8,128)(2,1)} %bitcast.160, ...), custom_call_target="tpu_custom_call" | custom-call | tf_op jit(solution)/shard_map/pallas_call | solution.py:629
  469.2 10.0 %shard_map.297 = (bf16[1280,1280]{1,0:T(8,128)(2,1)}, bf16[1280,1280]{1,0:T(8,128)(2,1)}, bf16[1280,1280]{1,0:T(8,128)(2,1)}, f32[256,1280]{1,0:T(8,128)S(1)}) custom-call(bf16[1024,1280]{1,0:T(8,128)(2,1)S(1)} %copy-done.2, bf16[256,1280]{1,0:T(8,128)(2,1)S(1)} %get-tuple-element.106.gq_ref, bf16[2,256,1280]{2,1,0:T(8,128)(2,1)S(1)} %copy-done.9, ...), custom_call_target="tpu_custom_call" | custom-call | flops 5033164800 | bytes 23592960 | tf_op jit(solution)/shard_map/pallas_call | solution.py:720
  481.5 3.0 fusion.8.refs_9_.refs_5_
  485.8 4.2 reshape.413.refs_1_
  490.0 2.4 fusion.24
  492.4 106.9 %shard_map.298 = (bf16[2,40,1280]{2,1,0:T(8,128)(2,1)}, bf16[2,28,1280]{2,1,0:T(8,128)(2,1)}, bf16[2,40,896]{2,1,0:T(8,128)(2,1)}, bf16[2,40,896]{2,1,0:T(8,128)...) custom-call(bf16[4,2,2,2,40,1280]{5,4,3,2,1,0:T(8,128)(2,1)} %bitcas, ...), custom_call_target="tpu_custom_call" | custom-call | tf_op jit(solution)/shard_map/pallas_call | solution.py:1236
  599.3 7.0 %shard_map.299 = (f32[2,2,160,896]{3,2,1,0:T(8,128)}, f32[2,2,160,896]{3,2,1,0:T(8,128)}, f32[2,2,112,1280]{3,2,1,0:T(8,128)}, f32[40,1280]{1,0:T(8,128)}, f32[2...) custom-call(bf16[4,160,896]{2,1,0:T(8,128)(2,1)} %fusion.13.refs_7_., ...), custom_call_target="tpu_custom_call" | custom-call | tf_op jit(solution)/shard_map/pallas_call | solution.py:1296
  610.4 2.7 fusion.17
  (165 shorter events, 42.9 us)
Async XLA Ops:
  7.2 291.2 %all-gather.6.cloned.1.call-start = ((), (), s32[]{:S(2)}) async-start(), calls=%async_computation.1 | async-start | bytes 2703360 | tf_op jit(solution)/shard_map/all_gather | solution.py:1373
  113.6 188.8 %all-gather.4.cloned.1.call-start = ((), (), s32[]{:S(2)}) async-start(), calls=%async_computation | async-start | bytes 4730880 | tf_op jit(solution)/shard_map/all_gather | solution.py:1373
  114.7 18.6 %copy-start.28 = (s32[1,2,4,128]{3,1,2,0:T(2,128)}, s32[1,2,4,128]{3,1,2,0:T(2,128)S(1)}, u32[]{:S(2)}) copy-start(s32[1,2,4,128]{3,1,2,0:T(2,128)S(1)} %copy.116) | copy-start | bytes 12292
  114.7 18.6 %copy-start.42 = (s32[256]{0:T(256)}, s32[256]{0:T(256)S(1)}, u32[]{:S(2)}) copy-start(s32[256]{0:T(256)S(1)} %iota_add_fusion.1) | copy-start | bytes 3076
  115.4 17.8 %copy-start.30 = (s32[4,1,256]{2,1,0:T(1,128)}, s32[4,1,256]{2,1,0:T(1,128)S(1)}, u32[]{:S(2)}) copy-start(s32[4,1,256]{2,1,0:T(1,128)S(1)} %slice.56) | copy-start | bytes 12292
  121.7 11.5 %copy-start.37 = (s32[256]{0:T(256)S(1)}, s32[256]{0:T(256)}, u32[]{:S(2)}) copy-start(s32[256]{0:T(256)} %param.18) | copy-start | bytes 3076
  133.2 9.3 %copy-start = (bf16[1024,1280]{1,0:T(8,128)(2,1)}, bf16[1024,1280]{1,0:T(8,128)(2,1)S(1)}, u32[]{:S(2)}) copy-start(bf16[1024,1280]{1,0:T(8,128)(2,1)S(1)} %get-tuple-element.86.v_ref) | copy-start | bytes 7864324
  133.5 9.1 %copy-start.12 = (bf16[256,1280]{1,0:T(8,128)(2,1)S(1)}, bf16[256,1280]{1,0:T(8,128)(2,1)}, u32[]{:S(2)}) copy-start(bf16[256,1280]{1,0:T(8,128)(2,1)} %rows_ref.1) | copy-start | bytes 1966084
  148.0 36.2 %copy-start.27 = (s32[2,2,2,8,256]{4,3,2,1,0:T(8,128)S(1)}, s32[2,2,2,8,256]{4,3,2,1,0:T(8,128)}, u32[]{:S(2)}) copy-start(s32[2,2,2,8,256]{4,3,2,1,0:T(8,128)} %get-tuple-element.87) | copy-start | bytes 196612
  184.1 4.4 copy-start.33
  242.8 49.3 %copy-start.40 = (f32[8,1,256]{2,1,0:T(1,128)S(1)}, f32[8,1,256]{2,1,0:T(1,128)}, u32[]{:S(2)}) copy-start(f32[8,1,256]{2,1,0:T(1,128)} %get-tuple-element.93) | copy-start | bytes 24580
  242.9 50.7 %copy-start.13 = (bf16[256,1280]{1,0:T(8,128)(2,1)S(1)}, bf16[256,1280]{1,0:T(8,128)(2,1)}, u32[]{:S(2)}) copy-start(bf16[256,1280]{1,0:T(8,128)(2,1)} %rows_ref.1) | copy-start | bytes 1966084
  242.9 50.9 %copy-start.45 = (s32[16]{0:T(128)S(1)}, s32[16]{0:T(128)}, u32[]{:S(2)}) copy-start(s32[16]{0:T(128)} %add.313) | copy-start | bytes 196
  242.9 51.5 %copy-start.29 = (s32[1,2,4,128]{3,1,2,0:T(2,128)S(1)}, s32[1,2,4,128]{3,1,2,0:T(2,128)}, u32[]{:S(2)}) copy-start(s32[1,2,4,128]{3,1,2,0:T(2,128)} %copy-done.28) | copy-start | bytes 12292
  242.9 51.5 %copy-start.31 = (s32[4,1,256]{2,1,0:T(1,128)S(1)}, s32[4,1,256]{2,1,0:T(1,128)}, u32[]{:S(2)}) copy-start(s32[4,1,256]{2,1,0:T(1,128)} %copy-done.30) | copy-start | bytes 12292
  242.9 51.5 %copy-start.38 = (s32[256]{0:T(256)S(1)}, s32[256]{0:T(256)}, u32[]{:S(2)}) copy-start(s32[256]{0:T(256)} %param.18) | copy-start | bytes 3076
  242.9 51.5 %copy-start.43 = (s32[256]{0:T(256)S(1)}, s32[256]{0:T(256)}, u32[]{:S(2)}) copy-start(s32[256]{0:T(256)} %copy-done.42) | copy-start | bytes 3076
  369.0 4.9 copy-start.21
  373.9 5.0 copy-start.3
  414.5 53.4 %copy-start.2 = (bf16[1024,1280]{1,0:T(8,128)(2,1)S(1)}, bf16[1024,1280]{1,0:T(8,128)(2,1)}, u32[]{:S(2)}) copy-start(bf16[1024,1280]{1,0:T(8,128)(2,1)} %fusion.2.rows_ref) | copy-start | bytes 7864324
  469.2 10.0 %copy-start.14 = (bf16[256,1280]{1,0:T(8,128)(2,1)S(1)}, bf16[256,1280]{1,0:T(8,128)(2,1)}, u32[]{:S(2)}) copy-start(bf16[256,1280]{1,0:T(8,128)(2,1)} %rows_ref.1) | copy-start | bytes 1966084
  469.2 10.0 %copy-start.36 = (f32[256]{0:T(256)S(1)}, f32[256]{0:T(256)}, u32[]{:S(2)}) copy-start(f32[256]{0:T(256)} %get-tuple-element.230) | copy-start | bytes 3076
  485.8 4.2 copy-start.46
  599.3 11.1 %copy-start.41 = (f32[256]{0:T(256)S(1)}, f32[256]{0:T(256)}, u32[]{:S(2)}) copy-start(f32[256]{0:T(256)} %get-tuple-element.229) | copy-start | bytes 3076
  (25 other events, 67.1 us)
Sparse Core Ops, SparseCore 0:
  113.8 59.2 all-gather.5
  176.5 63.5 all-gather.3
